TPU v7x, 128 devices: a whole 4x4x4 slice. The times are simulated.
128 devices in a mesh: blk: 32 (over x_hi, z, y), rep: 4 (over x_lo, core).
Axes of the slice: x: 4 (x_hi: 2, x_lo: 2; x = x_hi * 2 + x_lo), y: 4, z: 4, core: 2. Of those that a mesh axis runs over, the one named last changes fastest.
Arguments:
- features: bfloat16 [32768, 512], P('blk', 'rep'), may hold values from -6 to 6
- weight: bfloat16 [512, 512], P('rep'), may hold values from -0.25 to 0.25
- bias_vector: float32 [512], replicated, may hold values from -3 to 3
- cotangent: bfloat16 [32768, 512], P('blk', 'rep'), may hold values from -6 to 6
- tile_masks: int32 [32, 256, 4, 16, 128], P('blk'), may hold values from 0 to 255, as said below
- tile_rows: int32 [32, 256, 4], P('blk'), may hold values from 0 to 7, as said below
- tile_counts: int32 [32, 256], P('blk'), may hold values from 0 to 4, as said below
Outputs:
- activation: float32 [32768, 512], P('blk', 'rep')
- grad_features: float32 [32768, 512], P('blk', 'rep')
- grad_weight: float32 [512, 512], P('rep')
- grad_bias: float32 [512], replicated
Inputs may be any that keep to these rules, and one draw needn't show every extreme that they name: `tile_masks`: sparse edge bits. `tile_rows`: within one row block and tile column the live slots name different tile rows. `tile_counts`: each row block has a tile column with all 4 slots live; slots at or beyond the count are ignored.
All inputs are finite; a program needn't handle non-finite values.
Results may differ from a plain program's by a relative error of at most 0.0055.
Values may be sent and summed in bfloat16 or wider, within the bound.
A program may use at most 128 MiB of HBM per device.

v0:
```python
import math

import jax
import jax.numpy as jnp
from jax import lax
from jax.sharding import PartitionSpec as P


def unpack_tiles(mask_words):
    shifts = jnp.arange(8, dtype=jnp.int32)
    bit_values = jnp.bitwise_and(jnp.right_shift(mask_words[..., None], shifts), 1)
    bit_values = jnp.swapaxes(bit_values, -3, -2)
    return bit_values.reshape(bit_values.shape[:-2] + (bit_values.shape[-2] * 8,))


def row_counts(mask_words):
    total = jnp.zeros(mask_words.shape[:-2] + (mask_words.shape[-1],), jnp.int32)
    for shift in range(8):
        total = total + jnp.sum(jnp.bitwise_and(jnp.right_shift(mask_words, shift), 1), axis=-2)
    return total


def place_table(slot_rows, slot_counts, row_tiles):
    slot_count = slot_rows.shape[-1]
    is_live = jnp.arange(slot_count, dtype=jnp.int32) < slot_counts[..., None]
    hits = slot_rows[..., None] == jnp.arange(row_tiles, dtype=jnp.int32)
    return jnp.logical_and(hits, is_live[..., None]).astype(jnp.float32)


def body(features, weight, bias_vector, cotangent, tile_masks, tile_rows, tile_counts):
    tile_bits = tile_masks[0]
    slot_rows = tile_rows[0]
    slot_counts = tile_counts[0]
    nodes_blk, quarter = features.shape
    tile_size = tile_bits.shape[-1]
    row_tiles = nodes_blk // tile_size
    highest_precision = lax.Precision.HIGHEST
    tile_placement = place_table(slot_rows, slot_counts, row_tiles)
    counted = row_counts(tile_bits).astype(jnp.float32)
    degrees = 1.0 + jnp.einsum(
        "gst,gsr->tr", tile_placement, counted, precision=highest_precision
    ).reshape(nodes_blk)
    inv_root = lax.rsqrt(degrees)
    scaled = (features.astype(jnp.float32) * inv_root[:, None]).astype(jnp.bfloat16)
    empty_sum = jnp.zeros((nodes_blk, quarter), jnp.float32)
    shard_rows = lax.all_gather(scaled, "blk", axis=0, tiled=True)
    tile_count = shard_rows.shape[0] // tile_size
    per_turn = math.gcd(tile_count, 8)
    feature_tiles = shard_rows.reshape(tile_count // per_turn, per_turn, tile_size, quarter)

    def advance(turn_index, running_partial):
        tile_start = turn_index * per_turn
        mask_words = lax.dynamic_slice_in_dim(tile_bits, tile_start, per_turn, 0)
        local_weight = lax.dynamic_slice_in_dim(tile_placement, tile_start, per_turn, 0)
        current = lax.dynamic_index_in_dim(feature_tiles, turn_index, 0, keepdims=False)
        dense = unpack_tiles(mask_words).astype(jnp.bfloat16)
        tile_products = jnp.einsum(
            "gsrc,gcf->gsrf", dense, current, preferred_element_type=jnp.float32
        )
        return running_partial + jnp.einsum(
            "odu,odzy->uzy", local_weight, tile_products, precision=highest_precision
        )

    start_sum = empty_sum.reshape(row_tiles, tile_size, quarter)
    neighbour_sums = lax.fori_loop(0, tile_count // per_turn, advance, start_sum).reshape(
        empty_sum.shape
    )
    aggregate = (neighbour_sums * inv_root[:, None]).astype(jnp.bfloat16)
    partial_value = jnp.dot(aggregate, weight, preferred_element_type=jnp.float32)
    summed_hidden = lax.psum_scatter(partial_value, "rep", scatter_dimension=1, tiled=True)
    out_width = summed_hidden.shape[1]
    bias_here = lax.dynamic_slice_in_dim(
        bias_vector, lax.axis_index("rep") * out_width, out_width, 0
    )
    hidden = summed_hidden + bias_here
    logistic = jax.nn.sigmoid(hidden)
    activation = hidden * logistic
    slope_grad = (
        cotangent.astype(jnp.float32) * logistic * (1.0 + hidden * (1.0 - logistic))
    ).astype(jnp.bfloat16)
    slope_full = lax.all_gather(slope_grad, "rep", axis=1, tiled=True)
    weight_part = lax.dot_general(
        aggregate, slope_full, (((0,), (0,)), ((), ())), preferred_element_type=jnp.float32
    )
    bias_part = jnp.sum(slope_full.astype(jnp.float32), axis=0)
    grad_weight, grad_bias = lax.psum((weight_part, bias_part), "blk")
    back_product = lax.dot_general(
        slope_full, weight, (((1,), (1,)), ((), ())), preferred_element_type=jnp.float32
    )
    back_input = (back_product * inv_root[:, None]).astype(jnp.bfloat16)
    neighbour_tiles = back_input.reshape(row_tiles, tile_size, quarter).astype(jnp.float32)
    row_count = nodes_blk * lax.axis_size("blk")
    tile_count = row_count // tile_size
    local_per_turn = math.gcd(tile_count, 8)

    def one_turn(turn_index):
        tile_start = turn_index * local_per_turn
        mask_words = lax.dynamic_slice_in_dim(tile_bits, tile_start, local_per_turn, 0)
        local_weight = lax.dynamic_slice_in_dim(tile_placement, tile_start, local_per_turn, 0)
        selected_tile = jnp.einsum(
            "qnz,zhb->qnhb", local_weight, neighbour_tiles, precision=highest_precision
        ).astype(jnp.bfloat16)
        dense = unpack_tiles(mask_words).astype(jnp.bfloat16)
        return jnp.einsum(
            "gsrc,gsrf->gcf", dense, selected_tile, preferred_element_type=jnp.float32
        )

    blocks = lax.map(one_turn, jnp.arange(tile_count // local_per_turn, dtype=jnp.int32))
    back_sums = lax.psum_scatter(
        blocks.reshape(row_count, quarter), "blk", scatter_dimension=0, tiled=True
    )
    grad_features = back_sums * inv_root[:, None]
    return (activation, grad_features, grad_weight, grad_bias)


def solution(mesh):
    return jax.shard_map(
        body,
        mesh=mesh,
        in_specs=(
            P("blk", "rep"),
            P("rep", None),
            P(),
            P("blk", "rep"),
            P("blk", None, None, None, None),
            P("blk", None, None),
            P("blk", None),
        ),
        out_specs=(P("blk", "rep"), P("blk", "rep"), P("rep", None), P()),
        check_vma=False,
    )
```

profile of v0, /device:TPU:6, one launch (start us, length us, event | category | flops | bytes accessed | tf_op | source)
XLA Modules:
  0.0 1183.7 jit_solution(10449289435080985584)
XLA Ops:
  7.9 19.6 %and_reduce_fusion.6 = (s32[256,4,128]{2,1,0:T(4,128)S(1)}, s32[256,4,128]{2,1,0:T(4,128)S(1)}, s32[256,4,128]{2,1,0:T(4,128)S(1)}, s32[256,4,128]{2,1,0:T(4,128...) fusion(s32[1,256,4,16,128]{4,3,2,1,0:T(8,128)} %param.15), kind=kLoop, calls=%fused_computation.41 | loop fusion | flops 49283072 | bytes 12582912 | tf_op jit(solution)/shard_map/reduce_sum | solution.py:19
  29.5 104.5 %all-gather.3.cloned.1.call-done = bf16[32768,128]{1,0:T(8,128)(2,1)} async-done(((bf16[1024,128]{1,0:T(8,128)(2,1)}), bf16[32768,128]{1,0:T(8,128)(2,1)}) %all-gather.3.cloned.1.call-update) | async-done | bytes 8388624 | tf_op jit(solution)/shard_map/all_gather | solution.py:46
  134.0 231.2 %while.25 = (s32[]{:T(128)}, f32[8,128,128]{2,0,1:T(8,128)S(1)}, f32[256,4,8]{0,2,1:T(8,128)S(1)}, s32[256,4,16,128]{3,2,1,0:T(8,128)}, bf16[32,8,128,128]{3,2,1...) while((s32[]{:T(128)}, f32[8,128,128]{2,0,1:T(8,128)S(1)}, ...), condition=%wide.region_9.10_spmd.clone, body=%wide.region_8.9_spmd.clone.sunk | while | flops 186384384 | bytes 6310057 | solution.py:65
  136.7 4.5 fusion.76
  143.9 4.5 fusion.76
  151.1 4.5 fusion.76
  158.3 4.5 fusion.76
  165.6 4.5 fusion.76
  172.8 4.5 fusion.76
  180.0 4.5 fusion.76
  187.2 4.5 fusion.76
  194.5 4.5 fusion.76
  201.7 4.5 fusion.76
  208.9 4.5 fusion.76
  216.2 4.5 fusion.76
  223.4 4.5 fusion.76
  230.6 4.5 fusion.76
  237.8 4.5 fusion.76
  245.1 4.5 fusion.76
  252.3 4.5 fusion.76
  259.5 4.5 fusion.76
  266.7 4.5 fusion.76
  274.0 4.5 fusion.76
  281.2 4.5 fusion.76
  288.4 4.5 fusion.76
  295.7 4.5 fusion.76
  302.9 4.5 fusion.76
  310.1 4.5 fusion.76
  317.3 4.5 fusion.76
  324.6 4.5 fusion.76
  331.8 4.5 fusion.76
  339.0 4.5 fusion.76
  346.2 4.5 fusion.76
  353.5 4.5 fusion.76
  360.7 4.5 fusion.76
  368.2 26.4 %reduce-scatter.3.cloned.1.call-done = f32[1024,128]{1,0:T(8,128)} async-done(((f32[1024,512]{1,0:T(8,128)}), f32[1024,128]{1,0:T(8,128)}) %reduce-scatter.3.cloned.1.call-update) | async-done | bytes 524304 | tf_op jit(solution)/shard_map/reduce_scatter | solution.py:70
  394.6 2.2 multiply_convert_fusion
  396.8 22.6 %all-gather.5.cloned.1.call-done = bf16[1024,512]{1,0:T(8,128)(2,1)} async-done(((bf16[1024,128]{1,0:T(8,128)(2,1)}), bf16[1024,512]{1,0:T(8,128)(2,1)}) %all-gather.5.cloned.1.call-update) | async-done | bytes 1048592 | tf_op jit(solution)/shard_map/all_gather | solution.py:81
  421.2 179.4 %while.24 = (s32[]{:T(128)}, f32[32,8,128,128]{3,2,1,0:T(8,128)}, s32[32]{0:T(128)S(1)}, s32[256,4,16,128]{3,2,1,0:T(8,128)}, f32[256,4,8]{0,2,1:T(8,128)S(1)}, ...) while((s32[]{:T(128)}, f32[32,8,128,128]{3,2,1,0:T(8,128)}, ...), condition=%wide.region_12.13_spmd, body=%wide.region_11.12_spmd.sunk | while | flops 186646528 | bytes 3950771 | solution.py:108
  423.5 1.9 convolution_convert_fusion.2
  429.1 1.9 convolution_convert_fusion.2
  434.7 1.9 convolution_convert_fusion.2
  446.0 1.9 convolution_convert_fusion.2
  451.6 1.9 convolution_convert_fusion.2
  457.2 1.9 convolution_convert_fusion.2
  468.4 1.9 convolution_convert_fusion.2
  473.9 1.9 convolution_convert_fusion.2
  490.8 1.9 convolution_convert_fusion.2
  502.0 1.9 convolution_convert_fusion.2
  507.6 1.9 convolution_convert_fusion.2
  518.8 1.9 convolution_convert_fusion.2
  530.1 1.9 convolution_convert_fusion.2
  535.7 1.9 convolution_convert_fusion.2
  541.3 1.9 convolution_convert_fusion.2
  563.7 1.9 convolution_convert_fusion.2
  569.4 1.9 convolution_convert_fusion.2
  575.0 1.9 convolution_convert_fusion.2
  580.6 1.9 convolution_convert_fusion.2
  586.2 1.9 convolution_convert_fusion.2
  597.4 1.9 convolution_convert_fusion.2
  603.1 95.7 %psum.15 = f32[512]{0:T(512)} all-reduce(f32[512]{0:T(512)S(1)} %convert_reduce_fusion), channel_id=1, replica_groups=mesh['blk'=32,'rep'=4] {'blk'}, use_global_device_ids=true, to_apply=%region_16.17 | all-reduce | flops 512 | bytes 4096 | tf_op jit(solution)/shard_map/psum | solution.py:86
  698.9 127.6 %reduce-scatter.5.cloned.1.call-done = f32[1024,128]{1,0:T(8,128)} async-done(((f32[32768,128]{1,0:T(8,128)}), f32[1024,128]{1,0:T(8,128)}) %reduce-scatter.5.cloned.1.call-update) | async-done | bytes 524304 | tf_op jit(solution)/shard_map/reduce_scatter | solution.py:109
  826.5 2.0 broadcast_multiply_fusion
  828.5 346.9 %all-reduce.2.cloned.1.call-done = f32[128,512]{1,0:T(8,128)} async-done(((f32[128,512]{1,0:T(8,128)}), f32[128,512]{1,0:T(8,128)}) %all-reduce.2.cloned.1.call-update) | async-done | bytes 262160 | tf_op jit(solution)/shard_map/psum | solution.py:86
  (336 shorter events, 214.1 us)
Async XLA Ops:
  7.2 358.4 %copy-start = (bf16[128,512]{1,0:T(8,128)(2,1)S(1)}, bf16[128,512]{1,0:T(8,128)(2,1)}, u32[]{:S(2)}) copy-start(bf16[128,512]{1,0:T(8,128)(2,1)} %param.12) | copy-start | bytes 393220
  7.2 126.8 %all-gather.3.cloned.1.call-start = ((), (), s32[]{:S(2)}) async-start(), calls=%async_computation.2 | async-start | bytes 8650752 | tf_op jit(solution)/shard_map/all_gather | solution.py:46
  7.9 20.0 %copy-start.4 = (s32[1,256,4]{1,2,0:T(4,128)S(1)}, s32[1,256,4]{1,2,0:T(4,128)}, u32[]{:S(2)}) copy-start(s32[1,256,4]{1,2,0:T(4,128)} %param.16) | copy-start | bytes 12292
  7.9 20.3 %copy-start.2 = (bf16[1024,128]{1,0:T(8,128)(2,1)S(1)}, bf16[1024,128]{1,0:T(8,128)(2,1)}, u32[]{:S(2)}) copy-start(bf16[1024,128]{1,0:T(8,128)(2,1)} %param.11) | copy-start | bytes 786436
  29.2 365.4 %reduce-scatter.3.cloned.1.call-start = ((), (), s32[]{:S(2)}) async-start(), calls=%async_computation.3 | async-start | bytes 2621440 | tf_op jit(solution)/shard_map/reduce_scatter | solution.py:70
  134.0 260.6 %copy-start.3 = (bf16[1024,128]{1,0:T(8,128)(2,1)S(1)}, bf16[1024,128]{1,0:T(8,128)(2,1)}, u32[]{:S(2)}) copy-start(bf16[1024,128]{1,0:T(8,128)(2,1)} %param.14) | copy-start | bytes 786436
  367.4 52.0 %all-gather.5.cloned.1.call-start = ((), (), s32[]{:S(2)}) async-start(), calls=%async_computation.4 | async-start | bytes 1310720 | tf_op jit(solution)/shard_map/all_gather | solution.py:81
  396.8 429.7 %reduce-scatter.5.cloned.1.call-start = ((), (), s32[]{:S(2)}) async-start(), calls=%async_computation.5 | async-start | bytes 17301504 | tf_op jit(solution)/shard_map/reduce_scatter | solution.py:109
  600.6 1.2 copy-start.1
  600.7 574.8 %all-reduce.2.cloned.1.call-start = ((), (), s32[]{:S(2)}) async-start(), calls=%async_computation.6 | async-start | bytes 524288 | tf_op jit(solution)/shard_map/psum | solution.py:86
Sparse Core Ops, SparseCore 0:
  29.3 104.6 all-gather.2
  367.5 27.0 reduce-scatter.2
  396.9 22.4 all-gather.4
  600.8 225.6 reduce-scatter.4
  829.5 345.8 all-reduce.1
where the time goes:
time: 1190 us; the launch traced here: 1180 us
  waiting for transfers between devices  628 us (53%)
  matrix products  306 us (26%)
  blocking collectives  95.7 us (8%)
  local copies, waits for them, and re-layouts  90.5 us (8%)
  other arithmetic  26.3 us (2%)
  loops' own time  22.9 us (2%)
  between operations  13.9 us (1%)
    psum x1, waiting for transfers between devices, body(): grad_weight, grad_bias = lax.psum((weight_part, bias_part), 'blk')  347 us
    dot_general x32, matrix products, advance(): jnp.einsum('odu,odzy->uzy', local_weight, tile_products, precision=highes...  145 us
    reduce_scatter x1, waiting for transfers between devices, body(): lax.psum_scatter(blocks.reshape(row_count, quarter), 'blk', scatter_dimen...  128 us
    all_gather x1, waiting for transfers between devices, body(): shard_rows = lax.all_gather(scaled, 'blk', axis=0, tiled=True)  105 us
    psum x1, blocking collectives, body(): grad_weight, grad_bias = lax.psum((weight_part, bias_part), 'blk')  95.7 us
    shift_right_arithmetic x192, local copies, waits for them, and re-layouts, unpack_tiles(): jnp.right_shift(mask_words[..., None], shifts)  68 us
    dot_general x32, matrix products, one_turn(): jnp.einsum('qnz,zhb->qnhb', local_weight, neighbour_tiles, precision=high...  60.9 us
    dot_general x32, matrix products, advance(): jnp.einsum('gsrc,gcf->gsrf', dense, current, preferred_element_type=jnp.f...  50.8 us
  transfers between devices with their start and end apart: 5, of which 5 were waited for; matrix products, arithmetic and copies ran while one was open for 0% of the time, Pallas kernels for 0%

commit v1 on v0

v1 whole, which is shorter than its diff:
```python
import functools

import jax
import jax.numpy as jnp
import numpy as np
from jax import lax
from jax.experimental import pallas as pl
from jax.experimental.pallas import tpu as pltpu
from jax.sharding import PartitionSpec as P

MESH = pl.DeviceIdType.MESH
BF16 = jnp.bfloat16
F32 = jnp.float32
VMEM = pl.BlockSpec(memory_space=pltpu.VMEM)
SMEM = pl.BlockSpec(memory_space=pltpu.SMEM)
ANY = pl.BlockSpec(memory_space=pl.ANY)
DMA = pltpu.SemaphoreType.DMA
MIB = 2**20


class Place:
    def __init__(self):
        blk = lax.axis_index("blk")
        rep = lax.axis_index("rep")
        self.x, self.z, self.y = blk // 16, lax.rem(blk // 4, 4), lax.rem(blk, 4)
        self.xl, self.c = rep // 2, lax.rem(rep, 2)
        self.rep = rep
        self.xz = self.x * 4 + self.z

    def at(self, x=None, z=None, y=None, xl=None, c=None):
        x = self.x if x is None else x
        z = self.z if z is None else z
        y = self.y if y is None else y
        xl = self.xl if xl is None else xl
        c = self.c if c is None else c
        return (x * 16 + z * 4 + y, xl * 2 + c)

    def dy(self, n):
        return lax.rem(self.y + n, 4)

    def dz(self, n):
        return lax.rem(self.z + n, 4)


def greet(peers):
    barrier = pltpu.get_barrier_semaphore()
    for peer in peers:
        pl.semaphore_signal(barrier, inc=1, device_id=peer, device_id_type=MESH)
    pl.semaphore_wait(barrier, len(peers))


class Copies:
    def __init__(self, send, recv):
        self.send, self.recv, self.used = send, recv, []

    def start(self, src, dst, peer):
        n = len(self.used)
        copy = pltpu.make_async_remote_copy(
            src_ref=src, dst_ref=dst, send_sem=self.send.at[n], recv_sem=self.recv.at[n],
            device_id=peer, device_id_type=MESH,
        )
        copy.start()
        self.used.append(copy)
        return copy

    def wait_sends(self):
        for copy in self.used:
            copy.wait_send()


def prepare_kernel(meta_ref, masks_ref, feat_ref, perm_ref, m16_ref, xt_ref, row_ref, col_ref, d0, d1, d2, d3):
    step = pl.program_id(0)
    degs = (d0, d1, d2, d3)

    @pl.when(step == 0)
    def _():
        for d in degs:
            d[...] = jnp.zeros_like(d)

    group = masks_ref.shape[0]
    for g in range(group):
        for s in range(4):
            words = masks_ref[g, s]
            m16_ref[g, s * 16:(s + 1) * 16, :] = words.astype(jnp.int16)
            joined = jnp.bitwise_or(words[:8], jnp.left_shift(words[8:], 8))
            t = meta_ref[(step * group + g) * 4 + s]
            degs[s][t] += lax.population_count(joined)

    @pl.when(step == pl.num_programs(0) - 1)
    def _():
        total = (d0[0:8] + d1[0:8]) + (d2[0:8] + d3[0:8])
        degrees = 1.0 + jnp.sum(total, axis=1).astype(F32)
        inv = lax.rsqrt(degrees)
        for t in range(8):
            lanes = inv[t:t + 1, :]
            row_ref[:, t * 128:(t + 1) * 128] = jnp.broadcast_to(lanes, (8, 128))
            spread = jnp.broadcast_to(lanes, (128, 128))
            col_ref[t * 128:(t + 1) * 128, :] = spread.T
            feat = feat_ref[t * 128:(t + 1) * 128, :].astype(F32).T
            scaled = (feat * spread).astype(BF16)
            moved = jnp.dot(scaled, perm_ref[...], preferred_element_type=F32).astype(BF16)
            xt_ref[t // 4, :, (t % 4) * 128:(t % 4 + 1) * 128] = moved


def prepare(meta, masks, features, perm):
    group = 16
    steps = 256 // group
    fixed = lambda *shape: pl.BlockSpec(shape, lambda i: (0,) * len(shape))
    return pl.pallas_call(
        prepare_kernel,
        grid=(steps,),
        out_shape=(
            jax.ShapeDtypeStruct((256, 64, 128), jnp.int16),
            jax.ShapeDtypeStruct((2, 128, 512), BF16),
            jax.ShapeDtypeStruct((8, 1024), F32),
            jax.ShapeDtypeStruct((1024, 128), F32),
        ),
        in_specs=[
            SMEM,
            pl.BlockSpec((group, 4, 16, 128), lambda i: (i, 0, 0, 0)),
            fixed(1024, 128),
            fixed(128, 128),
        ],
        out_specs=(
            pl.BlockSpec((group, 64, 128), lambda i: (i, 0, 0)),
            fixed(2, 128, 512),
            fixed(8, 1024),
            fixed(1024, 128),
        ),
        scratch_shapes=[pltpu.VMEM((9, 8, 128), jnp.int32)] * 4,
        compiler_params=pltpu.CompilerParams(
            dimension_semantics=("arbitrary",), vmem_limit_bytes=24 * MIB
        ),
        name="prepare",
    )(meta, masks, features, perm)


def spread_kernel(m16, meta, xt, w, rm, rmeta, g, wc, send, recv, local):
    me = Place()
    sibling = me.at(c=1 - me.c)
    x_peer = me.at(x=1 - me.x)
    z_peers = [me.at(z=me.dz(n)) for n in (1, 2, 3)]
    y_peers = [me.at(y=me.dy(n)) for n in (1, 2, 3)]
    rep_peers = [sibling, me.at(xl=1 - me.xl), me.at(xl=1 - me.xl, c=1 - me.c)]
    greet(z_peers + y_peers + rep_peers + [x_peer])

    copies = Copies(send, recv)
    own, other = me.c, 1 - me.c
    to_sibling = copies.start(xt.at[other], g.at[me.xz, own], sibling)
    first = [copies.start(xt.at[own], g.at[me.xz, own], p) for p in z_peers]
    across = copies.start(xt.at[own], g.at[me.xz, own], x_peer)
    masks = []
    for n in (1, 2, 3):
        there = me.dy(n)
        peer = y_peers[n - 1]
        masks.append(copies.start(meta.at[there, own], rmeta.at[me.y], peer))
        masks.append(copies.start(m16.at[:, there, own], rm.at[me.y], peer))
    stays = [
        pltpu.make_async_copy(m16.at[:, me.y, own], rm.at[me.y], local.at[0]),
        pltpu.make_async_copy(meta.at[me.y, own], rmeta.at[me.y], local.at[1]),
        pltpu.make_async_copy(xt.at[own], g.at[me.xz, own], local.at[2]),
        pltpu.make_async_copy(w.at[me.rep], wc.at[me.rep], local.at[3]),
    ]
    for copy in stays:
        copy.start()
    weights = []
    for peer in rep_peers:
        weights.append(copies.start(w.at[peer[1]], wc.at[me.rep], peer))

    to_sibling.wait_recv()
    other_x = copies.start(g.at[me.xz, other], g.at[me.xz, other], x_peer)
    second = [copies.start(g.at[me.xz, other], g.at[me.xz, other], p) for p in z_peers]
    last = []
    for n in (1, 2, 3):
        first[n - 1].wait_recv()
        source = me.x * 4 + me.dz(4 - n)
        last.append(copies.start(g.at[source, own], g.at[source, own], x_peer))
    other_x.wait_recv()
    far = (1 - me.x) * 4 + me.z
    last += [copies.start(g.at[far, other], g.at[far, other], p) for p in z_peers]
    for copy in [across] + masks + weights + second + last:
        copy.wait_recv()
    copies.wait_sends()
    for copy in stays:
        copy.wait()


def spread(m16, meta, xt, w):
    return pl.pallas_call(
        spread_kernel,
        out_shape=(
            jax.ShapeDtypeStruct((4, 8, 4, 64, 128), jnp.int16),
            jax.ShapeDtypeStruct((4, 8, 128), jnp.int32),
            jax.ShapeDtypeStruct((8, 2, 128, 512), BF16),
            jax.ShapeDtypeStruct((4, 128, 128), BF16),
        ),
        in_specs=[ANY, VMEM, VMEM, VMEM],
        out_specs=(VMEM, VMEM, VMEM, VMEM),
        scratch_shapes=[DMA((24,)), DMA((24,)), DMA((4,))],
        compiler_params=pltpu.CompilerParams(
            collective_id=0, has_side_effects=True, vmem_limit_bytes=24 * MIB
        ),
        name="spread",
    )(m16, meta, xt, w)


def unpack_chunk(i, j, masks_ref, meta_ref, dense_ref, out_ref):
    one, zero = jnp.asarray(1, BF16), jnp.asarray(0, BF16)
    for tc in range(4):
        dense_ref[tc, 0:8] = jnp.zeros((8, 16, 128), jnp.int16)
        for s in range(4):
            t = meta_ref[i, 0, (j * 4 + tc) * 4 + s]
            dense_ref[tc, t] = masks_ref[i, j, tc, s * 16:(s + 1) * 16, :]
    for tc in range(4):
        for t in range(8):
            words = dense_ref[tc, t]
            for k in range(8):
                bits = jnp.where(jnp.bitwise_and(words, jnp.int16(1 << k)) != 0, one, zero)
                row = tc * 128 + k * 16
                out_ref[row:row + 16, t * 128:(t + 1) * 128] = bits


def forward_kernel(meta_ref, masks_ref, g_ref, o_ref, dense, a0, a1, acc):
    bufs = (a0, a1)
    unpack_chunk(0, 0, masks_ref, meta_ref, dense, a0)

    def step(n, _):
        i, pair = n // 4, lax.rem(n, 4)
        for h in range(2):
            later = jnp.minimum(n * 2 + h + 1, 31)
            unpack_chunk(later // 8, lax.rem(later, 8), masks_ref, meta_ref, dense, bufs[1 - h])
            prod = jnp.dot(g_ref[pair * 2 + h], bufs[h][...], preferred_element_type=F32)
            if h == 0:
                acc[...] = jnp.where(pair == 0, 0.0, acc[...]) + prod
            else:
                acc[...] += prod

        @pl.when(pair == 3)
        def _():
            o_ref[i] = acc[...].astype(BF16)

        return 0

    lax.fori_loop(0, 16, step, 0)


def backward_kernel(meta_ref, masks_ref, b_ref, o_ref, dense, a0, a1, acc):
    bufs = (a0, a1)
    unpack_chunk(0, 0, masks_ref, meta_ref, dense, a0)

    def step(n, _):
        j, pair = n // 2, lax.rem(n, 2)
        for h in range(2):
            later = jnp.minimum(n * 2 + h + 1, 31)
            unpack_chunk(lax.rem(later, 4), later // 4, masks_ref, meta_ref, dense, bufs[1 - h])
            prod = jnp.dot(bufs[h][...], b_ref[pair * 2 + h], preferred_element_type=F32)
            if h == 0:
                acc[...] = jnp.where(pair == 0, 0.0, acc[...]) + prod
            else:
                acc[...] += prod

        @pl.when(pair == 1)
        def _():
            o_ref[j] = acc[...].astype(BF16)

        return 0

    lax.fori_loop(0, 16, step, 0)


def product(kernel, name, out_shape, acc_shape, meta, masks, dense):
    return pl.pallas_call(
        kernel,
        out_shape=jax.ShapeDtypeStruct(out_shape, BF16),
        in_specs=[SMEM, VMEM, VMEM],
        out_specs=VMEM,
        scratch_shapes=[
            pltpu.VMEM((4, 9, 16, 128), jnp.int16),
            pltpu.VMEM((512, 1024), BF16),
            pltpu.VMEM((512, 1024), BF16),
            pltpu.VMEM(acc_shape, F32),
        ],
        compiler_params=pltpu.CompilerParams(vmem_limit_bytes=24 * MIB),
        name=name,
    )(meta, masks, dense)


def middle_kernel(part, row, col, wc, w, bias, cot, act, ball, gwx,
                  rc, snd, ry, agg, agg_t, slope, send, recv):
    me = Place()
    sibling = me.at(c=1 - me.c)
    xl_peer = me.at(xl=1 - me.xl)
    y_peers = [me.at(y=me.dy(n)) for n in (1, 2, 3)]
    greet([sibling, xl_peer] + y_peers)
    copies = Copies(send, recv)
    own, other = me.c, 1 - me.c

    halves = {}
    for n in (2, 1, 3, 0):
        halves[n] = copies.start(part.at[me.dy(n), other], rc.at[n], sibling)
    sums = {}
    for n in (2, 1, 3):
        halves[n].wait_recv()
        snd[n - 1] = (part[me.dy(n), own].astype(F32) + rc[n].astype(F32)).astype(BF16)
        sums[n] = copies.start(snd.at[n - 1], ry.at[n - 1], y_peers[n - 1])
    halves[0].wait_recv()
    for n in (1, 3, 2):
        sums[n].wait_recv()
    for t in range(8):
        lanes = slice(t * 128, (t + 1) * 128)
        total = part[me.y, own, :, lanes].astype(F32) + rc[0, :, lanes].astype(F32)
        for n in range(3):
            total = total + ry[n, :, lanes].astype(F32)
        total = total * row[0:1, lanes]
        agg_t[:, lanes] = total.astype(BF16)
        agg[me.rep, lanes, :] = total.T.astype(BF16)

    def gather_rep(buf):
        near = copies.start(buf.at[me.rep], buf.at[me.rep], sibling)
        far = copies.start(buf.at[me.rep], buf.at[me.rep], xl_peer)
        far.wait_recv()
        theirs = (1 - me.xl) * 2 + me.c
        passed = copies.start(buf.at[theirs], buf.at[theirs], sibling)
        near.wait_recv()
        passed.wait_recv()

    gather_rep(agg)

    def rows_forward(m, _):
        rows = pl.ds(pl.multiple_of(m * 256, 256), 256)
        hidden = jnp.dot(agg[0, rows, :], wc[0], preferred_element_type=F32)
        for q in range(1, 4):
            hidden = hidden + jnp.dot(agg[q, rows, :], wc[q], preferred_element_type=F32)
        hidden = hidden + bias[me.rep, 0:1, :]
        logistic = jax.nn.sigmoid(hidden)
        act[rows, :] = hidden * logistic
        value = cot[rows, :].astype(F32) * logistic * (1.0 + hidden * (1.0 - logistic))
        slope[me.rep, rows, :] = value.astype(BF16)
        return 0

    lax.fori_loop(0, 4, rows_forward, 0)
    gather_rep(slope)

    mine = pl.ds(pl.multiple_of(own * 128, 128), 128)

    def rows_backward(m, _):
        rows = pl.ds(pl.multiple_of(m * 256, 256), 256)
        total = jnp.zeros((256, 128), F32)
        for q in range(4):
            total = total + lax.dot_general(
                slope[q, rows, :], w[q], (((1,), (1,)), ((), ())), preferred_element_type=F32
            )
        ball[me.y, rows, mine] = (total * col[rows, :]).astype(BF16)
        return 0

    lax.fori_loop(0, 4, rows_backward, 0)
    block = ball.at[me.y, :, mine]
    gathered = [copies.start(block, block, p) for p in y_peers]
    shared = [copies.start(block, block, sibling)]
    ones = jnp.ones((8, 1024), BF16)
    for q in range(4):
        lanes = slice(q * 128, (q + 1) * 128)
        grad = jnp.dot(agg_t[...], slope[q], preferred_element_type=F32)
        gb = jnp.dot(ones, slope[q], preferred_element_type=F32)
        for n in range(4):
            gwx[n, 0:32, lanes] = grad[n * 32:(n + 1) * 32]
            gwx[n, 32:40, lanes] = gb
    for n in (1, 3, 2):
        gathered[n - 1].wait_recv()
        block = ball.at[me.dy(4 - n), :, mine]
        shared.append(copies.start(block, block, sibling))
    for copy in shared:
        copy.wait_recv()
    copies.wait_sends()


def middle(part, row, col, wc, w, bias, cot):
    return pl.pallas_call(
        middle_kernel,
        out_shape=(
            jax.ShapeDtypeStruct((1024, 128), F32),
            jax.ShapeDtypeStruct((4, 1024, 256), BF16),
            jax.ShapeDtypeStruct((4, 40, 512), F32),
        ),
        in_specs=[VMEM] * 7,
        out_specs=(VMEM, VMEM, VMEM),
        scratch_shapes=[
            pltpu.VMEM((4, 128, 1024), BF16),
            pltpu.VMEM((3, 128, 1024), BF16),
            pltpu.VMEM((3, 128, 1024), BF16),
            pltpu.VMEM((4, 1024, 128), BF16),
            pltpu.VMEM((128, 1024), BF16),
            pltpu.VMEM((4, 1024, 128), BF16),
            DMA((24,)),
            DMA((24,)),
        ],
        compiler_params=pltpu.CompilerParams(
            collective_id=1, has_side_effects=True, vmem_limit_bytes=32 * MIB
        ),
        name="middle",
    )(part, row, col, wc, w, bias, cot)


def settle_kernel(part, gwx, out, gw, az, a_sum, ax, bx, b_sum, bz, final,
                  wy, wz, wx_send, wx, send, recv, local):
    me = Place()
    sibling = me.at(c=1 - me.c)
    x_peer = me.at(x=1 - me.x)
    z_peers = [me.at(z=me.dz(n)) for n in (1, 2, 3)]
    y_peers = [me.at(y=me.dy(n)) for n in (1, 2, 3)]
    greet(z_peers + y_peers + [x_peer, sibling])
    copies = Copies(send, recv)
    own_x, other_x = me.x, 1 - me.x

    to_x = [copies.start(part.at[other_x, me.dz(n), 1], bx.at[n], x_peer) for n in (2, 1, 3, 0)]
    to_x = dict(zip((2, 1, 3, 0), to_x))
    weights = [copies.start(gwx.at[me.dy(n)], wy.at[me.y], y_peers[n - 1]) for n in (1, 2, 3)]
    to_z = {}
    for side in (1, 0):
        for n in (2, 1, 3):
            x_at = other_x if side else own_x
            to_z[side, n] = copies.start(part.at[x_at, me.dz(n), 0], az.at[side, n - 1], z_peers[n - 1])
    wy[me.y] = gwx[me.y]

    for copy in weights:
        copy.wait_recv()
    wz[me.z] = (wy[0] + wy[1]) + (wy[2] + wy[3])
    weights = [copies.start(wz.at[me.z], wz.at[me.z], p) for p in z_peers]

    b_out = {}
    for n in (2, 1, 3):
        to_x[n].wait_recv()
        b_sum[n - 1] = (part[own_x, me.dz(n), 1].astype(F32) + bx[n].astype(F32)).astype(BF16)
        b_out[n] = copies.start(b_sum.at[n - 1], bz.at[n - 1], z_peers[n - 1])
    for n in (1, 3, 2):
        to_z[1, n].wait_recv()
    total = part[other_x, me.z, 0].astype(F32)
    for n in range(3):
        total = total + az[1, n].astype(F32)
    a_sum[...] = total.astype(BF16)
    a_out = copies.start(a_sum, ax, x_peer)

    for copy in weights:
        copy.wait_recv()
    wx_send[...] = (wz[0] + wz[1]) + (wz[2] + wz[3])
    weight_x = copies.start(wx_send, wx, x_peer)

    to_x[0].wait_recv()
    for n in (1, 3, 2):
        b_out[n].wait_recv()
    total = part[own_x, me.z, 1].astype(F32) + bx[0].astype(F32)
    for n in range(3):
        total = total + bz[n].astype(F32)
    final[0, 256:512, :] = total[:, 0:128]
    final[1, 256:512, :] = total[:, 128:256]

    weight_x.wait_recv()
    gw[me.y] = wx_send[...] + wx[...]
    weights = [copies.start(gw.at[me.y], gw.at[me.y], p) for p in y_peers]

    for n in (1, 3, 2):
        to_z[0, n].wait_recv()
    a_out.wait_recv()
    total = part[own_x, me.z, 0].astype(F32) + ax[...].astype(F32)
    for n in range(3):
        total = total + az[0, n].astype(F32)
    final[0, 0:256, :] = total[:, 0:128]
    final[1, 0:256, :] = total[:, 128:256]
    swap = copies.start(final.at[1 - me.c], out.at[me.c], sibling)
    keep = pltpu.make_async_copy(final.at[me.c], out.at[me.c], local)
    keep.start()
    swap.wait_recv()
    for copy in weights:
        copy.wait_recv()
    keep.wait()
    copies.wait_sends()


def settle(part, gwx):
    half = (256, 256)
    return pl.pallas_call(
        settle_kernel,
        out_shape=(
            jax.ShapeDtypeStruct((2, 512, 128), F32),
            jax.ShapeDtypeStruct((4, 40, 512), F32),
        ),
        in_specs=[VMEM, VMEM],
        out_specs=(VMEM, VMEM),
        scratch_shapes=[
            pltpu.VMEM((2, 3) + half, BF16),
            pltpu.VMEM(half, BF16),
            pltpu.VMEM(half, BF16),
            pltpu.VMEM((4,) + half, BF16),
            pltpu.VMEM((3,) + half, BF16),
            pltpu.VMEM((3,) + half, BF16),
            pltpu.VMEM((2, 512, 128), F32),
            pltpu.VMEM((4, 40, 512), F32),
            pltpu.VMEM((4, 40, 512), F32),
            pltpu.VMEM((40, 512), F32),
            pltpu.VMEM((40, 512), F32),
            DMA((28,)),
            DMA((28,)),
            DMA,
        ],
        compiler_params=pltpu.CompilerParams(
            collective_id=2, has_side_effects=True, vmem_limit_bytes=32 * MIB
        ),
        name="settle",
    )(part, gwx)


def body(features, weight, bias_vector, cotangent, tile_masks, tile_rows, tile_counts):
    perm = np.zeros((128, 128), np.float32)
    for w in range(16):
        for k in range(8):
            perm[8 * w + k, 16 * k + w] = 1.0
    live = jnp.arange(4, dtype=jnp.int32) < tile_counts[0][:, None]
    place = jnp.where(live, tile_rows[0], 8).astype(jnp.int32)
    meta = place.reshape(8, 4, 2, 16).transpose(1, 2, 0, 3).reshape(4, 2, 1, 128)
    meta = jnp.broadcast_to(meta, (4, 2, 8, 128))
    weight_q = weight.reshape(128, 4, 128).transpose(1, 0, 2)

    m16, xt, row, col = prepare(place.reshape(1024), tile_masks[0], features, jnp.asarray(perm, BF16))
    rm, rmeta, g, wc = spread(m16.reshape(8, 4, 2, 4, 64, 128), meta, xt, weight_q)
    part = product(forward_kernel, "forward", (4, 256, 1024), (256, 1024), rmeta, rm, g.reshape(8, 256, 512))
    bias = jnp.broadcast_to(bias_vector.reshape(4, 1, 128), (4, 8, 128))
    act, ball, gwx = middle(part.reshape(4, 2, 128, 1024), row, col, wc, weight_q, bias, cotangent)
    back = product(backward_kernel, "backward", (8, 512, 256), (512, 256), rmeta, rm, ball)
    out, gw = settle(back.reshape(2, 4, 2, 256, 256), gwx)
    out = out.reshape(8, 8, 16, 128).transpose(0, 2, 1, 3).reshape(1024, 128) * col
    return act, out, gw[:, :32].reshape(128, 512), gw[0, 32]


def solution(mesh):
    return jax.shard_map(
        body,
        mesh=mesh,
        in_specs=(
            P("blk", "rep"),
            P("rep", None),
            P(),
            P("blk", "rep"),
            P("blk", None, None, None, None),
            P("blk", None, None),
            P("blk", None),
        ),
        out_specs=(P("blk", "rep"), P("blk", "rep"), P("rep", None), P()),
        check_vma=False,
    )
```

time: 1190 us -> 173 us (0.15)
  waiting for transfers between devices: 628 us -> 0 us
  matrix products: 306 us -> 0 us
  Pallas kernels: 0 us -> 154 us
  blocking collectives: 95.7 us -> 0 us
  local copies, waits for them, and re-layouts: 90.5 us -> 14 us
  other arithmetic: 26.3 us -> 2.38 us
  loops' own time: 22.9 us -> 0 us
  between operations: 13.9 us -> 0.85 us
    psum x1 -> x0, waiting for transfers between devices: 347 us -> none  [body(): grad_weight, grad_bias = lax.psum((weight_part, bias_part), 'blk')]
    dot_general x132 -> x0, matrix products: 306 us -> none  [the longest x32 145 us: advance(): jnp.einsum('odu,odzy->uzy', local_weight, tile_products, precision=highes...]
    reduce_scatter x2 -> x0, waiting for transfers between devices: 154 us -> none  [the longest x1 128 us: body(): lax.psum_scatter(blocks.reshape(row_count, quarter), 'blk', scatter_dimen...]
    pallas_call x0 -> x6, Pallas kernels: none -> 154 us  [the longest x1 51.4 us: middle(): pl.pallas_call(middle_kernel, out_shape=(jax.ShapeDtypeStruct((1024, 128)...]
    all_gather x2 -> x0, waiting for transfers between devices: 127 us -> none  [the longest x1 105 us: body(): shard_rows = lax.all_gather(scaled, 'blk', axis=0, tiled=True)]
    psum x1 -> x0, blocking collectives: 95.7 us -> none  [body(): grad_weight, grad_bias = lax.psum((weight_part, bias_part), 'blk')]
    shift_right_arithmetic x192 -> x0, local copies, waits for them, and re-layouts: 68 us -> none  [unpack_tiles(): jnp.right_shift(mask_words[..., None], shifts)]
    another operation x2 -> x0, loops' own time: 22.9 us -> none  [the longest x1 21.7 us: body(): lax.map(one_turn, jnp.arange(tile_count // local_per_turn, dtype=jnp.int32))]
  transfers between devices with their start and end apart: 5 -> 0, of which waited for: 5 -> 0; matrix products, arithmetic and copies ran while one was open for 0% -> 0% of each run, Pallas kernels for 0% -> 0%
where the time goes in v1:
time: 173 us; the launch traced here: 171 us
  Pallas kernels  154 us (89%)
  local copies, waits for them, and re-layouts  14 us (8%)
  other arithmetic  2.38 us (1%)
    pallas_call x1, Pallas kernels, middle(): pl.pallas_call(middle_kernel, out_shape=(jax.ShapeDtypeStruct((1024, 128)...  51.4 us
    pallas_call x2, Pallas kernels, product(): pl.pallas_call(kernel, out_shape=jax.ShapeDtypeStruct(out_shape, BF16), i...  35.8 us
    pallas_call x1, Pallas kernels, settle(): pl.pallas_call(settle_kernel, out_shape=(jax.ShapeDtypeStruct((2, 512, 12...  32.9 us
    pallas_call x1, Pallas kernels, spread(): pl.pallas_call(spread_kernel, out_shape=(jax.ShapeDtypeStruct((4, 8, 4, 6...  30.8 us
    unnamed x22, local copies, waits for them, and re-layouts  11.5 us

profile of v1, /device:TPU:6, one launch (start us, length us, event | category | flops | bytes accessed | tf_op | source)
XLA Modules:
  0.0 171.1 jit_solution(9229521219619609267)
XLA Ops:
  0.6 0.8 copy.21
  1.5 0.1 squeeze.11
  1.6 0.8 iota_compare_fusion
  2.4 0.1 lt.38
  2.5 0.0 copy-start
  2.5 3.4 %copy-done = s32[1,256,4,16,128]{4,3,2,1,0:T(8,128)S(1)} copy-done((s32[1,256,4,16,128]{4,3,2,1,0:T(8,128)S(1)}, s32[1,256,4,16,128]{4,3,2,1,0:T(8,128)}, u32[]{:S(2)}) %copy-start) | copy-done | bytes 8388632
  5.9 0.0 copy-start.3
  5.9 0.9 copy-done.3
  6.8 0.0 copy-start.5
  6.8 0.8 copy-done.5
  7.6 0.0 copy-start.7
  7.6 0.0 copy-start.6
  7.6 3.0 %prepare.1 = (s16[256,64,128]{2,1,0:T(8,128)(2,1)S(1)}, bf16[2,128,512]{2,1,0:T(8,128)(2,1)S(1)}, f32[8,1024]{1,0:T(8,128)S(1)}, f32[1024,128]{1,0:T(8,128)S(1)}) custom-call(s32[1024]{0:T(1024)S(1)} %broadcast_select_fusion.meta_ref, s32[256,4,16,128]{3,2,1,0:T(8,128)S(1)} %bitcast.23, bf16[1024,128]{1,0:T(8,128)(2,1)S(1)} %copy-done.3, ...), custom_call_target="tpu_custom_call" | custom-call | tf_op jit(solution)/shard_map/prepare/pallas_call | solution.py:109
  10.6 0.0 copy-start.1
  10.6 1.9 %copy-done.1 = s16[256,64,128]{2,1,0:T(8,128)(2,1)} copy-done((s16[256,64,128]{2,1,0:T(8,128)(2,1)}, s16[256,64,128]{2,1,0:T(8,128)(2,1)S(1)}, u32[]{:S(2)}) %copy-start.1) | copy-done | bytes 4194328
  12.6 0.1 squeeze.13
  12.7 0.1 copy.24
  12.8 0.5 broadcast.10
  13.3 0.0 copy-done.7
  13.3 0.7 reduce.3
  13.9 0.1 lt.42
  14.1 0.1 copy.22
  14.2 0.1 lt.40
  14.3 0.1 select_bitcast_fusion
  14.4 0.1 copy.25
  14.5 0.1 broadcast_in_dim.23
  14.6 0.0 copy-done.6
  14.6 0.1 copy.26
  14.7 0.1 copy.27
  14.9 0.0 copy-start.2
  14.9 2.2 %copy-done.2 = s16[256,64,128]{2,1,0:T(8,128)(2,1)S(1)} copy-done((s16[256,64,128]{2,1,0:T(8,128)(2,1)S(1)}, s16[256,64,128]{2,1,0:T(8,128)(2,1)}, u32[]{:S(2)}) %copy-start.2) | copy-done | bytes 4194328
  17.1 30.8 %spread.1 = (s16[4,8,4,64,128]{4,3,2,1,0:T(8,128)(2,1)S(1)}, s32[4,8,128]{2,1,0:T(8,128)S(1)}, bf16[8,2,128,512]{3,2,1,0:T(8,128)(2,1)S(1)}, bf16[4,128,128]{2,1,0:T(8,128)(2,1)S(1)}) custom-call(s16[8,4,2,4,64,128]{5,4,3,2,1,0:T(8,128)(2,1)S(1)} %bitcast.24, s32[4,2,8,128]{3,2,1,0:T(8,128)S(1)} %broadcast_in_dim.24.meta, ...), custom_call_target="tpu_custom_call" | custom-call | tf_op jit(solution)/shard_map/spread/pallas_call | solution.py:189
  47.9 0.0 copy-start.8
  47.9 0.0 copy-start.4
  47.9 19.2 %forward.1 = bf16[4,256,1024]{2,1,0:T(8,128)(2,1)S(1)} custom-call(s32[4,8,128]{2,1,0:T(8,128)S(1)} %get-tuple-element.19.meta_ref, s16[4,8,4,64,128]{4,3,2,1,0:T(8,128)(2,1)S(1)} %get-tuple-element.20.masks_ref, bf16[8,256,512]{2,1,0:T(8,128)(2,1)S(1)} %bitcast.25), custom_call_target="tpu_custom_call" | custom-call | tf_op jit(solution)/shard_map/forward/pallas_call | solution.py:272
  67.1 0.0 copy-done.8
  67.1 0.0 copy-done.4
  67.1 51.4 %middle.1 = (f32[1024,128]{1,0:T(8,128)S(1)}, bf16[4,1024,256]{2,1,0:T(8,128)(2,1)S(1)}, f32[4,40,512]{2,1,0:T(8,128)S(1)}) custom-call(bf16[4,2,128,1024]{3,2,1,0:T(8,128)(2,1)S(1)} %bitcast.21, f32[8,1024]{1,0:T(8,128)S(1)} %get-tuple-element.22.row, f32[1024,128]{1,0:T(8,128)S(1)} %get-tuple-element.23.col, ...), custom_call_target="tpu_custom_call" | custom-call | tf_op jit(solution)/shard_map/middle/pallas_call | solution.py:378
  118.6 16.6 %backward.1 = bf16[8,512,256]{2,1,0:T(8,128)(2,1)S(1)} custom-call(s32[4,8,128]{2,1,0:T(8,128)S(1)} %get-tuple-element.19.meta_ref, s16[4,8,4,64,128]{4,3,2,1,0:T(8,128)(2,1)S(1)} %get-tuple-element.20.masks_ref, bf16[4,1024,256]{2,1,0:T(8,128)(2,1)S(1)} %get-tuple-element.26.b_ref), custom_call_target="tpu_custom_call" | custom-call | tf_op jit(solution)/shard_map/backward/pallas_call | solution.py:272
  135.2 32.9 %settle.1 = (f32[2,512,128]{2,1,0:T(8,128)S(1)}, f32[4,40,512]{2,1,0:T(8,128)S(1)}) custom-call(bf16[2,4,2,256,256]{4,3,2,1,0:T(8,128)(2,1)S(1)} %bitcast.22, f32[4,40,512]{2,1,0:T(8,128)S(1)} %get-tuple-element.27.gwx), custom_call_target="tpu_custom_call" | custom-call | tf_op jit(solution)/shard_map/settle/pallas_call | solution.py:481
  168.0 0.2 copy.28
  168.2 0.8 bitcast_multiply_fusion
  169.1 0.7 slice.6
  169.8 0.6 slice.7
  170.4 0.8 copy.30
  (5 shorter events, 0.0 us)
Async XLA Ops:
  2.5 3.4 %copy-start = (s32[1,256,4,16,128]{4,3,2,1,0:T(8,128)S(1)}, s32[1,256,4,16,128]{4,3,2,1,0:T(8,128)}, u32[]{:S(2)}) copy-start(s32[1,256,4,16,128]{4,3,2,1,0:T(8,128)} %param.12) | copy-start | bytes 25165828
  5.9 0.9 copy-start.3
  6.8 0.8 copy-start.5
  7.6 5.7 %copy-start.7 = (s32[1,256]{1,0:T(1,128)S(1)}, s32[1,256]{1,0:T(1,128)}, u32[]{:S(2)}) copy-start(s32[1,256]{1,0:T(1,128)} %param.14) | copy-start | bytes 3076
  7.6 7.0 %copy-start.6 = (bf16[128,512]{1,0:T(8,128)(2,1)S(1)}, bf16[128,512]{1,0:T(8,128)(2,1)}, u32[]{:S(2)}) copy-start(bf16[128,512]{1,0:T(8,128)(2,1)} %param.9) | copy-start | bytes 393220
  10.6 1.9 %copy-start.1 = (s16[256,64,128]{2,1,0:T(8,128)(2,1)}, s16[256,64,128]{2,1,0:T(8,128)(2,1)S(1)}, u32[]{:S(2)}) copy-start(s16[256,64,128]{2,1,0:T(8,128)(2,1)S(1)} %get-tuple-element.17) | copy-start | bytes 12582916
  14.9 2.2 %copy-start.2 = (s16[256,64,128]{2,1,0:T(8,128)(2,1)S(1)}, s16[256,64,128]{2,1,0:T(8,128)(2,1)}, u32[]{:S(2)}) copy-start(s16[256,64,128]{2,1,0:T(8,128)(2,1)} %copy-done.1) | copy-start | bytes 12582916
  47.9 19.3 %copy-start.8 = (f32[512]{0:T(512)S(1)}, f32[512]{0:T(512)}, u32[]{:S(2)}) copy-start(f32[512]{0:T(512)} %param.10) | copy-start | bytes 6148
  47.9 19.3 %copy-start.4 = (bf16[1024,128]{1,0:T(8,128)(2,1)S(1)}, bf16[1024,128]{1,0:T(8,128)(2,1)}, u32[]{:S(2)}) copy-start(bf16[1024,128]{1,0:T(8,128)(2,1)} %cot.1) | copy-start | bytes 786436

commit v2 on v1

v2 whole, which is shorter than its diff:
```python
import functools

import jax
import jax.numpy as jnp
import numpy as np
from jax import lax
from jax.experimental import pallas as pl
from jax.experimental.pallas import tpu as pltpu
from jax.sharding import PartitionSpec as P

MESH = pl.DeviceIdType.MESH
BF16 = jnp.bfloat16
F32 = jnp.float32
VMEM = pl.BlockSpec(memory_space=pltpu.VMEM)
SMEM = pl.BlockSpec(memory_space=pltpu.SMEM)
DMA = pltpu.SemaphoreType.DMA
MIB = 2**20


class Place:
    def __init__(self):
        blk = lax.axis_index("blk")
        rep = lax.axis_index("rep")
        self.x, self.z, self.y = blk // 16, lax.rem(blk // 4, 4), lax.rem(blk, 4)
        self.xl, self.c = rep // 2, lax.rem(rep, 2)
        self.rep = rep
        self.xz = self.x * 4 + self.z

    def at(self, x=None, z=None, y=None, xl=None, c=None):
        x = self.x if x is None else x
        z = self.z if z is None else z
        y = self.y if y is None else y
        xl = self.xl if xl is None else xl
        c = self.c if c is None else c
        return (x * 16 + z * 4 + y, xl * 2 + c)

    def dy(self, n):
        return lax.rem(self.y + n, 4)

    def dz(self, n):
        return lax.rem(self.z + n, 4)


def greet(peers):
    barrier = pltpu.get_barrier_semaphore()
    for peer in peers:
        pl.semaphore_signal(barrier, inc=1, device_id=peer, device_id_type=MESH)
    pl.semaphore_wait(barrier, len(peers))


class Copies:
    def __init__(self, send, recv):
        self.send, self.recv, self.used = send, recv, []

    def start(self, src, dst, peer):
        n = len(self.used)
        copy = pltpu.make_async_remote_copy(
            src_ref=src, dst_ref=dst, send_sem=self.send.at[n], recv_sem=self.recv.at[n],
            device_id=peer, device_id_type=MESH,
        )
        copy.start()
        self.used.append(copy)
        return copy

    def wait_sends(self):
        for copy in self.used:
            copy.wait_send()


def prepare_kernel(meta_ref, masks_ref, feat_ref, perm_ref, m16_ref, xt_ref, row_ref, col_ref, d0, d1, d2, d3):
    step = pl.program_id(0)
    degs = (d0, d1, d2, d3)

    @pl.when(step == 0)
    def _():
        for d in degs:
            d[...] = jnp.zeros_like(d)

    group = masks_ref.shape[0]
    for g in range(group):
        for s in range(4):
            words = masks_ref[g, s]
            m16_ref[g, s * 16:(s + 1) * 16, :] = words.astype(jnp.int16)
            joined = jnp.bitwise_or(words[:8], jnp.left_shift(words[8:], 8))
            t = meta_ref[(step * group + g) * 4 + s]
            degs[s][t] += lax.population_count(joined)

    @pl.when(step == pl.num_programs(0) - 1)
    def _():
        total = (d0[0:8] + d1[0:8]) + (d2[0:8] + d3[0:8])
        degrees = 1.0 + jnp.sum(total, axis=1).astype(F32)
        inv = lax.rsqrt(degrees)
        for t in range(8):
            lanes = inv[t:t + 1, :]
            row_ref[:, t * 128:(t + 1) * 128] = jnp.broadcast_to(lanes, (8, 128))
            spread = jnp.broadcast_to(lanes, (128, 128))
            col_ref[t * 128:(t + 1) * 128, :] = spread.T
            feat = feat_ref[t * 128:(t + 1) * 128, :].astype(F32).T
            scaled = (feat * spread).astype(BF16)
            moved = jnp.dot(scaled, perm_ref[...], preferred_element_type=F32).astype(BF16)
            xt_ref[t // 4, :, (t % 4) * 128:(t % 4 + 1) * 128] = moved


def prepare(meta, masks, features, perm):
    group = 16
    steps = 256 // group
    fixed = lambda *shape: pl.BlockSpec(shape, lambda i: (0,) * len(shape))
    return pl.pallas_call(
        prepare_kernel,
        grid=(steps,),
        out_shape=(
            jax.ShapeDtypeStruct((256, 64, 128), jnp.int16),
            jax.ShapeDtypeStruct((2, 128, 512), BF16),
            jax.ShapeDtypeStruct((8, 1024), F32),
            jax.ShapeDtypeStruct((1024, 128), F32),
        ),
        in_specs=[
            SMEM,
            pl.BlockSpec((group, 4, 16, 128), lambda i: (i, 0, 0, 0)),
            fixed(1024, 128),
            fixed(128, 128),
        ],
        out_specs=(
            pl.BlockSpec((group, 64, 128), lambda i: (i, 0, 0)),
            fixed(2, 128, 512),
            fixed(8, 1024),
            fixed(1024, 128),
        ),
        scratch_shapes=[pltpu.VMEM((9, 8, 128), jnp.int32)] * 4,
        compiler_params=pltpu.CompilerParams(
            dimension_semantics=("arbitrary",), vmem_limit_bytes=24 * MIB
        ),
        name="prepare",
    )(meta, masks, features, perm)


def spread_kernel(m16, meta, xt, w, rm, rmeta, g, wc, send, recv, local):
    me = Place()
    sibling = me.at(c=1 - me.c)
    x_peer = me.at(x=1 - me.x)
    z_peers = [me.at(z=me.dz(n)) for n in (1, 2, 3)]
    y_peers = [me.at(y=me.dy(n)) for n in (1, 2, 3)]
    rep_peers = [sibling, me.at(xl=1 - me.xl), me.at(xl=1 - me.xl, c=1 - me.c)]
    greet(z_peers + y_peers + rep_peers + [x_peer])

    copies = Copies(send, recv)
    own, other = me.c, 1 - me.c

    def at(core, xz):
        return g.at[core, :, pl.ds(pl.multiple_of(xz * 512, 512), 512)]

    to_sibling = copies.start(xt.at[other], at(own, me.xz), sibling)
    first = [copies.start(xt.at[own], at(own, me.xz), p) for p in z_peers]
    across = copies.start(xt.at[own], at(own, me.xz), x_peer)
    masks = []
    for n in (1, 2, 3):
        there = me.dy(n)
        peer = y_peers[n - 1]
        masks.append(copies.start(meta.at[there, own], rmeta.at[me.y], peer))
        masks.append(copies.start(m16.at[:, there, own], rm.at[me.y], peer))
    stays = [
        pltpu.make_async_copy(m16.at[:, me.y, own], rm.at[me.y], local.at[0]),
        pltpu.make_async_copy(meta.at[me.y, own], rmeta.at[me.y], local.at[1]),
        pltpu.make_async_copy(xt.at[own], at(own, me.xz), local.at[2]),
        pltpu.make_async_copy(w.at[me.rep], wc.at[me.rep], local.at[3]),
    ]
    for copy in stays:
        copy.start()
    weights = []
    for peer in rep_peers:
        weights.append(copies.start(w.at[peer[1]], wc.at[me.rep], peer))

    to_sibling.wait_recv()
    other_x = copies.start(at(other, me.xz), at(other, me.xz), x_peer)
    second = [copies.start(at(other, me.xz), at(other, me.xz), p) for p in z_peers]
    last = []
    for n in (1, 2, 3):
        first[n - 1].wait_recv()
        source = me.x * 4 + me.dz(4 - n)
        last.append(copies.start(at(own, source), at(own, source), x_peer))
    other_x.wait_recv()
    far = (1 - me.x) * 4 + me.z
    last += [copies.start(at(other, far), at(other, far), p) for p in z_peers]
    for copy in [across] + masks + weights + second + last:
        copy.wait_recv()
    copies.wait_sends()
    for copy in stays:
        copy.wait()


def spread(m16, meta, xt, w):
    return pl.pallas_call(
        spread_kernel,
        out_shape=(
            jax.ShapeDtypeStruct((4, 8, 4, 64, 128), jnp.int16),
            jax.ShapeDtypeStruct((4, 8, 128), jnp.int32),
            jax.ShapeDtypeStruct((2, 128, 4096), BF16),
            jax.ShapeDtypeStruct((4, 128, 128), BF16),
        ),
        in_specs=[VMEM] * 4,
        out_specs=(VMEM, VMEM, VMEM, VMEM),
        scratch_shapes=[DMA((24,)), DMA((24,)), DMA((4,))],
        compiler_params=pltpu.CompilerParams(
            collective_id=0, has_side_effects=True, vmem_limit_bytes=24 * MIB
        ),
        name="spread",
    )(m16, meta, xt, w)


def place_kernel(meta_ref, masks_ref, dense_ref):
    def chunk(n, _):
        i, j = n // 8, lax.rem(n, 8)
        for tc in range(4):
            dense_ref[n, tc, 0:8] = jnp.zeros((8, 16, 128), jnp.int16)
            for s in range(4):
                t = meta_ref[i, 0, (j * 4 + tc) * 4 + s]
                dense_ref[n, tc, t] = masks_ref[i, j, tc, s * 16:(s + 1) * 16, :]
        return 0

    lax.fori_loop(0, 32, chunk, 0)


def place_tiles(meta, masks):
    return pl.pallas_call(
        place_kernel,
        out_shape=jax.ShapeDtypeStruct((32, 4, 9, 16, 128), jnp.int16),
        in_specs=[SMEM, VMEM],
        out_specs=VMEM,
        compiler_params=pltpu.CompilerParams(vmem_limit_bytes=16 * MIB),
        name="place",
    )(meta, masks)


def table(values, step):
    found = values[-1]
    for n in range(len(values) - 1):
        found = jnp.where(step == n, values[n], found)
    return found


def put_bits(words, out_ref, row, lane):
    one, zero = jnp.asarray(1, BF16), jnp.asarray(0, BF16)
    for k in range(8):
        bits = jnp.where(jnp.bitwise_and(words, jnp.int16(1 << k)) != 0, one, zero)
        out_ref[row + k * 16:row + (k + 1) * 16, lane:lane + 128] = bits


def layer_kernel(dense, g, row, col, wc, w, bias, cot, act, ball, gwx,
                 a0, a1, part, rc, snd, ry, agg, agg_t, slope,
                 core_s, core_r, sum_s, sum_r, send, recv):
    me = Place()
    sibling = me.at(c=1 - me.c)
    xl_peer = me.at(xl=1 - me.xl)
    y_peers = [me.at(y=me.dy(n)) for n in (1, 2, 3)]
    greet([sibling, xl_peer] + y_peers)
    copies = Copies(send, recv)
    own, other = me.c, 1 - me.c

    def unpack(s, out):
        i, pair = me.dy(table((2, 1, 3, 0), s // 4)), lax.rem(s, 4)
        for j in range(8):
            for tc in range(4):
                for t in range(2):
                    words = dense[i * 8 + j, tc, pair * 2 + t]
                    put_bits(words, out, j * 512 + tc * 128, t * 128)

    def to_sibling(s):
        return pltpu.make_async_remote_copy(
            src_ref=part.at[s, other], dst_ref=rc.at[s], send_sem=core_s.at[s], recv_sem=core_r.at[s],
            device_id=sibling, device_id_type=MESH,
        )

    def to_owner(s):
        return pltpu.make_async_remote_copy(
            src_ref=snd.at[s], dst_ref=ry.at[s], send_sem=sum_s.at[s], recv_sem=sum_r.at[s],
            device_id=me.at(y=me.dy(table((2, 1, 3), s // 4))), device_id_type=MESH,
        )

    def pass_on(s):
        to_sibling(s).wait_recv()
        snd[s] = (part[s, own].astype(F32) + rc[s].astype(F32)).astype(BF16)
        to_owner(s).start()

    def rows_of(m):
        return pl.ds(pl.multiple_of(m * 256, 256), 256)

    def rep_copy(buf, base, m, kind):
        theirs = (1 - me.xl) * 2 + me.c
        src = buf.at[theirs if kind == 2 else me.rep, rows_of(m), :]
        n = base + kind * 4 + m
        return pltpu.make_async_remote_copy(
            src_ref=src, dst_ref=src, send_sem=send.at[n], recv_sem=recv.at[n],
            device_id=xl_peer if kind == 1 else sibling, device_id_type=MESH,
        )

    def share(buf, base, m):
        rep_copy(buf, base, m, 1).start()
        rep_copy(buf, base, m, 0).start()

    def finish_sum(m):
        to_sibling(12 + m).wait_recv()
        for k in range(3):
            to_owner(4 * k + m).wait_recv()
        rows = rows_of(m)
        total = part[12 + m, own].astype(F32) + rc[12 + m].astype(F32)
        for k in range(3):
            total = total + ry[4 * k + m].astype(F32)
        total = total * row[0:1, rows]
        agg_t[:, rows] = total.astype(BF16)
        agg[me.rep, rows, :] = total.T.astype(BF16)
        share(agg, 0, m)

    bufs = (a0, a1)
    unpack(0, a0)

    def two_chunks(half, _):
        for h in range(2):
            s = half * 2 + h
            unpack(jnp.minimum(s + 1, 15), bufs[1 - h])
            prod = jnp.dot(g[...], bufs[h][...], preferred_element_type=F32).astype(BF16)
            part[s, 0] = prod[0:128]
            part[s, 1] = prod[128:256]
            to_sibling(s).start()

            @pl.when(jnp.logical_and(s >= 1, s <= 12))
            def _():
                pass_on(s - 1)

            @pl.when(s >= 13)
            def _():
                finish_sum(s - 13)

        return 0

    lax.fori_loop(0, 8, two_chunks, 0)
    finish_sum(3)

    def relay(buf, base, m):
        rep_copy(buf, base, m, 1).wait_recv()
        rep_copy(buf, base, m, 2).start()

    def settled(buf, base, m):
        rep_copy(buf, base, m, 0).wait_recv()
        rep_copy(buf, base, m, 2).wait_recv()

    def rows_forward(m):
        rows = rows_of(m)
        hidden = jnp.dot(agg[0, rows, :], wc[0], preferred_element_type=F32)
        for q in range(1, 4):
            hidden = hidden + jnp.dot(agg[q, rows, :], wc[q], preferred_element_type=F32)
        hidden = hidden + bias[me.rep, 0:1, :]
        logistic = jax.nn.sigmoid(hidden)
        act[rows, :] = hidden * logistic
        value = cot[rows, :].astype(F32) * logistic * (1.0 + hidden * (1.0 - logistic))
        slope[me.rep, rows, :] = value.astype(BF16)

    mine = pl.ds(pl.multiple_of(own * 128, 128), 128)

    def block(n, m):
        start = me.dy(n) * 1024 + m * 256
        return ball.at[pl.ds(pl.multiple_of(start, 256), 256), mine]

    def y_copy(n, m):
        k = 24 + (n - 1) * 4 + m
        return pltpu.make_async_remote_copy(
            src_ref=block(0, m), dst_ref=block(0, m), send_sem=send.at[k], recv_sem=recv.at[k],
            device_id=y_peers[n - 1], device_id_type=MESH,
        )

    def core_copy(n, m):
        k = 36 + n * 4 + m
        return pltpu.make_async_remote_copy(
            src_ref=block(n, m), dst_ref=block(n, m), send_sem=send.at[k], recv_sem=recv.at[k],
            device_id=sibling, device_id_type=MESH,
        )

    def rows_backward(m):
        rows = rows_of(m)
        total = jnp.zeros((256, 128), F32)
        for q in range(4):
            total = total + lax.dot_general(
                slope[q, rows, :], w[q], (((1,), (1,)), ((), ())), preferred_element_type=F32
            )
        here = pl.ds(pl.multiple_of(me.y * 1024 + m * 256, 256), 256)
        ball[here, mine] = (total * col[rows, :]).astype(BF16)
        for n in (2, 1, 3):
            y_copy(n, m).start()
        core_copy(0, m).start()

    def layer_step(m, _):
        @pl.when(m < 4)
        def _():
            relay(agg, 0, m)

        @pl.when(jnp.logical_and(m >= 1, m < 5))
        def _():
            settled(agg, 0, m - 1)
            rows_forward(m - 1)
            share(slope, 12, m - 1)

        @pl.when(jnp.logical_and(m >= 2, m < 6))
        def _():
            relay(slope, 12, m - 2)

        @pl.when(m >= 3)
        def _():
            settled(slope, 12, m - 3)
            rows_backward(m - 3)

        return 0

    lax.fori_loop(0, 7, layer_step, 0)

    ones = jnp.ones((8, 1024), BF16)
    for q in range(4):
        lanes = slice(q * 128, (q + 1) * 128)
        grad = jnp.dot(agg_t[...], slope[q], preferred_element_type=F32)
        gb = jnp.dot(ones, slope[q], preferred_element_type=F32)
        for n in range(4):
            gwx[n, 0:32, lanes] = grad[n * 32:(n + 1) * 32]
            gwx[n, 32:40, lanes] = gb

    def pass_blocks(m, _):
        for n in (1, 3, 2):
            y_copy(n, m).wait_recv()
            core_copy(4 - n, m).start()
        return 0

    lax.fori_loop(0, 4, pass_blocks, 0)

    def finish(m, _):
        for n in range(4):
            core_copy(n, m).wait()
        for n in (1, 2, 3):
            y_copy(n, m).wait_send()
            to_owner((n - 1) * 4 + m).wait_send()
        for kind in range(3):
            rep_copy(agg, 0, m, kind).wait_send()
            rep_copy(slope, 12, m, kind).wait_send()
        for n in range(4):
            to_sibling(n * 4 + m).wait_send()
        return 0

    lax.fori_loop(0, 4, finish, 0)


def layer(dense, g, row, col, wc, w, bias, cot):
    return pl.pallas_call(
        layer_kernel,
        out_shape=(
            jax.ShapeDtypeStruct((1024, 128), F32),
            jax.ShapeDtypeStruct((4096, 256), BF16),
            jax.ShapeDtypeStruct((4, 40, 512), F32),
        ),
        in_specs=[VMEM] * 8,
        out_specs=(VMEM, VMEM, VMEM),
        scratch_shapes=[
            pltpu.VMEM((4096, 256), BF16),
            pltpu.VMEM((4096, 256), BF16),
            pltpu.VMEM((16, 2, 128, 256), BF16),
            pltpu.VMEM((16, 128, 256), BF16),
            pltpu.VMEM((12, 128, 256), BF16),
            pltpu.VMEM((12, 128, 256), BF16),
            pltpu.VMEM((4, 1024, 128), BF16),
            pltpu.VMEM((128, 1024), BF16),
            pltpu.VMEM((4, 1024, 128), BF16),
            DMA((16,)),
            DMA((16,)),
            DMA((12,)),
            DMA((12,)),
            DMA((52,)),
            DMA((52,)),
        ],
        compiler_params=pltpu.CompilerParams(
            collective_id=1, has_side_effects=True, vmem_limit_bytes=36 * MIB
        ),
        name="layer",
    )(dense, g, row, col, wc, w, bias, cot)


STEPS = (
    (1, 1, 2), (0, 1, 2), (1, 1, 1), (0, 1, 1), (1, 1, 3), (0, 1, 3), (1, 1, 0), (0, 1, 0),
    (1, 0, 2), (1, 0, 1), (1, 0, 3), (0, 0, 2), (0, 0, 1), (0, 0, 3), (1, 0, 0), (0, 0, 0),
)
ORDER = {key: n for n, key in enumerate(STEPS)}


def settle_kernel(dense, ball, gwx, out, gw, a0, a1, part, az, a_sum, ax, bx, b_sum, bz, final,
                  wy, wz, wx_send, wx, send, recv, local):
    me = Place()
    sibling = me.at(c=1 - me.c)
    x_peer = me.at(x=1 - me.x)
    z_peers = [me.at(z=me.dz(n)) for n in (1, 2, 3)]
    y_peers = [me.at(y=me.dy(n)) for n in (1, 2, 3)]
    greet(z_peers + y_peers + [x_peer, sibling])

    def remote(n, src, dst, peer):
        return pltpu.make_async_remote_copy(
            src_ref=src, dst_ref=dst, send_sem=send.at[n], recv_sem=recv.at[n],
            device_id=peer, device_id_type=MESH,
        )

    x_first = {n: remote(n, part.at[ORDER[1, 1, n]], bx.at[n], x_peer) for n in range(4)}
    z_first = {
        (side, n): remote(4 + side * 3 + n - 1, part.at[ORDER[0, side, n]], az.at[side, n - 1], z_peers[n - 1])
        for side in range(2) for n in (1, 2, 3)
    }
    z_second = {n: remote(9 + n, b_sum.at[n - 1], bz.at[n - 1], z_peers[n - 1]) for n in (1, 2, 3)}
    x_second = remote(13, a_sum, ax, x_peer)
    w_y = [remote(13 + n, gwx.at[me.dy(n)], wy.at[me.y], y_peers[n - 1]) for n in (1, 2, 3)]
    w_z = [remote(16 + n, wz.at[me.z], wz.at[me.z], z_peers[n - 1]) for n in (1, 2, 3)]
    w_x = remote(20, wx_send, wx, x_peer)
    w_back = [remote(20 + n, gw.at[me.y], gw.at[me.y], y_peers[n - 1]) for n in (1, 2, 3)]

    def unpack(s, out_ref):
        half = table([step[0] for step in STEPS], s)
        side = table([step[1] for step in STEPS], s)
        dist = table([step[2] for step in STEPS], s)
        x = lax.rem(me.x + side, 2)
        j = x * 4 + lax.rem(me.z + dist, 4)
        for i in range(4):
            for tc in range(2):
                for t in range(8):
                    put_bits(dense[i * 8 + j, half * 2 + tc, t], out_ref, tc * 128, i * 1024 + t * 128)

    def pass_b(n):
        x_first[n].wait_recv()
        b_sum[n - 1] = (part[ORDER[1, 0, n]].astype(F32) + bx[n].astype(F32)).astype(BF16)
        z_second[n].start()

    def pass_a():
        total = part[ORDER[0, 1, 0]].astype(F32)
        for n in (1, 2, 3):
            z_first[1, n].wait_recv()
            total = total + az[1, n - 1].astype(F32)
        a_sum[...] = total.astype(BF16)
        x_second.start()

    def weights_z():
        for copy in w_y:
            copy.wait_recv()
        wz[me.z] = (wy[0] + wy[1]) + (wy[2] + wy[3])
        for copy in w_z:
            copy.start()

    def weights_x():
        for copy in w_z:
            copy.wait_recv()
        wx_send[...] = (wz[0] + wz[1]) + (wz[2] + wz[3])
        w_x.start()

    def weights_back():
        w_x.wait_recv()
        gw[me.y] = wx_send[...] + wx[...]
        for copy in w_back:
            copy.start()

    actions = {}
    for n in range(4):
        actions.setdefault(ORDER[1, 1, n], []).append(x_first[n].start)
    for key, copy in z_first.items():
        actions.setdefault(ORDER[(0,) + key], []).append(copy.start)
    actions.setdefault(6, []).append(weights_z)
    for n in (2, 1, 3):
        actions.setdefault(ORDER[1, 0, n] + 1, []).append(functools.partial(pass_b, n))
    actions.setdefault(11, []).append(pass_a)
    actions.setdefault(12, []).append(weights_x)
    actions.setdefault(14, []).append(weights_back)

    for copy in w_y:
        copy.start()
    wy[me.y] = gwx[me.y]
    bufs = (a0, a1)
    unpack(0, a0)

    def two_chunks(pair, _):
        for h in range(2):
            s = pair * 2 + h
            unpack(jnp.minimum(s + 1, 15), bufs[1 - h])
            part[s] = jnp.dot(bufs[h][...], ball[...], preferred_element_type=F32).astype(BF16)
            for at in sorted(actions):
                if at % 2 == h:
                    @pl.when(s == at)
                    def _():
                        for action in actions[at]:
                            action()
        return 0

    lax.fori_loop(0, 8, two_chunks, 0)

    total = part[ORDER[1, 0, 0]].astype(F32)
    x_first[0].wait_recv()
    total = total + bx[0].astype(F32)
    for n in (1, 2, 3):
        z_second[n].wait_recv()
        total = total + bz[n - 1].astype(F32)
    final[0, 256:512, :] = total[:, 0:128]
    final[1, 256:512, :] = total[:, 128:256]
    total = part[ORDER[0, 0, 0]].astype(F32)
    for n in (1, 2, 3):
        z_first[0, n].wait_recv()
        total = total + az[0, n - 1].astype(F32)
    x_second.wait_recv()
    total = total + ax[...].astype(F32)
    final[0, 0:256, :] = total[:, 0:128]
    final[1, 0:256, :] = total[:, 128:256]
    swap = remote(24, final.at[1 - me.c], out.at[me.c], sibling)
    swap.start()
    keep = pltpu.make_async_copy(final.at[me.c], out.at[me.c], local)
    keep.start()
    for copy in w_back:
        copy.wait_recv()
    swap.wait_recv()
    keep.wait()
    for copy in list(x_first.values()) + list(z_first.values()) + list(z_second.values()):
        copy.wait_send()
    for copy in [x_second, w_x, swap] + w_y + w_z + w_back:
        copy.wait_send()


def settle(dense, ball, gwx):
    half = (256, 256)
    return pl.pallas_call(
        settle_kernel,
        out_shape=(
            jax.ShapeDtypeStruct((2, 512, 128), F32),
            jax.ShapeDtypeStruct((4, 40, 512), F32),
        ),
        in_specs=[VMEM] * 3,
        out_specs=(VMEM, VMEM),
        scratch_shapes=[
            pltpu.VMEM((256, 4096), BF16),
            pltpu.VMEM((256, 4096), BF16),
            pltpu.VMEM((16,) + half, BF16),
            pltpu.VMEM((2, 3) + half, BF16),
            pltpu.VMEM(half, BF16),
            pltpu.VMEM(half, BF16),
            pltpu.VMEM((4,) + half, BF16),
            pltpu.VMEM((3,) + half, BF16),
            pltpu.VMEM((3,) + half, BF16),
            pltpu.VMEM((2, 512, 128), F32),
            pltpu.VMEM((4, 40, 512), F32),
            pltpu.VMEM((4, 40, 512), F32),
            pltpu.VMEM((40, 512), F32),
            pltpu.VMEM((40, 512), F32),
            DMA((25,)),
            DMA((25,)),
            DMA,
        ],
        compiler_params=pltpu.CompilerParams(
            collective_id=2, has_side_effects=True, vmem_limit_bytes=36 * MIB
        ),
        name="settle",
    )(dense, ball, gwx)


def body(features, weight, bias_vector, cotangent, tile_masks, tile_rows, tile_counts):
    perm = np.zeros((128, 128), np.float32)
    for w in range(16):
        for k in range(8):
            perm[8 * w + k, 16 * k + w] = 1.0
    live = jnp.arange(4, dtype=jnp.int32) < tile_counts[0][:, None]
    place = jnp.where(live, tile_rows[0], 8).astype(jnp.int32)
    meta = place.reshape(8, 4, 2, 16).transpose(1, 2, 0, 3).reshape(4, 2, 1, 128)
    meta = jnp.broadcast_to(meta, (4, 2, 8, 128))
    weight_q = weight.reshape(128, 4, 128).transpose(1, 0, 2)

    m16, xt, row, col = prepare(place.reshape(1024), tile_masks[0], features, jnp.asarray(perm, BF16))
    rm, rmeta, g, wc = spread(m16.reshape(8, 4, 2, 4, 64, 128), meta, xt, weight_q)
    dense = place_tiles(rmeta, rm)
    bias = jnp.broadcast_to(bias_vector.reshape(4, 1, 128), (4, 8, 128))
    act, ball, gwx = layer(dense, g.reshape(256, 4096), row, col, wc, weight_q, bias, cotangent)
    out, gw = settle(dense, ball, gwx)
    out = out.reshape(8, 8, 16, 128).transpose(0, 2, 1, 3).reshape(1024, 128) * col
    return act, out, gw[:, :32].reshape(128, 512), gw[0, 32]


def solution(mesh):
    return jax.shard_map(
        body,
        mesh=mesh,
        in_specs=(
            P("blk", "rep"),
            P("rep", None),
            P(),
            P("blk", "rep"),
            P("blk", None, None, None, None),
            P("blk", None, None),
            P("blk", None),
        ),
        out_specs=(P("blk", "rep"), P("blk", "rep"), P("rep", None), P()),
        check_vma=False,
    )
```

time: 173 us -> 148 us (0.86)
  Pallas kernels: 154 us -> 131 us
  local copies, waits for them, and re-layouts: 14 us -> 11.5 us
    pallas_call x3 -> x2, Pallas kernels: 87.2 us -> 58.5 us  [the longest x1 55.3 us: layer(): pl.pallas_call(layer_kernel, out_shape=(jax.ShapeDtypeStruct((1024, 128),...]
    pallas_call x1, Pallas kernels: 32.9 us -> 38.3 us  [settle(): pl.pallas_call(settle_kernel, out_shape=(jax.ShapeDtypeStruct((2, 512, 12...]
    unnamed x22 -> x12, local copies, waits for them, and re-layouts: 11.5 us -> 8.24 us
where the time goes in v2:
time: 148 us; the launch traced here: 146 us
  Pallas kernels  131 us (89%)
  local copies, waits for them, and re-layouts  11.5 us (8%)
  other arithmetic  3.05 us (2%)
    pallas_call x1, Pallas kernels, layer(): pl.pallas_call(layer_kernel, out_shape=(jax.ShapeDtypeStruct((1024, 128),...  55.3 us
    pallas_call x1, Pallas kernels, settle(): pl.pallas_call(settle_kernel, out_shape=(jax.ShapeDtypeStruct((2, 512, 12...  38.3 us
    pallas_call x1, Pallas kernels, spread(): pl.pallas_call(spread_kernel, out_shape=(jax.ShapeDtypeStruct((4, 8, 4, 6...  30.8 us
    unnamed x12, local copies, waits for them, and re-layouts  8.24 us
    pallas_call x1, Pallas kernels, place_tiles(): pl.pallas_call(place_kernel, out_shape=jax.ShapeDtypeStruct((32, 4, 9, 16...  3.15 us
    pallas_call x1, Pallas kernels, prepare(): pl.pallas_call(prepare_kernel, grid=(steps,), out_shape=(jax.ShapeDtypeSt...  3.01 us

profile of v2, /device:TPU:6, one launch (start us, length us, event | category | flops | bytes accessed | tf_op | source)
XLA Modules:
  0.0 146.0 jit_solution(18420008985188440629)
XLA Ops:
  0.6 0.5 broadcast.10
  1.1 1.3 reduce.3
  2.5 0.1 lt.40
  2.6 0.7 broadcast_in_dim.26.bias
  3.3 0.1 lt.42
  3.4 0.1 copy.22
  3.5 0.8 iota_compare_fusion
  4.3 0.1 lt.38
  4.5 0.8 copy.21
  5.3 0.1 squeeze.11
  5.4 0.1 squeeze.13
  5.5 0.1 copy.24
  5.6 0.1 select_bitcast_fusion
  5.7 0.1 copy.25
  5.8 0.1 broadcast_in_dim.23
  5.9 1.0 copy.26
  6.9 0.1 copy.27
  7.1 0.0 copy-start
  7.1 3.4 %copy-done = s32[1,256,4,16,128]{4,3,2,1,0:T(8,128)S(1)} copy-done((s32[1,256,4,16,128]{4,3,2,1,0:T(8,128)S(1)}, s32[1,256,4,16,128]{4,3,2,1,0:T(8,128)}, u32[]{:S(2)}) %copy-start) | copy-done | bytes 8388632
  10.4 0.0 copy-start.1
  10.4 0.9 copy-done.1
  11.4 0.0 copy-start.3
  11.4 0.8 copy-done.3
  12.2 3.0 %prepare.1 = (s16[256,64,128]{2,1,0:T(8,128)(2,1)S(1)}, bf16[2,128,512]{2,1,0:T(8,128)(2,1)S(1)}, f32[8,1024]{1,0:T(8,128)S(1)}, f32[1024,128]{1,0:T(8,128)S(1)}) custom-call(s32[1024]{0:T(1024)S(1)} %broadcast_select_fusion.meta_ref, s32[256,4,16,128]{3,2,1,0:T(8,128)S(1)} %bitcast.19, bf16[1024,128]{1,0:T(8,128)(2,1)S(1)} %copy-done.1, ...), custom_call_target="tpu_custom_call" | custom-call | tf_op jit(solution)/shard_map/prepare/pallas_call | solution.py:108
  15.2 30.8 %spread.1 = (s16[4,8,4,64,128]{4,3,2,1,0:T(8,128)(2,1)S(1)}, s32[4,8,128]{2,1,0:T(8,128)S(1)}, bf16[2,128,4096]{2,1,0:T(8,128)(2,1)S(1)}, bf16[4,128,128]{2,1,0:T(8,128)(2,1)S(1)}) custom-call(s16[8,4,2,4,64,128]{5,4,3,2,1,0:T(8,128)(2,1)S(1)} %bitcast.20, s32[4,2,8,128]{3,2,1,0:T(8,128)S(1)} %broadcast_in_dim.24.meta, ...), custom_call_target="tpu_custom_call" | custom-call | tf_op jit(solution)/shard_map/spread/pallas_call | solution.py:192
  46.0 0.0 copy-start.2
  46.0 3.1 %place.1.dense = s16[32,4,9,16,128]{4,3,2,1,0:T(8,128)(2,1)S(1)} custom-call(s32[4,8,128]{2,1,0:T(8,128)S(1)} %get-tuple-element.19.meta_ref, s16[4,8,4,64,128]{4,3,2,1,0:T(8,128)(2,1)S(1)} %get-tuple-element.20.masks_ref), custom_call_target="tpu_custom_call" | custom-call | tf_op jit(solution)/shard_map/place/pallas_call | solution.py:224
  49.1 0.0 copy-done.2
  49.2 55.3 %layer.1 = (f32[1024,128]{1,0:T(8,128)S(1)}, bf16[4096,256]{1,0:T(8,128)(2,1)S(1)}, f32[4,40,512]{2,1,0:T(8,128)S(1)}) custom-call(s16[32,4,9,16,128]{4,3,2,1,0:T(8,128)(2,1)S(1)} %place.1.dense, bf16[256,4096]{1,0:T(8,128)(2,1)S(1)} %bitcast.21, f32[8,1024]{1,0:T(8,128)S(1)} %get-tuple-element.22.row, f32[1024,128]{1,0:T(8,128)S(1)} %get-tuple-element.23.col, ...), custom_call_target="tpu_custom_call" | custom-call | tf_op jit(solution)/shard_map/layer/pallas_call | solution.py:448
  104.5 38.3 %settle.1 = (f32[2,512,128]{2,1,0:T(8,128)S(1)}, f32[4,40,512]{2,1,0:T(8,128)S(1)}) custom-call(s16[32,4,9,16,128]{4,3,2,1,0:T(8,128)(2,1)S(1)} %place.1.dense, bf16[4096,256]{1,0:T(8,128)(2,1)S(1)} %get-tuple-element.26.ball, f32[4,40,512]{2,1,0:T(8,128)S(1)} %get-tuple-element.27.gwx), custom_call_target="tpu_custom_call" | custom-call | tf_op jit(solution)/shard_map/settle/pallas_call | solution.py:623
  142.9 0.2 copy.28
  143.0 0.8 bitcast_multiply_fusion
  143.9 0.6 slice.7
  144.5 0.7 slice.6
  145.2 0.8 copy.30
  (4 shorter events, 0.0 us)
Async XLA Ops:
  7.1 3.4 %copy-start = (s32[1,256,4,16,128]{4,3,2,1,0:T(8,128)S(1)}, s32[1,256,4,16,128]{4,3,2,1,0:T(8,128)}, u32[]{:S(2)}) copy-start(s32[1,256,4,16,128]{4,3,2,1,0:T(8,128)} %param.12) | copy-start | bytes 25165828
  10.4 0.9 copy-start.1
  11.4 0.8 copy-start.3
  46.0 3.2 %copy-start.2 = (bf16[1024,128]{1,0:T(8,128)(2,1)S(1)}, bf16[1024,128]{1,0:T(8,128)(2,1)}, u32[]{:S(2)}) copy-start(bf16[1024,128]{1,0:T(8,128)(2,1)} %cot.1) | copy-start | bytes 786436

commit v3 on v2

v3 whole, which is shorter than its diff:
```python
import functools

import jax
import jax.numpy as jnp
from jax import lax
from jax.experimental import pallas as pl
from jax.experimental.pallas import tpu as pltpu
from jax.sharding import PartitionSpec as P

MESH = pl.DeviceIdType.MESH
BF16 = jnp.bfloat16
F32 = jnp.float32
VMEM = pl.BlockSpec(memory_space=pltpu.VMEM)
SMEM = pl.BlockSpec(memory_space=pltpu.SMEM)
DMA = pltpu.SemaphoreType.DMA
MIB = 2**20


class Place:
    def __init__(self):
        blk = lax.axis_index("blk")
        rep = lax.axis_index("rep")
        self.x, self.z, self.y = blk // 16, lax.rem(blk // 4, 4), lax.rem(blk, 4)
        self.xl, self.c = rep // 2, lax.rem(rep, 2)
        self.rep = rep
        self.xz = self.x * 4 + self.z

    def at(self, x=None, z=None, y=None, xl=None, c=None):
        x = self.x if x is None else x
        z = self.z if z is None else z
        y = self.y if y is None else y
        xl = self.xl if xl is None else xl
        c = self.c if c is None else c
        return (x * 16 + z * 4 + y, xl * 2 + c)

    def dy(self, n):
        return lax.rem(self.y + n, 4)

    def dz(self, n):
        return lax.rem(self.z + n, 4)


def greet(peers):
    barrier = pltpu.get_barrier_semaphore()
    for peer in peers:
        pl.semaphore_signal(barrier, inc=1, device_id=peer, device_id_type=MESH)
    pl.semaphore_wait(barrier, len(peers))


class Copies:
    def __init__(self, send, recv):
        self.send, self.recv, self.used = send, recv, []

    def start(self, src, dst, peer):
        n = len(self.used)
        copy = pltpu.make_async_remote_copy(
            src_ref=src, dst_ref=dst, send_sem=self.send.at[n], recv_sem=self.recv.at[n],
            device_id=peer, device_id_type=MESH,
        )
        copy.start()
        self.used.append(copy)
        return copy

    def wait_sends(self):
        for copy in self.used:
            copy.wait_send()


Y_ORDER = (2, 1, 3, 0)


def spread_kernel(rows_ref, counts_ref, masks, feat, w, dense, row, col, g, wc,
                  words, m16, rm, slots_s, slots_v, landed_v, landed_s, xt, send, recv, load, local):
    me = Place()
    own, other = me.c, 1 - me.c
    loads = []
    for q in range(8):
        half = own if q < 4 else other
        loads.append(pltpu.make_async_copy(masks.at[:, me.dy(Y_ORDER[q % 4]), half], words.at[q], load.at[q]))
        loads[q].start()

    sibling = me.at(c=1 - me.c)
    x_peer = me.at(x=1 - me.x)
    z_peers = [me.at(z=me.dz(n)) for n in (1, 2, 3)]
    y_peers = [me.at(y=me.dy(n)) for n in (1, 2, 3)]
    rep_peers = [sibling, me.at(xl=1 - me.xl), me.at(xl=1 - me.xl, c=1 - me.c)]
    greet(z_peers + y_peers + rep_peers + [x_peer])
    copies = Copies(send, recv)

    tile_row = lax.broadcasted_iota(jnp.int32, (8, 128), 0)

    def scan(q, degrees):
        n = Y_ORDER[q % 4]
        half = own if q < 4 else other
        loads[q].wait()

        def tiles(xz, degrees):
            first = ((xz * 4 + me.dy(n)) * 2 + half) * 4
            for tc in range(4):
                count = counts_ref[first + tc]
                for s in range(4):
                    slot = tc * 4 + s
                    t = jnp.where(s < count, rows_ref[s, first + tc], 8)
                    tile = words[q, xz, slot]
                    if q < 3:
                        m16[q, xz, slot] = tile.astype(jnp.int16)
                    elif q == 3:
                        rm[me.y, xz, slot] = tile.astype(jnp.int16)
                    if q < 4:
                        slots_s[q, 0, xz * 16 + slot] = t
                    joined = jnp.bitwise_or(tile[:8], jnp.left_shift(tile[8:], 8))
                    counted = jnp.sum(lax.population_count(joined), axis=0, keepdims=True)
                    degrees = degrees + jnp.where(tile_row == t, counted, 0)
            return degrees

        return lax.fori_loop(0, 8, tiles, degrees)

    degrees = jnp.zeros((8, 128), jnp.int32)
    mask_copies = []
    for q in range(3):
        degrees = scan(q, degrees)
        mask_copies.append(copies.start(m16.at[q], rm.at[me.y], y_peers[Y_ORDER[q] - 1]))
    for q in range(3, 8):
        degrees = scan(q, degrees)

    inv = lax.rsqrt(1.0 + degrees.astype(F32))
    place = lax.broadcasted_iota(jnp.int32, (128, 128), 1)
    source = 8 * jnp.bitwise_and(place, 15) + jnp.right_shift(place, 4)
    perm = jnp.where(lax.broadcasted_iota(jnp.int32, (128, 128), 0) == source, 1.0, 0.0).astype(BF16)
    for t in range(8):
        lanes = inv[t:t + 1, :]
        row[:, t * 128:(t + 1) * 128] = jnp.broadcast_to(lanes, (8, 128))
        spread = jnp.broadcast_to(lanes, (128, 128))
        col[t * 128:(t + 1) * 128, :] = spread.T
        scaled = (feat[t * 128:(t + 1) * 128, :].astype(F32).T * spread).astype(BF16)
        moved = jnp.dot(scaled, perm, preferred_element_type=F32).astype(BF16)
        xt[t // 4, :, (t % 4) * 128:(t % 4 + 1) * 128] = moved

    def at(core, xz):
        return g.at[xz, core]

    def weight_to(rep):
        return w.at[:, pl.ds(pl.multiple_of(rep * 128, 128), 128)]

    to_sibling = copies.start(xt.at[other], at(own, me.xz), sibling)
    first = [copies.start(xt.at[own], at(own, me.xz), p) for p in z_peers]
    across = copies.start(xt.at[own], at(own, me.xz), x_peer)
    stays = [
        pltpu.make_async_copy(xt.at[own], at(own, me.xz), local.at[0]),
        pltpu.make_async_copy(weight_to(me.rep), wc.at[me.rep], local.at[1]),
    ]
    for copy in stays:
        copy.start()
    to_vmem = pltpu.make_async_copy(slots_s, slots_v, local.at[2])
    to_vmem.start()
    to_vmem.wait()
    slot_copies = [copies.start(slots_v.at[q], landed_v.at[me.y], y_peers[Y_ORDER[q] - 1]) for q in range(3)]
    kept = pltpu.make_async_copy(slots_v.at[3], landed_v.at[me.y], local.at[3])
    kept.start()

    to_sibling.wait_recv()
    other_x = copies.start(at(other, me.xz), at(other, me.xz), x_peer)
    second = [copies.start(at(other, me.xz), at(other, me.xz), p) for p in z_peers]
    weights = [copies.start(weight_to(peer[1]), wc.at[me.rep], peer) for peer in rep_peers]

    kept.wait()
    for copy in slot_copies:
        copy.wait_recv()
    to_smem = pltpu.make_async_copy(landed_v, landed_s, local.at[4])
    to_smem.start()
    to_smem.wait()

    def put_tiles(n):
        i = me.dy(n)

        def column(j, _):
            for tc in range(4):
                rows = [landed_s[i, 0, j * 16 + tc * 4 + s] for s in range(4)]
                tiles = [rm[i, j, tc * 4 + s] for s in range(4)]
                for t in range(8):
                    found = jnp.zeros((16, 128), jnp.int16)
                    for s in range(4):
                        found = jnp.where(rows[s] == t, tiles[s], found)
                    dense[i * 8 + j, tc, t] = found
            return 0

        lax.fori_loop(0, 8, column, 0)

    put_tiles(0)
    last = []
    for n in (1, 2, 3):
        first[n - 1].wait_recv()
        source = me.x * 4 + me.dz(4 - n)
        last.append(copies.start(at(own, source), at(own, source), x_peer))
    other_x.wait_recv()
    far = (1 - me.x) * 4 + me.z
    last += [copies.start(at(other, far), at(other, far), p) for p in z_peers]
    for q in range(3):
        mask_copies[q].wait_recv()
        put_tiles(4 - Y_ORDER[q])
    for copy in [across] + weights + second + last:
        copy.wait_recv()
    copies.wait_sends()
    for copy in stays:
        copy.wait()


def spread(rows, counts, masks, features, w):
    return pl.pallas_call(
        spread_kernel,
        out_shape=(
            jax.ShapeDtypeStruct((32, 4, 8, 16, 128), jnp.int16),
            jax.ShapeDtypeStruct((8, 1024), F32),
            jax.ShapeDtypeStruct((1024, 128), F32),
            jax.ShapeDtypeStruct((8, 2, 128, 512), BF16),
            jax.ShapeDtypeStruct((4, 128, 128), BF16),
        ),
        in_specs=[SMEM, SMEM, pl.BlockSpec(memory_space=pltpu.HBM), VMEM, VMEM],
        out_specs=(VMEM,) * 5,
        scratch_shapes=[
            pltpu.VMEM((8, 8, 16, 16, 128), jnp.int32),
            pltpu.VMEM((3, 8, 16, 16, 128), jnp.int16),
            pltpu.VMEM((4, 8, 16, 16, 128), jnp.int16),
            pltpu.SMEM((4, 1, 128), jnp.int32),
            pltpu.VMEM((4, 1, 128), jnp.int32),
            pltpu.VMEM((4, 1, 128), jnp.int32),
            pltpu.SMEM((4, 1, 128), jnp.int32),
            pltpu.VMEM((2, 128, 512), BF16),
            DMA((24,)),
            DMA((24,)),
            DMA((8,)),
            DMA((5,)),
        ],
        compiler_params=pltpu.CompilerParams(
            collective_id=0, has_side_effects=True, vmem_limit_bytes=32 * MIB
        ),
        name="spread",
    )(rows, counts, masks, features, w)


def table(values, step):
    found = values[-1]
    for n in range(len(values) - 1):
        found = jnp.where(step == n, values[n], found)
    return found


def unpack(dense, i, j, out_ref):
    one, zero = jnp.asarray(1, BF16), jnp.asarray(0, BF16)
    for tc in range(4):
        for t in range(8):
            words = dense[i * 8 + j, tc, t]
            for k in range(8):
                bits = jnp.where(jnp.bitwise_and(words, jnp.int16(1 << k)) != 0, one, zero)
                first = tc * 128 + k * 16
                out_ref[first:first + 16, t * 128:(t + 1) * 128] = bits


def layer_kernel(dense, g, row, col, wc, w, bias, cot, act, ball, gwx,
                 a0, a1, acc, part, rc, snd, ry, agg, agg_t, slope,
                 core_s, core_r, sum_s, sum_r, send, recv):
    me = Place()
    sibling = me.at(c=1 - me.c)
    xl_peer = me.at(xl=1 - me.xl)
    y_peers = [me.at(y=me.dy(n)) for n in (1, 2, 3)]
    greet([sibling, xl_peer] + y_peers)
    copies = Copies(send, recv)
    own, other = me.c, 1 - me.c

    def to_sibling(s):
        return pltpu.make_async_remote_copy(
            src_ref=part.at[s, other], dst_ref=rc.at[s], send_sem=core_s.at[s], recv_sem=core_r.at[s],
            device_id=sibling, device_id_type=MESH,
        )

    def to_owner(s):
        return pltpu.make_async_remote_copy(
            src_ref=snd.at[s], dst_ref=ry.at[s], send_sem=sum_s.at[s], recv_sem=sum_r.at[s],
            device_id=me.at(y=me.dy(table((2, 1, 3), s))), device_id_type=MESH,
        )

    def pass_on(s):
        to_sibling(s).wait_recv()
        snd[s] = (part[s, own].astype(F32) + rc[s].astype(F32)).astype(BF16)
        to_owner(s).start()

    def rows_of(m):
        return pl.ds(pl.multiple_of(m * 256, 256), 256)

    def rep_copy(buf, base, m, kind):
        theirs = (1 - me.xl) * 2 + me.c
        src = buf.at[theirs if kind == 2 else me.rep, rows_of(m), :]
        n = base + kind * 4 + m
        return pltpu.make_async_remote_copy(
            src_ref=src, dst_ref=src, send_sem=send.at[n], recv_sem=recv.at[n],
            device_id=xl_peer if kind == 1 else sibling, device_id_type=MESH,
        )

    def share(buf, base, m):
        rep_copy(buf, base, m, 1).start()
        rep_copy(buf, base, m, 0).start()

    def finish_sum(m):
        rows = rows_of(m)
        total = part[3, own, :, rows].astype(F32) + rc[3, :, rows].astype(F32)
        for k in range(3):
            total = total + ry[k, :, rows].astype(F32)
        total = total * row[0:1, rows]
        agg_t[:, rows] = total.astype(BF16)
        agg[me.rep, rows, :] = total.T.astype(BF16)
        share(agg, 0, m)

    def chunk(c):
        return me.dy(table((2, 1, 3, 0), c // 8)), lax.rem(c, 8)

    bufs = (a0, a1)
    unpack(dense, *chunk(0), a0)

    def two_chunks(n, _):
        k, pair = n // 4, lax.rem(n, 4)
        for h in range(2):
            unpack(dense, *chunk(jnp.minimum(n * 2 + h + 1, 31)), bufs[1 - h])
            prod = jnp.dot(g[pair * 2 + h], bufs[h][...], preferred_element_type=F32)
            if h == 0:
                acc[...] = jnp.where(pair == 0, 0.0, acc[...]) + prod
            else:
                acc[...] += prod

        @pl.when(pair == 3)
        def _():
            part[k, 0] = acc[0:128].astype(BF16)
            part[k, 1] = acc[128:256].astype(BF16)
            to_sibling(k).start()

        @pl.when(jnp.logical_and(pair == 0, k >= 1))
        def _():
            pass_on(k - 1)

        return 0

    lax.fori_loop(0, 16, two_chunks, 0)
    to_sibling(3).wait_recv()
    for k in range(3):
        to_owner(k).wait_recv()
    for m in range(4):
        finish_sum(m)

    def relay(buf, base, m):
        rep_copy(buf, base, m, 1).wait_recv()
        rep_copy(buf, base, m, 2).start()

    def settled(buf, base, m):
        rep_copy(buf, base, m, 0).wait_recv()
        rep_copy(buf, base, m, 2).wait_recv()

    def rows_forward(m):
        rows = rows_of(m)
        hidden = jnp.dot(agg[0, rows, :], wc[0], preferred_element_type=F32)
        for q in range(1, 4):
            hidden = hidden + jnp.dot(agg[q, rows, :], wc[q], preferred_element_type=F32)
        hidden = hidden + bias[pl.ds(me.rep, 1), :]
        logistic = jax.nn.sigmoid(hidden)
        act[rows, :] = hidden * logistic
        value = cot[rows, :].astype(F32) * logistic * (1.0 + hidden * (1.0 - logistic))
        slope[me.rep, rows, :] = value.astype(BF16)

    mine = pl.ds(pl.multiple_of(own * 128, 128), 128)

    def block(n, m):
        start = me.dy(n) * 1024 + m * 256
        return ball.at[pl.ds(pl.multiple_of(start, 256), 256), mine]

    def y_copy(n, m):
        k = 24 + (n - 1) * 4 + m
        return pltpu.make_async_remote_copy(
            src_ref=block(0, m), dst_ref=block(0, m), send_sem=send.at[k], recv_sem=recv.at[k],
            device_id=y_peers[n - 1], device_id_type=MESH,
        )

    def core_copy(n, m):
        k = 36 + n * 4 + m
        return pltpu.make_async_remote_copy(
            src_ref=block(n, m), dst_ref=block(n, m), send_sem=send.at[k], recv_sem=recv.at[k],
            device_id=sibling, device_id_type=MESH,
        )

    def rows_backward(m):
        rows = rows_of(m)
        total = jnp.zeros((256, 128), F32)
        for q in range(4):
            total = total + lax.dot_general(
                slope[q, rows, :], w[:, q * 128:(q + 1) * 128], (((1,), (1,)), ((), ())), preferred_element_type=F32
            )
        here = pl.ds(pl.multiple_of(me.y * 1024 + m * 256, 256), 256)
        ball[here, mine] = (total * col[rows, :]).astype(BF16)
        for n in (2, 1, 3):
            y_copy(n, m).start()
        core_copy(0, m).start()

    def layer_step(m, _):
        @pl.when(m < 4)
        def _():
            relay(agg, 0, m)

        @pl.when(jnp.logical_and(m >= 1, m < 5))
        def _():
            settled(agg, 0, m - 1)
            rows_forward(m - 1)
            share(slope, 12, m - 1)

        @pl.when(jnp.logical_and(m >= 2, m < 6))
        def _():
            relay(slope, 12, m - 2)

        @pl.when(m >= 3)
        def _():
            settled(slope, 12, m - 3)
            rows_backward(m - 3)

        return 0

    lax.fori_loop(0, 7, layer_step, 0)

    ones = jnp.ones((8, 1024), BF16)
    for q in range(4):
        lanes = slice(q * 128, (q + 1) * 128)
        grad = jnp.dot(agg_t[...], slope[q], preferred_element_type=F32)
        gb = jnp.dot(ones, slope[q], preferred_element_type=F32)
        for n in range(4):
            gwx[n, 0:32, lanes] = grad[n * 32:(n + 1) * 32]
            gwx[n, 32:40, lanes] = gb

    def pass_blocks(m, _):
        for n in (1, 3, 2):
            y_copy(n, m).wait_recv()
            core_copy(4 - n, m).start()
        return 0

    lax.fori_loop(0, 4, pass_blocks, 0)

    def finish(m, _):
        for n in range(4):
            core_copy(n, m).wait()
        for n in (1, 2, 3):
            y_copy(n, m).wait_send()
        for kind in range(3):
            rep_copy(agg, 0, m, kind).wait_send()
            rep_copy(slope, 12, m, kind).wait_send()
        to_sibling(m).wait_send()
        return 0

    lax.fori_loop(0, 4, finish, 0)
    for k in range(3):
        to_owner(k).wait_send()


def layer(dense, g, row, col, wc, w, bias, cot):
    return pl.pallas_call(
        layer_kernel,
        out_shape=(
            jax.ShapeDtypeStruct((1024, 128), F32),
            jax.ShapeDtypeStruct((4096, 256), BF16),
            jax.ShapeDtypeStruct((4, 40, 512), F32),
        ),
        in_specs=[VMEM] * 8,
        out_specs=(VMEM, VMEM, VMEM),
        scratch_shapes=[
            pltpu.VMEM((512, 1024), BF16),
            pltpu.VMEM((512, 1024), BF16),
            pltpu.VMEM((256, 1024), F32),
            pltpu.VMEM((4, 2, 128, 1024), BF16),
            pltpu.VMEM((4, 128, 1024), BF16),
            pltpu.VMEM((3, 128, 1024), BF16),
            pltpu.VMEM((3, 128, 1024), BF16),
            pltpu.VMEM((4, 1024, 128), BF16),
            pltpu.VMEM((128, 1024), BF16),
            pltpu.VMEM((4, 1024, 128), BF16),
            DMA((4,)),
            DMA((4,)),
            DMA((3,)),
            DMA((3,)),
            DMA((52,)),
            DMA((52,)),
        ],
        compiler_params=pltpu.CompilerParams(
            collective_id=1, has_side_effects=True, vmem_limit_bytes=36 * MIB
        ),
        name="layer",
    )(dense, g, row, col, wc, w, bias, cot)


BLOCKS = ((1, 2), (1, 1), (1, 3), (1, 0), (0, 2), (0, 1), (0, 3), (0, 0))
ORDER = {key: n for n, key in enumerate(BLOCKS)}


def settle_kernel(dense, ball, gwx, out, gw, a0, a1, acc, part, az, a_sum, ax, bx, b_sum, bz, final,
                  wy, wz, wx_send, wx, send, recv, local):
    me = Place()
    sibling = me.at(c=1 - me.c)
    x_peer = me.at(x=1 - me.x)
    z_peers = [me.at(z=me.dz(n)) for n in (1, 2, 3)]
    y_peers = [me.at(y=me.dy(n)) for n in (1, 2, 3)]
    greet(z_peers + y_peers + [x_peer, sibling])

    def remote(n, src, dst, peer):
        return pltpu.make_async_remote_copy(
            src_ref=src, dst_ref=dst, send_sem=send.at[n], recv_sem=recv.at[n],
            device_id=peer, device_id_type=MESH,
        )

    x_first = {n: remote(n, part.at[ORDER[1, n], 1], bx.at[n], x_peer) for n in range(4)}
    z_first = {
        (side, n): remote(4 + side * 3 + n - 1, part.at[ORDER[side, n], 0], az.at[side, n - 1], z_peers[n - 1])
        for side in range(2) for n in (1, 2, 3)
    }
    z_second = {n: remote(9 + n, b_sum.at[n - 1], bz.at[n - 1], z_peers[n - 1]) for n in (1, 2, 3)}
    x_second = remote(13, a_sum, ax, x_peer)
    w_y = [remote(13 + n, gwx.at[me.dy(n)], wy.at[me.y], y_peers[n - 1]) for n in (1, 2, 3)]
    w_z = [remote(16 + n, wz.at[me.z], wz.at[me.z], z_peers[n - 1]) for n in (1, 2, 3)]
    w_x = remote(20, wx_send, wx, x_peer)
    w_back = [remote(20 + n, gw.at[me.y], gw.at[me.y], y_peers[n - 1]) for n in (1, 2, 3)]

    def pass_b(n):
        x_first[n].wait_recv()
        b_sum[n - 1] = (part[ORDER[0, n], 1].astype(F32) + bx[n].astype(F32)).astype(BF16)
        z_second[n].start()

    def pass_a():
        total = part[ORDER[1, 0], 0].astype(F32)
        for n in (1, 2, 3):
            z_first[1, n].wait_recv()
            total = total + az[1, n - 1].astype(F32)
        a_sum[...] = total.astype(BF16)
        x_second.start()

    def weights_z():
        for copy in w_y:
            copy.wait_recv()
        wz[me.z] = (wy[0] + wy[1]) + (wy[2] + wy[3])
        for copy in w_z:
            copy.start()

    def weights_x():
        for copy in w_z:
            copy.wait_recv()
        wx_send[...] = (wz[0] + wz[1]) + (wz[2] + wz[3])
        w_x.start()

    def weights_back():
        w_x.wait_recv()
        gw[me.y] = wx_send[...] + wx[...]
        for copy in w_back:
            copy.start()

    actions = {n: [] for n in range(8)}
    for n in range(4):
        actions[ORDER[1, n]].append(x_first[n].start)
    for n in (2, 1, 3):
        actions[ORDER[0, n]].append(functools.partial(pass_b, n))
    for key, copy in z_first.items():
        actions[ORDER[key]].append(copy.start)
    actions[3].append(weights_z)
    actions[4].append(pass_a)
    actions[5].append(weights_x)
    actions[6].append(weights_back)

    for copy in w_y:
        copy.start()
    wy[me.y] = gwx[me.y]

    def chunk(c):
        at = c // 4
        x = lax.rem(me.x + table([block[0] for block in BLOCKS], at), 2)
        z = lax.rem(me.z + table([block[1] for block in BLOCKS], at), 4)
        return lax.rem(c, 4), x * 4 + z

    bufs = (a0, a1)
    unpack(dense, *chunk(0), a0)

    def two_chunks(step, _):
        block, pair = step // 2, lax.rem(step, 2)
        for h in range(2):
            unpack(dense, *chunk(jnp.minimum(step * 2 + h + 1, 31)), bufs[1 - h])
            prod = jnp.dot(bufs[h][...], ball[pair * 2 + h], preferred_element_type=F32)
            if h == 0:
                acc[...] = jnp.where(pair == 0, 0.0, acc[...]) + prod
            else:
                acc[...] += prod

        @pl.when(pair == 1)
        def _():
            part[block, 0] = acc[0:256].astype(BF16)
            part[block, 1] = acc[256:512].astype(BF16)

        for at, calls in actions.items():
            if calls:
                @pl.when(step == at * 2 + 1)
                def _():
                    for call in calls:
                        call()

        return 0

    lax.fori_loop(0, 16, two_chunks, 0)

    total = part[ORDER[0, 0], 1].astype(F32)
    x_first[0].wait_recv()
    total = total + bx[0].astype(F32)
    for n in (1, 2, 3):
        z_second[n].wait_recv()
        total = total + bz[n - 1].astype(F32)
    final[0, 256:512, :] = total[:, 0:128]
    final[1, 256:512, :] = total[:, 128:256]
    total = part[ORDER[0, 0], 0].astype(F32)
    for n in (1, 2, 3):
        z_first[0, n].wait_recv()
        total = total + az[0, n - 1].astype(F32)
    x_second.wait_recv()
    total = total + ax[...].astype(F32)
    final[0, 0:256, :] = total[:, 0:128]
    final[1, 0:256, :] = total[:, 128:256]
    swap = remote(24, final.at[1 - me.c], out.at[me.c], sibling)
    swap.start()
    keep = pltpu.make_async_copy(final.at[me.c], out.at[me.c], local)
    keep.start()
    for copy in w_back:
        copy.wait_recv()
    swap.wait_recv()
    keep.wait()
    for copy in list(x_first.values()) + list(z_first.values()) + list(z_second.values()):
        copy.wait_send()
    for copy in [x_second, w_x, swap] + w_y + w_z + w_back:
        copy.wait_send()


def settle(dense, ball, gwx):
    half = (256, 256)
    return pl.pallas_call(
        settle_kernel,
        out_shape=(
            jax.ShapeDtypeStruct((2, 512, 128), F32),
            jax.ShapeDtypeStruct((4, 40, 512), F32),
        ),
        in_specs=[VMEM] * 3,
        out_specs=(VMEM, VMEM),
        scratch_shapes=[
            pltpu.VMEM((512, 1024), BF16),
            pltpu.VMEM((512, 1024), BF16),
            pltpu.VMEM((512, 256), F32),
            pltpu.VMEM((8, 2) + half, BF16),
            pltpu.VMEM((2, 3) + half, BF16),
            pltpu.VMEM(half, BF16),
            pltpu.VMEM(half, BF16),
            pltpu.VMEM((4,) + half, BF16),
            pltpu.VMEM((3,) + half, BF16),
            pltpu.VMEM((3,) + half, BF16),
            pltpu.VMEM((2, 512, 128), F32),
            pltpu.VMEM((4, 40, 512), F32),
            pltpu.VMEM((4, 40, 512), F32),
            pltpu.VMEM((40, 512), F32),
            pltpu.VMEM((40, 512), F32),
            DMA((25,)),
            DMA((25,)),
            DMA,
        ],
        compiler_params=pltpu.CompilerParams(
            collective_id=2, has_side_effects=True, vmem_limit_bytes=36 * MIB
        ),
        name="settle",
    )(dense, ball, gwx)


def body(features, weight, bias_vector, cotangent, tile_masks, tile_rows, tile_counts):
    masks = tile_masks.reshape(8, 4, 2, 16, 16, 128)
    dense, row, col, g, wc = spread(tile_rows[0].T, tile_counts.reshape(256), masks, features, weight)
    act, ball, gwx = layer(
        dense, g.reshape(8, 256, 512), row, col, wc, weight, bias_vector.reshape(4, 128), cotangent
    )
    out, gw = settle(dense, ball.reshape(4, 1024, 256), gwx)
    out = out.reshape(8, 8, 16, 128).transpose(0, 2, 1, 3).reshape(1024, 128) * col
    return act, out, gw[:, :32].reshape(128, 512), gw[0, 32]


def solution(mesh):
    return jax.shard_map(
        body,
        mesh=mesh,
        in_specs=(
            P("blk", "rep"),
            P("rep", None),
            P(),
            P("blk", "rep"),
            P("blk", None, None, None, None),
            P("blk", None, None),
            P("blk", None),
        ),
        out_specs=(P("blk", "rep"), P("blk", "rep"), P("rep", None), P()),
        check_vma=False,
    )
```

time: 148 us -> 140 us (0.946)
  local copies, waits for them, and re-layouts: 11.5 us -> 8.85 us
  other arithmetic: 3.05 us -> 0.86 us
  Pallas kernels: 131 us -> 129 us
    pallas_call x3 -> x1, Pallas kernels: 37 us -> 44.7 us  [spread(): pl.pallas_call(spread_kernel, out_shape=(jax.ShapeDtypeStruct((32, 4, 8,...]
    pallas_call x1, Pallas kernels: 38.3 us -> 32.8 us  [settle(): pl.pallas_call(settle_kernel, out_shape=(jax.ShapeDtypeStruct((2, 512, 12...]
    pallas_call x1, Pallas kernels: 55.3 us -> 51.3 us  [layer(): pl.pallas_call(layer_kernel, out_shape=(jax.ShapeDtypeStruct((1024, 128),...]
    unnamed x12 -> x15, local copies, waits for them, and re-layouts: 8.24 us -> 7.39 us
where the time goes in v3:
time: 140 us; the launch traced here: 139 us
  Pallas kernels  129 us (92%)
  local copies, waits for them, and re-layouts  8.85 us (6%)
    pallas_call x1, Pallas kernels, layer(): pl.pallas_call(layer_kernel, out_shape=(jax.ShapeDtypeStruct((1024, 128),...  51.3 us
    pallas_call x1, Pallas kernels, spread(): pl.pallas_call(spread_kernel, out_shape=(jax.ShapeDtypeStruct((32, 4, 8,...  44.7 us
    pallas_call x1, Pallas kernels, settle(): pl.pallas_call(settle_kernel, out_shape=(jax.ShapeDtypeStruct((2, 512, 12...  32.8 us
    unnamed x15, local copies, waits for them, and re-layouts  7.39 us

profile of v3, /device:TPU:6, one launch (start us, length us, event | category | flops | bytes accessed | tf_op | source)
XLA Modules:
  0.0 139.2 jit_solution(9579302613916342089)
XLA Ops:
  0.6 0.0 copy-start
  0.6 3.4 %copy-done = s32[1,256,4,16,128]{4,3,2,1,0:T(8,128)S(1)} copy-done((s32[1,256,4,16,128]{4,3,2,1,0:T(8,128)S(1)}, s32[1,256,4,16,128]{4,3,2,1,0:T(8,128)}, u32[]{:S(2)}) %copy-start) | copy-done | bytes 8388632
  4.0 0.0 copy-start.1
  4.0 0.9 copy-done.1
  4.9 0.0 copy-start.2
  4.9 0.9 copy-done.2
  5.9 0.0 copy-start.4
  5.9 0.7 copy-done.4
  6.6 0.0 copy-start.6
  6.6 0.7 copy-done.6
  7.2 0.0 copy-start.3
  7.2 0.0 copy-start.5
  7.2 44.7 %spread.1 = (s16[32,4,8,16,128]{4,3,2,1,0:T(8,128)(2,1)S(1)}, f32[8,1024]{1,0:T(8,128)S(1)}, f32[1024,128]{1,0:T(8,128)S(1)}, bf16[8,2,128,512]{3,2,1,0:T(8,128)(2,1)S(1)}, bf16[4,128,128]{2,1,0:T(8,128)(2,1)S(1)}) custom-call(s32[4,256]{1,0:T(4,128)S(1)} %bitcast.19, s32[256]{0:T(256)S(1)} %bitcast.21, s32[8,4,2,16,16,128]{5,4,3,2,1,0:T(8,128)S(1)} %bitcast.15, ...), custom_call_target="tpu_custom_call" | custom-call | tf_op jit(solution)/shard_map/spread/pallas_call | solution.py:209
  51.9 0.0 copy-done.3
  51.9 0.0 copy-done.5
  51.9 51.3 %layer.1 = (f32[1024,128]{1,0:T(8,128)S(1)}, bf16[4096,256]{1,0:T(8,128)(2,1)S(1)}, f32[4,40,512]{2,1,0:T(8,128)S(1)}) custom-call(s16[32,4,8,16,128]{4,3,2,1,0:T(8,128)(2,1)S(1)} %get-tuple-element.14.dense, bf16[8,256,512]{2,1,0:T(8,128)(2,1)S(1)} %bitcast.17, f32[8,1024]{1,0:T(8,128)S(1)} %get-tuple-element.16.row, ...), custom_call_target="tpu_custom_call" | custom-call | tf_op jit(solution)/shard_map/layer/pallas_call | solution.py:458
  103.3 32.8 %settle.1 = (f32[2,512,128]{2,1,0:T(8,128)S(1)}, f32[4,40,512]{2,1,0:T(8,128)S(1)}) custom-call(s16[32,4,8,16,128]{4,3,2,1,0:T(8,128)(2,1)S(1)} %get-tuple-element.14.dense, bf16[4,1024,256]{2,1,0:T(8,128)(2,1)S(1)} %bitcast.16, f32[4,40,512]{2,1,0:T(8,128)S(1)} %get-tuple-element.21.gwx), custom_call_target="tpu_custom_call" | custom-call | tf_op jit(solution)/shard_map/settle/pallas_call | solution.py:638
  136.0 0.2 copy.11
  136.2 0.9 bitcast_multiply_fusion
  137.1 0.6 slice.7
  137.7 0.7 slice.6
  138.4 0.8 copy.13
Async XLA Ops:
  0.6 3.4 %copy-start = (s32[1,256,4,16,128]{4,3,2,1,0:T(8,128)S(1)}, s32[1,256,4,16,128]{4,3,2,1,0:T(8,128)}, u32[]{:S(2)}) copy-start(s32[1,256,4,16,128]{4,3,2,1,0:T(8,128)} %param.11) | copy-start | bytes 25165828
  4.0 0.9 copy-start.1
  4.9 0.9 copy-start.2
  5.9 0.7 copy-start.4
  6.6 0.7 copy-start.6
  7.2 44.7 %copy-start.3 = (bf16[1024,128]{1,0:T(8,128)(2,1)S(1)}, bf16[1024,128]{1,0:T(8,128)(2,1)}, u32[]{:S(2)}) copy-start(bf16[1024,128]{1,0:T(8,128)(2,1)} %cot.1) | copy-start | bytes 786436
  7.2 44.7 %copy-start.5 = (f32[512]{0:T(512)S(1)}, f32[512]{0:T(512)}, u32[]{:S(2)}) copy-start(f32[512]{0:T(512)} %param.9) | copy-start | bytes 6148

commit v4 on v3

--- a/solution.py
+++ b/solution.py
@@ -163,19 +163,12 @@
     second = [copies.start(at(other, me.xz), at(other, me.xz), p) for p in z_peers]
     weights = [copies.start(weight_to(peer[1]), wc.at[me.rep], peer) for peer in rep_peers]
 
-    kept.wait()
-    for copy in slot_copies:
-        copy.wait_recv()
-    to_smem = pltpu.make_async_copy(landed_v, landed_s, local.at[4])
-    to_smem.start()
-    to_smem.wait()
-
-    def put_tiles(n):
+    def put_tiles(n, slot_rows, at):
         i = me.dy(n)
 
         def column(j, _):
             for tc in range(4):
-                rows = [landed_s[i, 0, j * 16 + tc * 4 + s] for s in range(4)]
+                rows = [slot_rows[at, 0, j * 16 + tc * 4 + s] for s in range(4)]
                 tiles = [rm[i, j, tc * 4 + s] for s in range(4)]
                 for t in range(8):
                     found = jnp.zeros((16, 128), jnp.int16)
@@ -186,7 +179,6 @@
 
         lax.fori_loop(0, 8, column, 0)
 
-    put_tiles(0)
     last = []
     for n in (1, 2, 3):
         first[n - 1].wait_recv()
@@ -195,9 +187,16 @@
     other_x.wait_recv()
     far = (1 - me.x) * 4 + me.z
     last += [copies.start(at(other, far), at(other, far), p) for p in z_peers]
+    put_tiles(0, slots_s, 3)
+    kept.wait()
+    for copy in slot_copies:
+        copy.wait_recv()
+    to_smem = pltpu.make_async_copy(landed_v, landed_s, local.at[4])
+    to_smem.start()
+    to_smem.wait()
     for q in range(3):
         mask_copies[q].wait_recv()
-        put_tiles(4 - Y_ORDER[q])
+        put_tiles(4 - Y_ORDER[q], landed_s, me.dy(4 - Y_ORDER[q]))
     for copy in [across] + weights + second + last:
         copy.wait_recv()
     copies.wait_sends()
@@ -232,7 +231,7 @@
             DMA((5,)),
         ],
         compiler_params=pltpu.CompilerParams(
-            collective_id=0, has_side_effects=True, vmem_limit_bytes=32 * MIB
+            collective_id=0, has_side_effects=True, vmem_limit_bytes=44 * MIB
         ),
         name="spread",
     )(rows, counts, masks, features, w)
@@ -273,19 +272,21 @@
             device_id=sibling, device_id_type=MESH,
         )
 
-    def to_owner(s):
-        return pltpu.make_async_remote_copy(
-            src_ref=snd.at[s], dst_ref=ry.at[s], send_sem=sum_s.at[s], recv_sem=sum_r.at[s],
-            device_id=me.at(y=me.dy(table((2, 1, 3), s))), device_id_type=MESH,
-        )
-
-    def pass_on(s):
-        to_sibling(s).wait_recv()
-        snd[s] = (part[s, own].astype(F32) + rc[s].astype(F32)).astype(BF16)
-        to_owner(s).start()
-
     def rows_of(m):
         return pl.ds(pl.multiple_of(m * 256, 256), 256)
+
+    def to_owner(k, m):
+        return pltpu.make_async_remote_copy(
+            src_ref=snd.at[k, m], dst_ref=ry.at[k, m], send_sem=sum_s.at[k * 4 + m], recv_sem=sum_r.at[k * 4 + m],
+            device_id=me.at(y=me.dy(table((2, 1, 3), k))), device_id_type=MESH,
+        )
+
+    def pass_on(k):
+        to_sibling(k).wait_recv()
+        for m in range(4):
+            rows = slice(m * 256, (m + 1) * 256)
+            snd[k, m] = (part[k, own, :, rows].astype(F32) + rc[k, :, rows].astype(F32)).astype(BF16)
+            to_owner(k, m).start()
 
     def rep_copy(buf, base, m, kind):
         theirs = (1 - me.xl) * 2 + me.c
@@ -301,10 +302,12 @@
         rep_copy(buf, base, m, 0).start()
 
     def finish_sum(m):
-        rows = rows_of(m)
+        for k in range(3):
+            to_owner(k, m).wait_recv()
+        rows = slice(m * 256, (m + 1) * 256)
         total = part[3, own, :, rows].astype(F32) + rc[3, :, rows].astype(F32)
         for k in range(3):
-            total = total + ry[k, :, rows].astype(F32)
+            total = total + ry[k, m].astype(F32)
         total = total * row[0:1, rows]
         agg_t[:, rows] = total.astype(BF16)
         agg[me.rep, rows, :] = total.T.astype(BF16)
@@ -340,8 +343,6 @@
 
     lax.fori_loop(0, 16, two_chunks, 0)
     to_sibling(3).wait_recv()
-    for k in range(3):
-        to_owner(k).wait_recv()
     for m in range(4):
         finish_sum(m)
 
@@ -443,6 +444,7 @@
             core_copy(n, m).wait()
         for n in (1, 2, 3):
             y_copy(n, m).wait_send()
+            to_owner(n - 1, m).wait_send()
         for kind in range(3):
             rep_copy(agg, 0, m, kind).wait_send()
             rep_copy(slope, 12, m, kind).wait_send()
@@ -450,8 +452,6 @@
         return 0
 
     lax.fori_loop(0, 4, finish, 0)
-    for k in range(3):
-        to_owner(k).wait_send()
 
 
 def layer(dense, g, row, col, wc, w, bias, cot):
@@ -470,15 +470,15 @@
             pltpu.VMEM((256, 1024), F32),
             pltpu.VMEM((4, 2, 128, 1024), BF16),
             pltpu.VMEM((4, 128, 1024), BF16),
-            pltpu.VMEM((3, 128, 1024), BF16),
-            pltpu.VMEM((3, 128, 1024), BF16),
+            pltpu.VMEM((3, 4, 128, 256), BF16),
+            pltpu.VMEM((3, 4, 128, 256), BF16),
             pltpu.VMEM((4, 1024, 128), BF16),
             pltpu.VMEM((128, 1024), BF16),
             pltpu.VMEM((4, 1024, 128), BF16),
             DMA((4,)),
             DMA((4,)),
-            DMA((3,)),
-            DMA((3,)),
+            DMA((12,)),
+            DMA((12,)),
             DMA((52,)),
             DMA((52,)),
         ],

time: 140 us -> 124 us (0.89)
  Pallas kernels: 129 us -> 116 us
  local copies, waits for them, and re-layouts: 8.85 us -> 5.48 us
    pallas_call x1, Pallas kernels: 44.7 us -> 35.8 us  [spread(): pl.pallas_call(spread_kernel, out_shape=(jax.ShapeDtypeStruct((32, 4, 8,...]
    unnamed x15, local copies, waits for them, and re-layouts: 7.39 us -> 4.02 us
    pallas_call x1, Pallas kernels: 51.3 us -> 48.4 us  [layer(): pl.pallas_call(layer_kernel, out_shape=(jax.ShapeDtypeStruct((1024, 128),...]
where the time goes in v4:
time: 124 us
  Pallas kernels  116 us (94%)
  local copies, waits for them, and re-layouts  5.48 us (4%)
    pallas_call x1, Pallas kernels, layer(): pl.pallas_call(layer_kernel, out_shape=(jax.ShapeDtypeStruct((1024, 128),...  48.4 us
    pallas_call x1, Pallas kernels, spread(): pl.pallas_call(spread_kernel, out_shape=(jax.ShapeDtypeStruct((32, 4, 8,...  35.8 us
    pallas_call x1, Pallas kernels, settle(): pl.pallas_call(settle_kernel, out_shape=(jax.ShapeDtypeStruct((2, 512, 12...  32.3 us
    unnamed x15, local copies, waits for them, and re-layouts  4.02 us

profile of v4, /device:TPU:6, one launch (start us, length us, event | category | flops | bytes accessed | tf_op | source)
XLA Modules:
  0.0 123.5 jit_solution(12953449583625241595)
XLA Ops:
  0.6 0.0 copy-start
  0.6 0.9 copy-done
  1.5 0.0 copy-start.2
  1.5 0.9 copy-done.2
  2.5 0.0 copy-start.4
  2.5 0.7 copy-done.4
  3.2 0.0 copy-start.6
  3.2 0.7 copy-done.6
  3.9 0.0 copy-start.1
  3.9 0.0 copy-start.3
  3.9 0.0 copy-start.5
  3.9 35.8 %spread.1 = (s16[32,4,8,16,128]{4,3,2,1,0:T(8,128)(2,1)S(1)}, f32[8,1024]{1,0:T(8,128)S(1)}, f32[1024,128]{1,0:T(8,128)S(1)}, bf16[8,2,128,512]{3,2,1,0:T(8,128)(2,1)S(1)}, bf16[4,128,128]{2,1,0:T(8,128)(2,1)S(1)}) custom-call(s32[4,256]{1,0:T(4,128)S(1)} %bitcast.18, s32[256]{0:T(256)S(1)} %bitcast.20, s32[8,4,2,16,16,128]{5,4,3,2,1,0:T(8,128)} %bitcast.21, ...), custom_call_target="tpu_custom_call" | custom-call | tf_op jit(solution)/shard_map/spread/pallas_call | solution.py:208
  39.7 0.0 copy-done.1
  39.7 0.0 copy-done.3
  39.7 0.0 copy-done.5
  39.7 48.4 %layer.1 = (f32[1024,128]{1,0:T(8,128)S(1)}, bf16[4096,256]{1,0:T(8,128)(2,1)S(1)}, f32[4,40,512]{2,1,0:T(8,128)S(1)}) custom-call(s16[32,4,8,16,128]{4,3,2,1,0:T(8,128)(2,1)S(1)} %get-tuple-element.14.dense, bf16[8,256,512]{2,1,0:T(8,128)(2,1)S(1)} %bitcast.16, f32[8,1024]{1,0:T(8,128)S(1)} %get-tuple-element.16.row, ...), custom_call_target="tpu_custom_call" | custom-call | tf_op jit(solution)/shard_map/layer/pallas_call | solution.py:458
  88.1 32.3 %settle.1 = (f32[2,512,128]{2,1,0:T(8,128)S(1)}, f32[4,40,512]{2,1,0:T(8,128)S(1)}) custom-call(s16[32,4,8,16,128]{4,3,2,1,0:T(8,128)(2,1)S(1)} %get-tuple-element.14.dense, bf16[4,1024,256]{2,1,0:T(8,128)(2,1)S(1)} %bitcast.15, f32[4,40,512]{2,1,0:T(8,128)S(1)} %get-tuple-element.21.gwx), custom_call_target="tpu_custom_call" | custom-call | tf_op jit(solution)/shard_map/settle/pallas_call | solution.py:638
  120.4 0.2 copy.11
  120.6 0.9 bitcast_multiply_fusion
  121.4 0.6 slice.7
  122.0 0.7 slice.6
  122.7 0.8 copy.13
Async XLA Ops:
  0.6 0.9 copy-start
  1.5 0.9 copy-start.2
  2.5 0.7 copy-start.4
  3.2 0.7 copy-start.6
  3.9 35.8 %copy-start.1 = (bf16[128,512]{1,0:T(8,128)(2,1)S(1)}, bf16[128,512]{1,0:T(8,128)(2,1)}, u32[]{:S(2)}) copy-start(bf16[128,512]{1,0:T(8,128)(2,1)} %w.3) | copy-start | bytes 393220
  3.9 35.8 %copy-start.3 = (bf16[1024,128]{1,0:T(8,128)(2,1)S(1)}, bf16[1024,128]{1,0:T(8,128)(2,1)}, u32[]{:S(2)}) copy-start(bf16[1024,128]{1,0:T(8,128)(2,1)} %cot.1) | copy-start | bytes 786436
  3.9 35.8 %copy-start.5 = (f32[512]{0:T(512)S(1)}, f32[512]{0:T(512)}, u32[]{:S(2)}) copy-start(f32[512]{0:T(512)} %param.9) | copy-start | bytes 6148

commit v5 on v4

--- a/solution.py
+++ b/solution.py
@@ -69,7 +69,7 @@
 Y_ORDER = (2, 1, 3, 0)
 
 
-def spread_kernel(rows_ref, counts_ref, masks, feat, w, dense, row, col, g, wc,
+def spread_kernel(rows_ref, counts_ref, masks, feat, w, cot, dense, row, col, g, wc, cotr,
                   words, m16, rm, slots_s, slots_v, landed_v, landed_s, xt, send, recv, load, local):
     me = Place()
     own, other = me.c, 1 - me.c
@@ -87,6 +87,13 @@
     greet(z_peers + y_peers + rep_peers + [x_peer])
     copies = Copies(send, recv)
 
+    def cot_rows(rep):
+        return cot.at[pl.ds(pl.multiple_of(rep * 256, 256), 256), :]
+
+    early = []
+    for peer in rep_peers:
+        early.append(copies.start(cot_rows(peer[1]), cotr.at[me.rep], peer))
+        early.append(copies.start(w, wc.at[me.rep], peer))
     tile_row = lax.broadcasted_iota(jnp.int32, (8, 128), 0)
 
     def scan(q, degrees):
@@ -139,15 +146,13 @@
     def at(core, xz):
         return g.at[xz, core]
 
-    def weight_to(rep):
-        return w.at[:, pl.ds(pl.multiple_of(rep * 128, 128), 128)]
-
     to_sibling = copies.start(xt.at[other], at(own, me.xz), sibling)
     first = [copies.start(xt.at[own], at(own, me.xz), p) for p in z_peers]
     across = copies.start(xt.at[own], at(own, me.xz), x_peer)
     stays = [
         pltpu.make_async_copy(xt.at[own], at(own, me.xz), local.at[0]),
-        pltpu.make_async_copy(weight_to(me.rep), wc.at[me.rep], local.at[1]),
+        pltpu.make_async_copy(w, wc.at[me.rep], local.at[1]),
+        pltpu.make_async_copy(cot_rows(me.rep), cotr.at[me.rep], local.at[5]),
     ]
     for copy in stays:
         copy.start()
@@ -161,7 +166,6 @@
     to_sibling.wait_recv()
     other_x = copies.start(at(other, me.xz), at(other, me.xz), x_peer)
     second = [copies.start(at(other, me.xz), at(other, me.xz), p) for p in z_peers]
-    weights = [copies.start(weight_to(peer[1]), wc.at[me.rep], peer) for peer in rep_peers]
 
     def put_tiles(n, slot_rows, at):
         i = me.dy(n)
@@ -197,14 +201,14 @@
     for q in range(3):
         mask_copies[q].wait_recv()
         put_tiles(4 - Y_ORDER[q], landed_s, me.dy(4 - Y_ORDER[q]))
-    for copy in [across] + weights + second + last:
+    for copy in [across] + early + second + last:
         copy.wait_recv()
     copies.wait_sends()
     for copy in stays:
         copy.wait()
 
 
-def spread(rows, counts, masks, features, w):
+def spread(rows, counts, masks, features, w, cot):
     return pl.pallas_call(
         spread_kernel,
         out_shape=(
@@ -212,10 +216,11 @@
             jax.ShapeDtypeStruct((8, 1024), F32),
             jax.ShapeDtypeStruct((1024, 128), F32),
             jax.ShapeDtypeStruct((8, 2, 128, 512), BF16),
-            jax.ShapeDtypeStruct((4, 128, 128), BF16),
+            jax.ShapeDtypeStruct((4, 128, 512), BF16),
+            jax.ShapeDtypeStruct((4, 256, 128), BF16),
         ),
-        in_specs=[SMEM, SMEM, pl.BlockSpec(memory_space=pltpu.HBM), VMEM, VMEM],
-        out_specs=(VMEM,) * 5,
+        in_specs=[SMEM, SMEM, pl.BlockSpec(memory_space=pltpu.HBM), VMEM, VMEM, VMEM],
+        out_specs=(VMEM,) * 6,
         scratch_shapes=[
             pltpu.VMEM((8, 8, 16, 16, 128), jnp.int32),
             pltpu.VMEM((3, 8, 16, 16, 128), jnp.int16),
@@ -225,16 +230,16 @@
             pltpu.VMEM((4, 1, 128), jnp.int32),
             pltpu.SMEM((4, 1, 128), jnp.int32),
             pltpu.VMEM((2, 128, 512), BF16),
-            DMA((24,)),
-            DMA((24,)),
+            DMA((27,)),
+            DMA((27,)),
             DMA((8,)),
-            DMA((5,)),
+            DMA((6,)),
         ],
         compiler_params=pltpu.CompilerParams(
             collective_id=0, has_side_effects=True, vmem_limit_bytes=44 * MIB
         ),
         name="spread",
-    )(rows, counts, masks, features, w)
+    )(rows, counts, masks, features, w, cot)
 
 
 def table(values, step):
@@ -255,14 +260,15 @@
                 out_ref[first:first + 16, t * 128:(t + 1) * 128] = bits
 
 
-def layer_kernel(dense, g, row, col, wc, w, bias, cot, act, ball, gwx,
-                 a0, a1, acc, part, rc, snd, ry, agg, agg_t, slope,
+def layer_kernel(dense, g, row, col, wc, bias, cotr, act, ball, gwx,
+                 a0, a1, acc, part, rc, snd, ry, agg_s, agg, agg_t, slope, act_s, back_s,
                  core_s, core_r, sum_s, sum_r, send, recv):
     me = Place()
     sibling = me.at(c=1 - me.c)
     xl_peer = me.at(xl=1 - me.xl)
+    xl_other = me.at(xl=1 - me.xl, c=1 - me.c)
     y_peers = [me.at(y=me.dy(n)) for n in (1, 2, 3)]
-    greet([sibling, xl_peer] + y_peers)
+    greet([sibling, xl_peer, xl_other] + y_peers)
     copies = Copies(send, recv)
     own, other = me.c, 1 - me.c
 
@@ -287,31 +293,6 @@
             rows = slice(m * 256, (m + 1) * 256)
             snd[k, m] = (part[k, own, :, rows].astype(F32) + rc[k, :, rows].astype(F32)).astype(BF16)
             to_owner(k, m).start()
-
-    def rep_copy(buf, base, m, kind):
-        theirs = (1 - me.xl) * 2 + me.c
-        src = buf.at[theirs if kind == 2 else me.rep, rows_of(m), :]
-        n = base + kind * 4 + m
-        return pltpu.make_async_remote_copy(
-            src_ref=src, dst_ref=src, send_sem=send.at[n], recv_sem=recv.at[n],
-            device_id=xl_peer if kind == 1 else sibling, device_id_type=MESH,
-        )
-
-    def share(buf, base, m):
-        rep_copy(buf, base, m, 1).start()
-        rep_copy(buf, base, m, 0).start()
-
-    def finish_sum(m):
-        for k in range(3):
-            to_owner(k, m).wait_recv()
-        rows = slice(m * 256, (m + 1) * 256)
-        total = part[3, own, :, rows].astype(F32) + rc[3, :, rows].astype(F32)
-        for k in range(3):
-            total = total + ry[k, m].astype(F32)
-        total = total * row[0:1, rows]
-        agg_t[:, rows] = total.astype(BF16)
-        agg[me.rep, rows, :] = total.T.astype(BF16)
-        share(agg, 0, m)
 
     def chunk(c):
         return me.dy(table((2, 1, 3, 0), c // 8)), lax.rem(c, 8)
@@ -343,118 +324,102 @@
 
     lax.fori_loop(0, 16, two_chunks, 0)
     to_sibling(3).wait_recv()
-    for m in range(4):
-        finish_sum(m)
-
-    def relay(buf, base, m):
-        rep_copy(buf, base, m, 1).wait_recv()
-        rep_copy(buf, base, m, 2).start()
-
-    def settled(buf, base, m):
-        rep_copy(buf, base, m, 0).wait_recv()
-        rep_copy(buf, base, m, 2).wait_recv()
-
-    def rows_forward(m):
+
+    def finish_sum(m, out):
+        for k in range(3):
+            to_owner(k, m).wait_recv()
         rows = rows_of(m)
+        total = part[3, own, :, rows].astype(F32) + rc[3, :, rows].astype(F32)
+        for k in range(3):
+            total = total + ry[k, m].astype(F32)
+        total = total * row[0:1, rows]
+        agg_t[:, rows] = total.astype(BF16)
+        out[...] = total.T.astype(BF16)
+
+    swaps = []
+    peers = (xl_peer, xl_other, sibling)
+    for n in range(3):
+        finish_sum(peers[n][1], agg_s.at[n])
+        swaps.append(copies.start(agg_s.at[n], agg.at[me.rep], peers[n]))
+    finish_sum(me.rep, agg.at[me.rep])
+    for copy in reversed(swaps):
+        copy.wait_recv()
+
+    for half in range(2):
+        rows = slice(half * 128, (half + 1) * 128)
         hidden = jnp.dot(agg[0, rows, :], wc[0], preferred_element_type=F32)
         for q in range(1, 4):
             hidden = hidden + jnp.dot(agg[q, rows, :], wc[q], preferred_element_type=F32)
-        hidden = hidden + bias[pl.ds(me.rep, 1), :]
+        hidden = hidden + bias[...]
         logistic = jax.nn.sigmoid(hidden)
-        act[rows, :] = hidden * logistic
-        value = cot[rows, :].astype(F32) * logistic * (1.0 + hidden * (1.0 - logistic))
-        slope[me.rep, rows, :] = value.astype(BF16)
-
-    mine = pl.ds(pl.multiple_of(own * 128, 128), 128)
-
-    def block(n, m):
-        start = me.dy(n) * 1024 + m * 256
-        return ball.at[pl.ds(pl.multiple_of(start, 256), 256), mine]
-
-    def y_copy(n, m):
-        k = 24 + (n - 1) * 4 + m
-        return pltpu.make_async_remote_copy(
-            src_ref=block(0, m), dst_ref=block(0, m), send_sem=send.at[k], recv_sem=recv.at[k],
-            device_id=y_peers[n - 1], device_id_type=MESH,
-        )
-
-    def core_copy(n, m):
-        k = 36 + n * 4 + m
-        return pltpu.make_async_remote_copy(
-            src_ref=block(n, m), dst_ref=block(n, m), send_sem=send.at[k], recv_sem=recv.at[k],
-            device_id=sibling, device_id_type=MESH,
-        )
-
-    def rows_backward(m):
-        rows = rows_of(m)
-        total = jnp.zeros((256, 128), F32)
+        value = hidden * logistic
+        factor = logistic * (1.0 + hidden * (1.0 - logistic))
         for q in range(4):
-            total = total + lax.dot_general(
-                slope[q, rows, :], w[:, q * 128:(q + 1) * 128], (((1,), (1,)), ((), ())), preferred_element_type=F32
+            lanes = slice(q * 128, (q + 1) * 128)
+            act_s[q, rows, :] = value[:, lanes]
+            slope[me.rep, rows, lanes] = (cotr[q, rows, :].astype(F32) * factor[:, lanes]).astype(BF16)
+
+    def block(y, rep):
+        return ball.at[pl.ds(pl.multiple_of(y * 1024 + rep * 256, 256), 256), :]
+
+    def back_into(xl, out):
+        for core in range(2):
+            value = lax.dot_general(
+                slope[me.rep], wc[xl * 2 + core], (((1,), (1,)), ((), ())), preferred_element_type=F32
             )
-        here = pl.ds(pl.multiple_of(me.y * 1024 + m * 256, 256), 256)
-        ball[here, mine] = (total * col[rows, :]).astype(BF16)
-        for n in (2, 1, 3):
-            y_copy(n, m).start()
-        core_copy(0, m).start()
-
-    def layer_step(m, _):
-        @pl.when(m < 4)
-        def _():
-            relay(agg, 0, m)
-
-        @pl.when(jnp.logical_and(m >= 1, m < 5))
-        def _():
-            settled(agg, 0, m - 1)
-            rows_forward(m - 1)
-            share(slope, 12, m - 1)
-
-        @pl.when(jnp.logical_and(m >= 2, m < 6))
-        def _():
-            relay(slope, 12, m - 2)
-
-        @pl.when(m >= 3)
-        def _():
-            settled(slope, 12, m - 3)
-            rows_backward(m - 3)
-
-        return 0
-
-    lax.fori_loop(0, 7, layer_step, 0)
-
-    ones = jnp.ones((8, 1024), BF16)
-    for q in range(4):
-        lanes = slice(q * 128, (q + 1) * 128)
-        grad = jnp.dot(agg_t[...], slope[q], preferred_element_type=F32)
-        gb = jnp.dot(ones, slope[q], preferred_element_type=F32)
-        for n in range(4):
-            gwx[n, 0:32, lanes] = grad[n * 32:(n + 1) * 32]
-            gwx[n, 32:40, lanes] = gb
-
-    def pass_blocks(m, _):
-        for n in (1, 3, 2):
-            y_copy(n, m).wait_recv()
-            core_copy(4 - n, m).start()
-        return 0
-
-    lax.fori_loop(0, 4, pass_blocks, 0)
-
-    def finish(m, _):
-        for n in range(4):
-            core_copy(n, m).wait()
-        for n in (1, 2, 3):
-            y_copy(n, m).wait_send()
-            to_owner(n - 1, m).wait_send()
-        for kind in range(3):
-            rep_copy(agg, 0, m, kind).wait_send()
-            rep_copy(slope, 12, m, kind).wait_send()
-        to_sibling(m).wait_send()
-        return 0
-
-    lax.fori_loop(0, 4, finish, 0)
-
-
-def layer(dense, g, row, col, wc, w, bias, cot):
+            out[:, core * 128:(core + 1) * 128] = (value * col[rows_of(me.rep), :]).astype(BF16)
+
+    theirs = (1 - me.xl) * 2 + me.c
+    back_into(1 - me.xl, back_s)
+    from_xl = copies.start(back_s, block(me.y, me.rep), xl_peer)
+    back_into(me.xl, block(me.y, me.rep))
+
+    def send_block(rep):
+        here = block(me.y, rep)
+        return [copies.start(here, here, y_peers[n - 1]) for n in (2, 1, 3)] + [copies.start(here, here, sibling)]
+
+    mine = send_block(me.rep)
+    slope_far = copies.start(slope.at[me.rep], slope.at[me.rep], xl_peer)
+    slope_near = copies.start(slope.at[me.rep], slope.at[me.rep], sibling)
+    from_xl.wait_recv()
+    passed = send_block(theirs)
+    acts = [
+        copies.start(act_s.at[peer[1]], act.at[rows_of(me.rep), :], peer)
+        for peer in (xl_peer, xl_other, sibling)
+    ]
+    act[rows_of(me.rep), :] = act_s[me.rep]
+    slope_far.wait_recv()
+    slope_relay = copies.start(slope.at[theirs], slope.at[theirs], sibling)
+
+    relays = []
+    for sent, rep in ((mine, me.rep), (passed, theirs)):
+        if rep is theirs:
+            slope_near.wait_recv()
+            slope_relay.wait_recv()
+            ones = jnp.ones((8, 256), BF16)
+            grad = jnp.zeros((128, 512), F32)
+            gb = jnp.zeros((8, 512), F32)
+            for q in range(4):
+                grad = grad + jnp.dot(agg_t[:, q * 256:(q + 1) * 256], slope[q], preferred_element_type=F32)
+                gb = gb + jnp.dot(ones, slope[q], preferred_element_type=F32)
+            for n in range(4):
+                gwx[n, 0:32, :] = grad[n * 32:(n + 1) * 32]
+                gwx[n, 32:40, :] = gb
+        for n, copy in zip((2, 1, 3), sent):
+            copy.wait_recv()
+            here = block(me.dy(4 - n), rep)
+            relays.append(copies.start(here, here, sibling))
+    for copy in [mine[3], passed[3]] + relays + acts:
+        copy.wait_recv()
+    copies.wait_sends()
+    for k in range(3):
+        for m in range(4):
+            to_owner(k, m).wait_send()
+    for k in range(4):
+        to_sibling(k).wait_send()
+
+
+def layer(dense, g, row, col, wc, bias, cotr):
     return pl.pallas_call(
         layer_kernel,
         out_shape=(
@@ -462,7 +427,7 @@
             jax.ShapeDtypeStruct((4096, 256), BF16),
             jax.ShapeDtypeStruct((4, 40, 512), F32),
         ),
-        in_specs=[VMEM] * 8,
+        in_specs=[VMEM] * 7,
         out_specs=(VMEM, VMEM, VMEM),
         scratch_shapes=[
             pltpu.VMEM((512, 1024), BF16),
@@ -472,21 +437,24 @@
             pltpu.VMEM((4, 128, 1024), BF16),
             pltpu.VMEM((3, 4, 128, 256), BF16),
             pltpu.VMEM((3, 4, 128, 256), BF16),
-            pltpu.VMEM((4, 1024, 128), BF16),
+            pltpu.VMEM((3, 256, 128), BF16),
+            pltpu.VMEM((4, 256, 128), BF16),
             pltpu.VMEM((128, 1024), BF16),
-            pltpu.VMEM((4, 1024, 128), BF16),
+            pltpu.VMEM((4, 256, 512), BF16),
+            pltpu.VMEM((4, 256, 128), F32),
+            pltpu.VMEM((256, 256), BF16),
             DMA((4,)),
             DMA((4,)),
             DMA((12,)),
             DMA((12,)),
-            DMA((52,)),
-            DMA((52,)),
+            DMA((24,)),
+            DMA((24,)),
         ],
         compiler_params=pltpu.CompilerParams(
             collective_id=1, has_side_effects=True, vmem_limit_bytes=36 * MIB
         ),
         name="layer",
-    )(dense, g, row, col, wc, w, bias, cot)
+    )(dense, g, row, col, wc, bias, cotr)
 
 
 BLOCKS = ((1, 2), (1, 1), (1, 3), (1, 0), (0, 2), (0, 1), (0, 3), (0, 0))
@@ -672,10 +640,10 @@
 
 def body(features, weight, bias_vector, cotangent, tile_masks, tile_rows, tile_counts):
     masks = tile_masks.reshape(8, 4, 2, 16, 16, 128)
-    dense, row, col, g, wc = spread(tile_rows[0].T, tile_counts.reshape(256), masks, features, weight)
-    act, ball, gwx = layer(
-        dense, g.reshape(8, 256, 512), row, col, wc, weight, bias_vector.reshape(4, 128), cotangent
+    dense, row, col, g, wc, cotr = spread(
+        tile_rows[0].T, tile_counts.reshape(256), masks, features, weight, cotangent
     )
+    act, ball, gwx = layer(dense, g.reshape(8, 256, 512), row, col, wc, bias_vector.reshape(1, 512), cotr)
     out, gw = settle(dense, ball.reshape(4, 1024, 256), gwx)
     out = out.reshape(8, 8, 16, 128).transpose(0, 2, 1, 3).reshape(1024, 128) * col
     return act, out, gw[:, :32].reshape(128, 512), gw[0, 32]

time: 124 us -> 123 us (level)
  Pallas kernels: 116 us -> 114 us
    pallas_call x1, Pallas kernels: 48.4 us -> 45.8 us  [layer(): pl.pallas_call(layer_kernel, out_shape=(jax.ShapeDtypeStruct((1024, 128),...]
    unnamed x15 -> x13, local copies, waits for them, and re-layouts: 4.02 us -> 4.96 us
where the time goes in v5:
time: 123 us; the launch traced here: 122 us
  Pallas kernels  114 us (93%)
  local copies, waits for them, and re-layouts  6.42 us (5%)
    pallas_call x1, Pallas kernels, layer(): pl.pallas_call(layer_kernel, out_shape=(jax.ShapeDtypeStruct((1024, 128),...  45.8 us
    pallas_call x1, Pallas kernels, spread(): pl.pallas_call(spread_kernel, out_shape=(jax.ShapeDtypeStruct((32, 4, 8,...  35.9 us
    pallas_call x1, Pallas kernels, settle(): pl.pallas_call(settle_kernel, out_shape=(jax.ShapeDtypeStruct((2, 512, 12...  32.1 us
    unnamed x13, local copies, waits for them, and re-layouts  4.96 us

profile of v5, /device:TPU:6, one launch (start us, length us, event | category | flops | bytes accessed | tf_op | source)
XLA Modules:
  0.0 121.8 jit_solution(1025585376471965219)
XLA Ops:
  0.6 0.0 copy-start
  0.6 0.9 copy-done
  1.6 0.0 copy-start.1
  1.6 0.9 copy-done.1
  2.5 0.0 copy-start.2
  2.5 0.9 copy-done.2
  3.4 0.0 copy-start.3
  3.4 0.7 copy-done.3
  4.1 0.0 copy-start.5
  4.1 0.7 copy-done.5
  4.8 0.0 copy-start.4
  4.8 35.9 %spread.1 = (s16[32,4,8,16,128]{4,3,2,1,0:T(8,128)(2,1)S(1)}, f32[8,1024]{1,0:T(8,128)S(1)}, f32[1024,128]{1,0:T(8,128)S(1)}, bf16[8,2,128,512]{3,2,1,0:T(8,128)...) custom-call(s32[4,256]{1,0:T(4,128)S(1)} %bitcast.18, s32[256]{0:T(256)S(1)} %bitcast.20, ...), custom_call_target="tpu_custom_call" | custom-call | tf_op jit(solution)/shard_map/spread/pallas_call | solution.py:212
  40.7 0.0 copy-done.4
  40.7 45.8 %layer.1 = (f32[1024,128]{1,0:T(8,128)S(1)}, bf16[4096,256]{1,0:T(8,128)(2,1)S(1)}, f32[4,40,512]{2,1,0:T(8,128)S(1)}) custom-call(s16[32,4,8,16,128]{4,3,2,1,0:T(8,128)(2,1)S(1)} %get-tuple-element.15.dense, bf16[8,256,512]{2,1,0:T(8,128)(2,1)S(1)} %bitcast.16, f32[8,1024]{1,0:T(8,128)S(1)} %get-tuple-element.17.row, ...), custom_call_target="tpu_custom_call" | custom-call | tf_op jit(solution)/shard_map/layer/pallas_call | solution.py:423
  86.5 32.1 %settle.1 = (f32[2,512,128]{2,1,0:T(8,128)S(1)}, f32[4,40,512]{2,1,0:T(8,128)S(1)}) custom-call(s16[32,4,8,16,128]{4,3,2,1,0:T(8,128)(2,1)S(1)} %get-tuple-element.15.dense, bf16[4,1024,256]{2,1,0:T(8,128)(2,1)S(1)} %bitcast.15, f32[4,40,512]{2,1,0:T(8,128)S(1)} %get-tuple-element.23.gwx), custom_call_target="tpu_custom_call" | custom-call | tf_op jit(solution)/shard_map/settle/pallas_call | solution.py:606
  118.6 0.2 copy.11
  118.8 0.9 bitcast_multiply_fusion
  119.7 0.6 slice.7
  120.2 0.7 slice.6
  121.0 0.8 copy.13
Async XLA Ops:
  0.6 1.0 copy-start
  1.6 0.9 copy-start.1
  2.5 0.9 copy-start.2
  3.4 0.7 copy-start.3
  4.1 0.7 copy-start.5
  4.8 35.9 %copy-start.4 = (f32[512]{0:T(512)S(1)}, f32[512]{0:T(512)}, u32[]{:S(2)}) copy-start(f32[512]{0:T(512)} %param.9) | copy-start | bytes 6148

commit v6 on v5

--- a/solution.py
+++ b/solution.py
@@ -10,10 +10,10 @@
 MESH = pl.DeviceIdType.MESH
 BF16 = jnp.bfloat16
 F32 = jnp.float32
-VMEM = pl.BlockSpec(memory_space=pltpu.VMEM)
-SMEM = pl.BlockSpec(memory_space=pltpu.SMEM)
+HBM = pl.BlockSpec(memory_space=pltpu.HBM)
 DMA = pltpu.SemaphoreType.DMA
 MIB = 2**20
+VMEM_MIB = 60
 
 
 class Place:
@@ -38,13 +38,6 @@
 
     def dz(self, n):
         return lax.rem(self.z + n, 4)
-
-
-def greet(peers):
-    barrier = pltpu.get_barrier_semaphore()
-    for peer in peers:
-        pl.semaphore_signal(barrier, inc=1, device_id=peer, device_id_type=MESH)
-    pl.semaphore_wait(barrier, len(peers))
 
 
 class Copies:
@@ -69,50 +62,82 @@
 Y_ORDER = (2, 1, 3, 0)
 
 
-def spread_kernel(rows_ref, counts_ref, masks, feat, w, cot, dense, row, col, g, wc, cotr,
-                  words, m16, rm, slots_s, slots_v, landed_v, landed_s, xt, send, recv, load, local):
-    me = Place()
+def spread(me, rows_hbm, counts_hbm, masks, feat_hbm, w, bias_hbm, cot, dense, row, col, g, wc, cotr, bias,
+           rows_ref, counts_ref, feat, words, m16, rm, slots_s, slots_v, landed_v, landed_s, xt, send, recv, load, local):
     own, other = me.c, 1 - me.c
+    small = [
+        pltpu.make_async_copy(rows_hbm, rows_ref, local.at[6]),
+        pltpu.make_async_copy(counts_hbm, counts_ref, local.at[7]),
+    ]
+    for copy in small:
+        copy.start()
     loads = []
     for q in range(8):
         half = own if q < 4 else other
         loads.append(pltpu.make_async_copy(masks.at[:, me.dy(Y_ORDER[q % 4]), half], words.at[q], load.at[q]))
         loads[q].start()
+    feat_load = pltpu.make_async_copy(feat_hbm, feat, local.at[8])
+    feat_load.start()
 
     sibling = me.at(c=1 - me.c)
     x_peer = me.at(x=1 - me.x)
     z_peers = [me.at(z=me.dz(n)) for n in (1, 2, 3)]
     y_peers = [me.at(y=me.dy(n)) for n in (1, 2, 3)]
     rep_peers = [sibling, me.at(xl=1 - me.xl), me.at(xl=1 - me.xl, c=1 - me.c)]
-    greet(z_peers + y_peers + rep_peers + [x_peer])
+    everyone = z_peers + y_peers + rep_peers + [x_peer]
+    barrier = pltpu.get_barrier_semaphore()
+    for peer in everyone:
+        pl.semaphore_signal(barrier, inc=1, device_id=peer, device_id_type=MESH)
+
+    def narrow(q):
+        loads[q].wait()
+
+        def tiles(xz, _):
+            for slot in range(16):
+                tile = words[q, xz, slot].astype(jnp.int16)
+                if q < 3:
+                    m16[q, xz, slot] = tile
+                else:
+                    rm[me.y, xz, slot] = tile
+            return 0
+
+        lax.fori_loop(0, 8, tiles, 0)
+
+    narrow(0)
+    pl.semaphore_wait(barrier, len(everyone))
     copies = Copies(send, recv)
 
     def cot_rows(rep):
         return cot.at[pl.ds(pl.multiple_of(rep * 256, 256), 256), :]
 
+    mask_copies = []
+    for q in range(3):
+        if q:
+            narrow(q)
+        mask_copies.append(copies.start(m16.at[q], rm.at[me.y], y_peers[Y_ORDER[q] - 1]))
     early = []
     for peer in rep_peers:
         early.append(copies.start(cot_rows(peer[1]), cotr.at[me.rep], peer))
         early.append(copies.start(w, wc.at[me.rep], peer))
+    narrow(3)
+    for copy in small:
+        copy.wait()
     tile_row = lax.broadcasted_iota(jnp.int32, (8, 128), 0)
 
     def scan(q, degrees):
         n = Y_ORDER[q % 4]
         half = own if q < 4 else other
-        loads[q].wait()
+        if q >= 4:
+            loads[q].wait()
 
         def tiles(xz, degrees):
             first = ((xz * 4 + me.dy(n)) * 2 + half) * 4
             for tc in range(4):
-                count = counts_ref[first + tc]
+                count = counts_ref[0, first + tc]
                 for s in range(4):
                     slot = tc * 4 + s
                     t = jnp.where(s < count, rows_ref[s, first + tc], 8)
                     tile = words[q, xz, slot]
-                    if q < 3:
-                        m16[q, xz, slot] = tile.astype(jnp.int16)
-                    elif q == 3:
-                        rm[me.y, xz, slot] = tile.astype(jnp.int16)
                     if q < 4:
                         slots_s[q, 0, xz * 16 + slot] = t
                     joined = jnp.bitwise_or(tile[:8], jnp.left_shift(tile[8:], 8))
@@ -123,17 +148,14 @@
         return lax.fori_loop(0, 8, tiles, degrees)
 
     degrees = jnp.zeros((8, 128), jnp.int32)
-    mask_copies = []
-    for q in range(3):
-        degrees = scan(q, degrees)
-        mask_copies.append(copies.start(m16.at[q], rm.at[me.y], y_peers[Y_ORDER[q] - 1]))
-    for q in range(3, 8):
+    for q in range(8):
         degrees = scan(q, degrees)
 
     inv = lax.rsqrt(1.0 + degrees.astype(F32))
     place = lax.broadcasted_iota(jnp.int32, (128, 128), 1)
     source = 8 * jnp.bitwise_and(place, 15) + jnp.right_shift(place, 4)
     perm = jnp.where(lax.broadcasted_iota(jnp.int32, (128, 128), 0) == source, 1.0, 0.0).astype(BF16)
+    feat_load.wait()
     for t in range(8):
         lanes = inv[t:t + 1, :]
         row[:, t * 128:(t + 1) * 128] = jnp.broadcast_to(lanes, (8, 128))
@@ -153,6 +175,7 @@
         pltpu.make_async_copy(xt.at[own], at(own, me.xz), local.at[0]),
         pltpu.make_async_copy(w, wc.at[me.rep], local.at[1]),
         pltpu.make_async_copy(cot_rows(me.rep), cotr.at[me.rep], local.at[5]),
+        pltpu.make_async_copy(bias_hbm, bias, local.at[9]),
     ]
     for copy in stays:
         copy.start()
@@ -201,45 +224,17 @@
     for q in range(3):
         mask_copies[q].wait_recv()
         put_tiles(4 - Y_ORDER[q], landed_s, me.dy(4 - Y_ORDER[q]))
-    for copy in [across] + early + second + last:
+    for copy in [across] + second + last:
         copy.wait_recv()
-    copies.wait_sends()
-    for copy in stays:
-        copy.wait()
-
-
-def spread(rows, counts, masks, features, w, cot):
-    return pl.pallas_call(
-        spread_kernel,
-        out_shape=(
-            jax.ShapeDtypeStruct((32, 4, 8, 16, 128), jnp.int16),
-            jax.ShapeDtypeStruct((8, 1024), F32),
-            jax.ShapeDtypeStruct((1024, 128), F32),
-            jax.ShapeDtypeStruct((8, 2, 128, 512), BF16),
-            jax.ShapeDtypeStruct((4, 128, 512), BF16),
-            jax.ShapeDtypeStruct((4, 256, 128), BF16),
-        ),
-        in_specs=[SMEM, SMEM, pl.BlockSpec(memory_space=pltpu.HBM), VMEM, VMEM, VMEM],
-        out_specs=(VMEM,) * 6,
-        scratch_shapes=[
-            pltpu.VMEM((8, 8, 16, 16, 128), jnp.int32),
-            pltpu.VMEM((3, 8, 16, 16, 128), jnp.int16),
-            pltpu.VMEM((4, 8, 16, 16, 128), jnp.int16),
-            pltpu.SMEM((4, 1, 128), jnp.int32),
-            pltpu.VMEM((4, 1, 128), jnp.int32),
-            pltpu.VMEM((4, 1, 128), jnp.int32),
-            pltpu.SMEM((4, 1, 128), jnp.int32),
-            pltpu.VMEM((2, 128, 512), BF16),
-            DMA((27,)),
-            DMA((27,)),
-            DMA((8,)),
-            DMA((6,)),
-        ],
-        compiler_params=pltpu.CompilerParams(
-            collective_id=0, has_side_effects=True, vmem_limit_bytes=44 * MIB
-        ),
-        name="spread",
-    )(rows, counts, masks, features, w, cot)
+    stays[0].wait()
+
+    def parameters():
+        for copy in early:
+            copy.wait_recv()
+        for copy in stays[1:]:
+            copy.wait()
+
+    return parameters, copies.wait_sends
 
 
 def table(values, step):
@@ -260,15 +255,13 @@
                 out_ref[first:first + 16, t * 128:(t + 1) * 128] = bits
 
 
-def layer_kernel(dense, g, row, col, wc, bias, cotr, act, ball, gwx,
-                 a0, a1, acc, part, rc, snd, ry, agg_s, agg, agg_t, slope, act_s, back_s,
-                 core_s, core_r, sum_s, sum_r, send, recv):
-    me = Place()
+def layer(me, parameters, dense, g, row, col, wc, bias, cotr, act, ball, gwx, a0, a1,
+          acc, part, rc, snd, ry, agg_s, agg, agg_t, slope, act_s, back_s,
+          core_s, core_r, sum_s, sum_r, send, recv, local):
     sibling = me.at(c=1 - me.c)
     xl_peer = me.at(xl=1 - me.xl)
     xl_other = me.at(xl=1 - me.xl, c=1 - me.c)
     y_peers = [me.at(y=me.dy(n)) for n in (1, 2, 3)]
-    greet([sibling, xl_peer, xl_other] + y_peers)
     copies = Copies(send, recv)
     own, other = me.c, 1 - me.c
 
@@ -304,7 +297,7 @@
         k, pair = n // 4, lax.rem(n, 4)
         for h in range(2):
             unpack(dense, *chunk(jnp.minimum(n * 2 + h + 1, 31)), bufs[1 - h])
-            prod = jnp.dot(g[pair * 2 + h], bufs[h][...], preferred_element_type=F32)
+            prod = jnp.dot(g[pair * 2 + h].reshape(256, 512), bufs[h][...], preferred_element_type=F32)
             if h == 0:
                 acc[...] = jnp.where(pair == 0, 0.0, acc[...]) + prod
             else:
@@ -342,6 +335,7 @@
         finish_sum(peers[n][1], agg_s.at[n])
         swaps.append(copies.start(agg_s.at[n], agg.at[me.rep], peers[n]))
     finish_sum(me.rep, agg.at[me.rep])
+    parameters()
     for copy in reversed(swaps):
         copy.wait_recv()
 
@@ -387,7 +381,8 @@
         copies.start(act_s.at[peer[1]], act.at[rows_of(me.rep), :], peer)
         for peer in (xl_peer, xl_other, sibling)
     ]
-    act[rows_of(me.rep), :] = act_s[me.rep]
+    act_kept = pltpu.make_async_copy(act_s.at[me.rep], act.at[rows_of(me.rep), :], local)
+    act_kept.start()
     slope_far.wait_recv()
     slope_relay = copies.start(slope.at[theirs], slope.at[theirs], sibling)
 
@@ -409,66 +404,33 @@
             copy.wait_recv()
             here = block(me.dy(4 - n), rep)
             relays.append(copies.start(here, here, sibling))
-    for copy in [mine[3], passed[3]] + relays + acts:
+    for copy in [mine[3], passed[3]] + relays:
         copy.wait_recv()
-    copies.wait_sends()
-    for k in range(3):
-        for m in range(4):
-            to_owner(k, m).wait_send()
-    for k in range(4):
-        to_sibling(k).wait_send()
-
-
-def layer(dense, g, row, col, wc, bias, cotr):
-    return pl.pallas_call(
-        layer_kernel,
-        out_shape=(
-            jax.ShapeDtypeStruct((1024, 128), F32),
-            jax.ShapeDtypeStruct((4096, 256), BF16),
-            jax.ShapeDtypeStruct((4, 40, 512), F32),
-        ),
-        in_specs=[VMEM] * 7,
-        out_specs=(VMEM, VMEM, VMEM),
-        scratch_shapes=[
-            pltpu.VMEM((512, 1024), BF16),
-            pltpu.VMEM((512, 1024), BF16),
-            pltpu.VMEM((256, 1024), F32),
-            pltpu.VMEM((4, 2, 128, 1024), BF16),
-            pltpu.VMEM((4, 128, 1024), BF16),
-            pltpu.VMEM((3, 4, 128, 256), BF16),
-            pltpu.VMEM((3, 4, 128, 256), BF16),
-            pltpu.VMEM((3, 256, 128), BF16),
-            pltpu.VMEM((4, 256, 128), BF16),
-            pltpu.VMEM((128, 1024), BF16),
-            pltpu.VMEM((4, 256, 512), BF16),
-            pltpu.VMEM((4, 256, 128), F32),
-            pltpu.VMEM((256, 256), BF16),
-            DMA((4,)),
-            DMA((4,)),
-            DMA((12,)),
-            DMA((12,)),
-            DMA((24,)),
-            DMA((24,)),
-        ],
-        compiler_params=pltpu.CompilerParams(
-            collective_id=1, has_side_effects=True, vmem_limit_bytes=36 * MIB
-        ),
-        name="layer",
-    )(dense, g, row, col, wc, bias, cotr)
+
+    def finish():
+        for copy in acts:
+            copy.wait_recv()
+        act_kept.wait()
+        copies.wait_sends()
+        for k in range(3):
+            for m in range(4):
+                to_owner(k, m).wait_send()
+        for k in range(4):
+            to_sibling(k).wait_send()
+
+    return finish
 
 
 BLOCKS = ((1, 2), (1, 1), (1, 3), (1, 0), (0, 2), (0, 1), (0, 3), (0, 0))
 ORDER = {key: n for n, key in enumerate(BLOCKS)}
 
 
-def settle_kernel(dense, ball, gwx, out, gw, a0, a1, acc, part, az, a_sum, ax, bx, b_sum, bz, final,
-                  wy, wz, wx_send, wx, send, recv, local):
-    me = Place()
+def settle(me, dense, col, ball, gwx, out, gw, a0, a1,
+           acc, part, az, a_sum, ax, bx, b_sum, bz, hold, final, wy, wz, wx_send, wx, gw_own, send, recv, local):
     sibling = me.at(c=1 - me.c)
     x_peer = me.at(x=1 - me.x)
     z_peers = [me.at(z=me.dz(n)) for n in (1, 2, 3)]
     y_peers = [me.at(y=me.dy(n)) for n in (1, 2, 3)]
-    greet(z_peers + y_peers + [x_peer, sibling])
 
     def remote(n, src, dst, peer):
         return pltpu.make_async_remote_copy(
@@ -486,7 +448,8 @@
     w_y = [remote(13 + n, gwx.at[me.dy(n)], wy.at[me.y], y_peers[n - 1]) for n in (1, 2, 3)]
     w_z = [remote(16 + n, wz.at[me.z], wz.at[me.z], z_peers[n - 1]) for n in (1, 2, 3)]
     w_x = remote(20, wx_send, wx, x_peer)
-    w_back = [remote(20 + n, gw.at[me.y], gw.at[me.y], y_peers[n - 1]) for n in (1, 2, 3)]
+    w_back = [remote(20 + n, gw_own, gw.at[me.y], y_peers[n - 1]) for n in (1, 2, 3)]
+    w_kept = pltpu.make_async_copy(gw_own, gw.at[me.y], local.at[0])
 
     def pass_b(n):
         x_first[n].wait_recv()
@@ -516,7 +479,8 @@
 
     def weights_back():
         w_x.wait_recv()
-        gw[me.y] = wx_send[...] + wx[...]
+        gw_own[...] = wx_send[...] + wx[...]
+        w_kept.start()
         for copy in w_back:
             copy.start()
 
@@ -549,7 +513,7 @@
         block, pair = step // 2, lax.rem(step, 2)
         for h in range(2):
             unpack(dense, *chunk(jnp.minimum(step * 2 + h + 1, 31)), bufs[1 - h])
-            prod = jnp.dot(bufs[h][...], ball[pair * 2 + h], preferred_element_type=F32)
+            prod = jnp.dot(bufs[h][...], ball[pl.ds(pl.multiple_of((pair * 2 + h) * 1024, 1024), 1024), :], preferred_element_type=F32)
             if h == 0:
                 acc[...] = jnp.where(pair == 0, 0.0, acc[...]) + prod
             else:
@@ -571,82 +535,204 @@
 
     lax.fori_loop(0, 16, two_chunks, 0)
 
+    def place(tile, total):
+        here = slice(tile * 128, tile * 128 + 256)
+        for q in range(2):
+            hold[q * 512 + tile * 128:q * 512 + tile * 128 + 256, :] = total[:, q * 128:(q + 1) * 128]
+        for t in range(tile, tile + 2):
+            for w in range(16):
+                first = t * 128 + w * 8
+                scale = col[pl.ds(pl.multiple_of(me.c * 512 + first, 8), 8), :]
+                for q in range(2):
+                    final[q, first:first + 8, :] = hold[pl.ds(q * 512 + t * 128 + w, 8, stride=16), :] * scale
+        at = tile // 2
+        swap = remote(24 + at, final.at[1 - me.c, here], out.at[me.c, here], sibling)
+        keep = pltpu.make_async_copy(final.at[me.c, here], out.at[me.c, here], local.at[1 + at])
+        swap.start()
+        keep.start()
+        return swap, keep
+
     total = part[ORDER[0, 0], 1].astype(F32)
     x_first[0].wait_recv()
     total = total + bx[0].astype(F32)
     for n in (1, 2, 3):
         z_second[n].wait_recv()
         total = total + bz[n - 1].astype(F32)
-    final[0, 256:512, :] = total[:, 0:128]
-    final[1, 256:512, :] = total[:, 128:256]
+    swaps = [place(2, total)]
     total = part[ORDER[0, 0], 0].astype(F32)
     for n in (1, 2, 3):
         z_first[0, n].wait_recv()
         total = total + az[0, n - 1].astype(F32)
     x_second.wait_recv()
     total = total + ax[...].astype(F32)
-    final[0, 0:256, :] = total[:, 0:128]
-    final[1, 0:256, :] = total[:, 128:256]
-    swap = remote(24, final.at[1 - me.c], out.at[me.c], sibling)
-    swap.start()
-    keep = pltpu.make_async_copy(final.at[me.c], out.at[me.c], local)
-    keep.start()
+    swaps.append(place(0, total))
     for copy in w_back:
         copy.wait_recv()
-    swap.wait_recv()
-    keep.wait()
+    for swap, keep in swaps:
+        swap.wait_recv()
+        keep.wait()
+    w_kept.wait()
     for copy in list(x_first.values()) + list(z_first.values()) + list(z_second.values()):
         copy.wait_send()
-    for copy in [x_second, w_x, swap] + w_y + w_z + w_back:
+    for copy in [x_second, w_x] + [swap for swap, _ in swaps] + w_y + w_z + w_back:
         copy.wait_send()
 
 
-def settle(dense, ball, gwx):
-    half = (256, 256)
-    return pl.pallas_call(
-        settle_kernel,
+HALF = (256, 256)
+HELD = (
+    pltpu.VMEM((32, 4, 8, 16, 128), jnp.int16),
+    pltpu.VMEM((8, 1024), F32),
+    pltpu.VMEM((1024, 128), F32),
+    pltpu.VMEM((8, 2, 128, 512), BF16),
+    pltpu.VMEM((4, 128, 512), BF16),
+    pltpu.VMEM((4, 256, 128), BF16),
+    pltpu.VMEM((1, 512), F32),
+    pltpu.VMEM((4096, 256), BF16),
+    pltpu.VMEM((4, 40, 512), F32),
+    pltpu.VMEM((512, 1024), BF16),
+    pltpu.VMEM((512, 1024), BF16),
+)
+SPREAD = (
+    pltpu.SMEM((4, 256), jnp.int32),
+    pltpu.SMEM((1, 256), jnp.int32),
+    pltpu.VMEM((1024, 128), BF16),
+    pltpu.VMEM((8, 8, 16, 16, 128), jnp.int32),
+    pltpu.VMEM((3, 8, 16, 16, 128), jnp.int16),
+    pltpu.VMEM((4, 8, 16, 16, 128), jnp.int16),
+    pltpu.SMEM((4, 1, 128), jnp.int32),
+    pltpu.VMEM((4, 1, 128), jnp.int32),
+    pltpu.VMEM((4, 1, 128), jnp.int32),
+    pltpu.SMEM((4, 1, 128), jnp.int32),
+    pltpu.VMEM((2, 128, 512), BF16),
+    DMA((27,)),
+    DMA((27,)),
+    DMA((8,)),
+    DMA((10,)),
+)
+LAYER = (
+    pltpu.VMEM((256, 1024), F32),
+    pltpu.VMEM((4, 2, 128, 1024), BF16),
+    pltpu.VMEM((4, 128, 1024), BF16),
+    pltpu.VMEM((3, 4, 128, 256), BF16),
+    pltpu.VMEM((3, 4, 128, 256), BF16),
+    pltpu.VMEM((3, 256, 128), BF16),
+    pltpu.VMEM((4, 256, 128), BF16),
+    pltpu.VMEM((128, 1024), BF16),
+    pltpu.VMEM((4, 256, 512), BF16),
+    pltpu.VMEM((4, 256, 128), F32),
+    pltpu.VMEM((256, 256), BF16),
+    DMA((4,)),
+    DMA((4,)),
+    DMA((12,)),
+    DMA((12,)),
+    DMA((24,)),
+    DMA((24,)),
+    DMA,
+)
+SETTLE = (
+    pltpu.VMEM((512, 256), F32),
+    pltpu.VMEM((8, 2) + HALF, BF16),
+    pltpu.VMEM((2, 3) + HALF, BF16),
+    pltpu.VMEM(HALF, BF16),
+    pltpu.VMEM(HALF, BF16),
+    pltpu.VMEM((4,) + HALF, BF16),
+    pltpu.VMEM((3,) + HALF, BF16),
+    pltpu.VMEM((3,) + HALF, BF16),
+    pltpu.VMEM((1024, 128), F32),
+    pltpu.VMEM((2, 512, 128), F32),
+    pltpu.VMEM((4, 40, 512), F32),
+    pltpu.VMEM((4, 40, 512), F32),
+    pltpu.VMEM((40, 512), F32),
+    pltpu.VMEM((40, 512), F32),
+    pltpu.VMEM((40, 512), F32),
+    DMA((26,)),
+    DMA((26,)),
+    DMA((3,)),
+)
+
+
+def all_kernel(*refs):
+    groups, first = [], 0
+    for size in (7, 3, len(HELD), len(SPREAD), len(LAYER), len(SETTLE)):
+        groups.append(refs[first:first + size])
+        first += size
+    ins, (act, out, gw), held, spread_refs, layer_refs, settle_refs = groups
+    dense, row, col, g, wc, cotr, bias, ball, gwx, a0, a1 = held
+    me = Place()
+    parameters, finish_spread = spread(me, *ins, dense, row, col, g, wc, cotr, bias, *spread_refs)
+    finish_layer = layer(
+        me, parameters, dense, g, row, col, wc, bias, cotr, act, ball, gwx, a0, a1, *layer_refs
+    )
+    settle(me, dense, col, ball, gwx, out, gw, a0, a1, *settle_refs)
+    finish_layer()
+    finish_spread()
+
+
+def results_kernel(act, out, gw, act_out, feat_out, gw_out, gb_out, act_v, feat_v, gw_v, load, store):
+    loads = [pltpu.make_async_copy(gw, gw_v, load.at[0])]
+    for n in range(2):
+        here = slice(n * 512, n * 512 + 512)
+        loads.append(pltpu.make_async_copy(act.at[here], act_v.at[here], load.at[1 + n]))
+        loads.append(pltpu.make_async_copy(out.at[here], feat_v.at[here], load.at[3 + n]))
+    for copy in loads:
+        copy.start()
+    loads[0].wait()
+    stores = [
+        pltpu.make_async_copy(gw_v.at[:, 0:32], gw_out, store.at[0]),
+        pltpu.make_async_copy(gw_v.at[0, 32:33], gb_out, store.at[1]),
+    ]
+    for copy in stores:
+        copy.start()
+    for n in range(2):
+        here = slice(n * 512, n * 512 + 512)
+        loads[1 + 2 * n].wait()
+        stores.append(pltpu.make_async_copy(act_v.at[here], act_out.at[here], store.at[2 + n]))
+        stores[-1].start()
+        loads[2 + 2 * n].wait()
+        stores.append(pltpu.make_async_copy(feat_v.at[here], feat_out.at[here], store.at[4 + n]))
+        stores[-1].start()
+    for copy in stores:
+        copy.wait()
+
+
+def body(features, weight, bias_vector, cotangent, tile_masks, tile_rows, tile_counts):
+    masks = tile_masks.reshape(8, 4, 2, 16, 16, 128)
+    act, out, gw = pl.pallas_call(
+        all_kernel,
         out_shape=(
+            jax.ShapeDtypeStruct((1024, 128), F32),
             jax.ShapeDtypeStruct((2, 512, 128), F32),
             jax.ShapeDtypeStruct((4, 40, 512), F32),
         ),
-        in_specs=[VMEM] * 3,
-        out_specs=(VMEM, VMEM),
+        in_specs=[HBM] * 7,
+        out_specs=(HBM,) * 3,
+        scratch_shapes=HELD + SPREAD + LAYER + SETTLE,
+        compiler_params=pltpu.CompilerParams(
+            collective_id=0, has_side_effects=True, vmem_limit_bytes=VMEM_MIB * MIB
+        ),
+        name="layer",
+    )(tile_rows[0].T, tile_counts, masks, features, weight, bias_vector.reshape(1, 512), cotangent)
+    act, out, gw, gb = pl.pallas_call(
+        results_kernel,
+        out_shape=(
+            jax.ShapeDtypeStruct((1024, 128), F32),
+            jax.ShapeDtypeStruct((1024, 128), F32),
+            jax.ShapeDtypeStruct((4, 32, 512), F32),
+            jax.ShapeDtypeStruct((1, 512), F32),
+        ),
+        in_specs=[HBM] * 3,
+        out_specs=(HBM,) * 4,
         scratch_shapes=[
-            pltpu.VMEM((512, 1024), BF16),
-            pltpu.VMEM((512, 1024), BF16),
-            pltpu.VMEM((512, 256), F32),
-            pltpu.VMEM((8, 2) + half, BF16),
-            pltpu.VMEM((2, 3) + half, BF16),
-            pltpu.VMEM(half, BF16),
-            pltpu.VMEM(half, BF16),
-            pltpu.VMEM((4,) + half, BF16),
-            pltpu.VMEM((3,) + half, BF16),
-            pltpu.VMEM((3,) + half, BF16),
-            pltpu.VMEM((2, 512, 128), F32),
+            pltpu.VMEM((1024, 128), F32),
+            pltpu.VMEM((1024, 128), F32),
             pltpu.VMEM((4, 40, 512), F32),
-            pltpu.VMEM((4, 40, 512), F32),
-            pltpu.VMEM((40, 512), F32),
-            pltpu.VMEM((40, 512), F32),
-            DMA((25,)),
-            DMA((25,)),
-            DMA,
+            DMA((5,)),
+            DMA((6,)),
         ],
-        compiler_params=pltpu.CompilerParams(
-            collective_id=2, has_side_effects=True, vmem_limit_bytes=36 * MIB
-        ),
-        name="settle",
-    )(dense, ball, gwx)
-
-
-def body(features, weight, bias_vector, cotangent, tile_masks, tile_rows, tile_counts):
-    masks = tile_masks.reshape(8, 4, 2, 16, 16, 128)
-    dense, row, col, g, wc, cotr = spread(
-        tile_rows[0].T, tile_counts.reshape(256), masks, features, weight, cotangent
-    )
-    act, ball, gwx = layer(dense, g.reshape(8, 256, 512), row, col, wc, bias_vector.reshape(1, 512), cotr)
-    out, gw = settle(dense, ball.reshape(4, 1024, 256), gwx)
-    out = out.reshape(8, 8, 16, 128).transpose(0, 2, 1, 3).reshape(1024, 128) * col
-    return act, out, gw[:, :32].reshape(128, 512), gw[0, 32]
+        compiler_params=pltpu.CompilerParams(vmem_limit_bytes=VMEM_MIB * MIB),
+        name="results",
+    )(act, out.reshape(1024, 128), gw)
+    return act, out, gw.reshape(128, 512), gb.reshape(512)
 
 
 def solution(mesh):

time: 123 us -> 111 us (0.902)
  local copies, waits for them, and re-layouts: 6.42 us -> 0 us
  Pallas kernels: 114 us -> 110 us
    unnamed x13 -> x0, local copies, waits for them, and re-layouts: 4.96 us -> none
    pallas_call x3 -> x2, Pallas kernels: 114 us -> 110 us  [the longest x1 108 us: body(): pl.pallas_call(all_kernel, out_shape=(jax.ShapeDtypeStruct((1024, 128), F...]
    slice x2 -> x0, local copies, waits for them, and re-layouts: 1.3 us -> none  [body(): return (act, out, gw[:, :32].reshape(128, 512), gw[0, 32])]
where the time goes in v6:
time: 111 us
  Pallas kernels  110 us (99%)
    pallas_call x1, Pallas kernels, body(): pl.pallas_call(all_kernel, out_shape=(jax.ShapeDtypeStruct((1024, 128), F...  108 us

profile of v6, /device:TPU:6, one launch (start us, length us, event | category | flops | bytes accessed | tf_op | source)
XLA Modules:
  0.0 110.6 jit_solution(11917041353720544084)
XLA Ops:
  0.6 107.9 %layer.1 = (f32[1024,128]{1,0:T(8,128)}, f32[2,512,128]{2,1,0:T(8,128)}, f32[4,40,512]{2,1,0:T(8,128)}) custom-call(s32[4,256]{1,0:T(4,128)} %bitcast.10, s32[1,256]{1,0:T(1,128)} %refs_1_.1, s32[8,4,2,16,16,128]{5,4,3,2,1,0:T(8,128)} %bitcast.8, bf16[1024,128]{1,0:T(8,128)(2,1)} %refs_3_.1, bf16[128,512]{1,0:T(8,128)(2,1)} %refs_4_.1, f32[1,512]{1,0:T(1,128)} %bitcast.11, ...), custom_call_target="tpu_custom_call" | custom-call | tf_op jit(solution)/shard_map/layer/pallas_call | solution.py:700
  108.5 2.1 %results.1 = (f32[1024,128]{1,0:T(8,128)}, f32[1024,128]{1,0:T(8,128)}, f32[4,32,512]{2,1,0:T(8,128)}, f32[1,512]{1,0:T(1,128)}) custom-call(f32[1024,128]{1,0:T(8,128)} %get-tuple-element.11.act, f32[1024,128]{1,0:T(8,128)} %bitcast.9, f32[4,40,512]{2,1,0:T(8,128)} %get-tuple-element.13.gw), custom_call_target="tpu_custom_call" | custom-call | tf_op jit(solution)/shard_map/results/pallas_call | solution.py:715

commit v7 on v6

--- a/solution.py
+++ b/solution.py
@@ -38,6 +38,9 @@
 
     def dz(self, n):
         return lax.rem(self.z + n, 4)
+
+    def column(self, n):
+        return lax.rem(self.x + n // 4, 2) * 4 + self.dz(4 - lax.rem(n, 4))
 
 
 class Copies:
@@ -60,6 +63,7 @@
 
 
 Y_ORDER = (2, 1, 3, 0)
+ROWS = (0, 2, 1, 3)
 
 
 def spread(me, rows_hbm, counts_hbm, masks, feat_hbm, w, bias_hbm, cot, dense, row, col, g, wc, cotr, bias,
@@ -206,6 +210,7 @@
 
         lax.fori_loop(0, 8, column, 0)
 
+    put_tiles(0, slots_s, 3)
     last = []
     for n in (1, 2, 3):
         first[n - 1].wait_recv()
@@ -214,19 +219,31 @@
     other_x.wait_recv()
     far = (1 - me.x) * 4 + me.z
     last += [copies.start(at(other, far), at(other, far), p) for p in z_peers]
-    put_tiles(0, slots_s, 3)
-    kept.wait()
-    for copy in slot_copies:
-        copy.wait_recv()
-    to_smem = pltpu.make_async_copy(landed_v, landed_s, local.at[4])
-    to_smem.start()
-    to_smem.wait()
-    for q in range(3):
+
+    def arrive(column):
+        n = column % 4
+        if column == 0:
+            stays[0].wait()
+        elif column < 4:
+            second[n - 1].wait_recv()
+        elif column == 4:
+            across.wait_recv()
+        else:
+            last[n - 1].wait_recv()
+            last[n + 2].wait_recv()
+
+    def slots():
+        kept.wait()
+        for copy in slot_copies:
+            copy.wait_recv()
+        to_smem = pltpu.make_async_copy(landed_v, landed_s, local.at[4])
+        to_smem.start()
+        to_smem.wait()
+
+    def place_tiles(n):
+        q = Y_ORDER.index(4 - n)
         mask_copies[q].wait_recv()
-        put_tiles(4 - Y_ORDER[q], landed_s, me.dy(4 - Y_ORDER[q]))
-    for copy in [across] + second + last:
-        copy.wait_recv()
-    stays[0].wait()
+        put_tiles(n, landed_s, me.dy(n))
 
     def parameters():
         for copy in early:
@@ -234,7 +251,7 @@
         for copy in stays[1:]:
             copy.wait()
 
-    return parameters, copies.wait_sends
+    return arrive, slots, place_tiles, parameters, copies.wait_sends
 
 
 def table(values, step):
@@ -255,7 +272,7 @@
                 out_ref[first:first + 16, t * 128:(t + 1) * 128] = bits
 
 
-def layer(me, parameters, dense, g, row, col, wc, bias, cotr, act, ball, gwx, a0, a1,
+def layer(me, arrive, slots, place_tiles, parameters, dense, g, row, col, wc, bias, cotr, act, ball, gwx, a0, a1,
           acc, part, rc, snd, ry, agg_s, agg, agg_t, slope, act_s, back_s,
           core_s, core_r, sum_s, sum_r, send, recv, local):
     sibling = me.at(c=1 - me.c)
@@ -276,28 +293,42 @@
 
     def to_owner(k, m):
         return pltpu.make_async_remote_copy(
-            src_ref=snd.at[k, m], dst_ref=ry.at[k, m], send_sem=sum_s.at[k * 4 + m], recv_sem=sum_r.at[k * 4 + m],
-            device_id=me.at(y=me.dy(table((2, 1, 3), k))), device_id_type=MESH,
+            src_ref=snd.at[k - 1, m], dst_ref=ry.at[k - 1, m],
+            send_sem=sum_s.at[k * 4 + m - 4], recv_sem=sum_r.at[k * 4 + m - 4],
+            device_id=me.at(y=me.dy(table(ROWS, k))), device_id_type=MESH,
         )
 
     def pass_on(k):
         to_sibling(k).wait_recv()
         for m in range(4):
             rows = slice(m * 256, (m + 1) * 256)
-            snd[k, m] = (part[k, own, :, rows].astype(F32) + rc[k, :, rows].astype(F32)).astype(BF16)
+            snd[k - 1, m] = (part[k, own, :, rows].astype(F32) + rc[k, :, rows].astype(F32)).astype(BF16)
             to_owner(k, m).start()
 
     def chunk(c):
-        return me.dy(table((2, 1, 3, 0), c // 8)), lax.rem(c, 8)
+        return me.dy(table(ROWS, c // 8)), me.column(lax.rem(c, 8))
 
     bufs = (a0, a1)
     unpack(dense, *chunk(0), a0)
 
     def two_chunks(n, _):
         k, pair = n // 4, lax.rem(n, 4)
+        for step in range(4):
+            @pl.when(n == step)
+            def _():
+                arrive(step * 2)
+                arrive(step * 2 + 1)
+
+        for step in range(1, 4):
+            @pl.when(n == step * 4 - 1)
+            def _():
+                if step == 1:
+                    slots()
+                place_tiles(ROWS[step])
+
         for h in range(2):
             unpack(dense, *chunk(jnp.minimum(n * 2 + h + 1, 31)), bufs[1 - h])
-            prod = jnp.dot(g[pair * 2 + h].reshape(256, 512), bufs[h][...], preferred_element_type=F32)
+            prod = jnp.dot(g[me.column(pair * 2 + h)].reshape(256, 512), bufs[h][...], preferred_element_type=F32)
             if h == 0:
                 acc[...] = jnp.where(pair == 0, 0.0, acc[...]) + prod
             else:
@@ -309,20 +340,21 @@
             part[k, 1] = acc[128:256].astype(BF16)
             to_sibling(k).start()
 
-        @pl.when(jnp.logical_and(pair == 0, k >= 1))
+        @pl.when(jnp.logical_and(pair == 0, k >= 2))
         def _():
             pass_on(k - 1)
 
         return 0
 
     lax.fori_loop(0, 16, two_chunks, 0)
-    to_sibling(3).wait_recv()
+    pass_on(3)
+    to_sibling(0).wait_recv()
 
     def finish_sum(m, out):
-        for k in range(3):
+        for k in (1, 2, 3):
             to_owner(k, m).wait_recv()
         rows = rows_of(m)
-        total = part[3, own, :, rows].astype(F32) + rc[3, :, rows].astype(F32)
+        total = part[0, own, :, rows].astype(F32) + rc[0, :, rows].astype(F32)
         for k in range(3):
             total = total + ry[k, m].astype(F32)
         total = total * row[0:1, rows]
@@ -412,7 +444,7 @@
             copy.wait_recv()
         act_kept.wait()
         copies.wait_sends()
-        for k in range(3):
+        for k in (1, 2, 3):
             for m in range(4):
                 to_owner(k, m).wait_send()
         for k in range(4):
@@ -421,7 +453,7 @@
     return finish
 
 
-BLOCKS = ((1, 2), (1, 1), (1, 3), (1, 0), (0, 2), (0, 1), (0, 3), (0, 0))
+BLOCKS = ((1, 2), (0, 2), (1, 1), (1, 3), (0, 1), (0, 3), (1, 0), (0, 0))
 ORDER = {key: n for n, key in enumerate(BLOCKS)}
 
 
@@ -487,13 +519,13 @@
     actions = {n: [] for n in range(8)}
     for n in range(4):
         actions[ORDER[1, n]].append(x_first[n].start)
-    for n in (2, 1, 3):
-        actions[ORDER[0, n]].append(functools.partial(pass_b, n))
     for key, copy in z_first.items():
         actions[ORDER[key]].append(copy.start)
-    actions[3].append(weights_z)
-    actions[4].append(pass_a)
-    actions[5].append(weights_x)
+    for n, step in ((2, 2), (1, 4), (3, 5)):
+        actions[step].append(functools.partial(pass_b, n))
+    actions[1].append(weights_z)
+    actions[3].append(weights_x)
+    actions[6].append(pass_a)
     actions[6].append(weights_back)
 
     for copy in w_y:
@@ -659,9 +691,9 @@
     ins, (act, out, gw), held, spread_refs, layer_refs, settle_refs = groups
     dense, row, col, g, wc, cotr, bias, ball, gwx, a0, a1 = held
     me = Place()
-    parameters, finish_spread = spread(me, *ins, dense, row, col, g, wc, cotr, bias, *spread_refs)
+    *arrivals, finish_spread = spread(me, *ins, dense, row, col, g, wc, cotr, bias, *spread_refs)
     finish_layer = layer(
-        me, parameters, dense, g, row, col, wc, bias, cotr, act, ball, gwx, a0, a1, *layer_refs
+        me, *arrivals, dense, g, row, col, wc, bias, cotr, act, ball, gwx, a0, a1, *layer_refs
     )
     settle(me, dense, col, ball, gwx, out, gw, a0, a1, *settle_refs)
     finish_layer()

time: 111 us -> 114 us (1.027)
  Pallas kernels: 110 us -> 113 us
    pallas_call x1, Pallas kernels: 108 us -> 111 us  [body(): pl.pallas_call(all_kernel, out_shape=(jax.ShapeDtypeStruct((1024, 128), F...]
where the time goes in v7:
time: 114 us
  Pallas kernels  113 us (99%)
    pallas_call x1, Pallas kernels, body(): pl.pallas_call(all_kernel, out_shape=(jax.ShapeDtypeStruct((1024, 128), F...  111 us

profile of v7, /device:TPU:6, one launch (start us, length us, event | category | flops | bytes accessed | tf_op | source)
XLA Modules:
  0.0 113.6 jit_solution(13969523780107465582)
XLA Ops:
  0.6 110.8 %layer.1 = (f32[1024,128]{1,0:T(8,128)}, f32[2,512,128]{2,1,0:T(8,128)}, f32[4,40,512]{2,1,0:T(8,128)}) custom-call(s32[4,256]{1,0:T(4,128)} %bitcast.10, s32[1,256]{1,0:T(1,128)} %refs_1_.1, s32[8,4,2,16,16,128]{5,4,3,2,1,0:T(8,128)} %bitcast.8, bf16[1024,128]{1,0:T(8,128)(2,1)} %refs_3_.1, bf16[128,512]{1,0:T(8,128)(2,1)} %refs_4_.1, f32[1,512]{1,0:T(1,128)} %bitcast.11, ...), custom_call_target="tpu_custom_call" | custom-call | tf_op jit(solution)/shard_map/layer/pallas_call | solution.py:732
  111.4 2.1 %results.1 = (f32[1024,128]{1,0:T(8,128)}, f32[1024,128]{1,0:T(8,128)}, f32[4,32,512]{2,1,0:T(8,128)}, f32[1,512]{1,0:T(1,128)}) custom-call(f32[1024,128]{1,0:T(8,128)} %get-tuple-element.11.act, f32[1024,128]{1,0:T(8,128)} %bitcast.9, f32[4,40,512]{2,1,0:T(8,128)} %get-tuple-element.13.gw), custom_call_target="tpu_custom_call" | custom-call | tf_op jit(solution)/shard_map/results/pallas_call | solution.py:747

commit v8 on v7

--- a/solution.py
+++ b/solution.py
@@ -63,11 +63,11 @@
 
 
 Y_ORDER = (2, 1, 3, 0)
-ROWS = (0, 2, 1, 3)
-
-
-def spread(me, rows_hbm, counts_hbm, masks, feat_hbm, w, bias_hbm, cot, dense, row, col, g, wc, cotr, bias,
-           rows_ref, counts_ref, feat, words, m16, rm, slots_s, slots_v, landed_v, landed_s, xt, send, recv, load, local):
+ROWS = (2, 1, 3, 0)
+
+
+def spread(me, rows_hbm, counts_hbm, masks, feat_hbm, w, bias_hbm, cot, dense, row, col, gs, wc, cotr, bias,
+           rows_ref, counts_ref, feat, g, inv_s, scale, words, m16, rm, slots_s, slots_v, landed_v, landed_s, xt, send, recv, load, local):
     own, other = me.c, 1 - me.c
     small = [
         pltpu.make_async_copy(rows_hbm, rows_ref, local.at[6]),
@@ -88,7 +88,8 @@
     z_peers = [me.at(z=me.dz(n)) for n in (1, 2, 3)]
     y_peers = [me.at(y=me.dy(n)) for n in (1, 2, 3)]
     rep_peers = [sibling, me.at(xl=1 - me.xl), me.at(xl=1 - me.xl, c=1 - me.c)]
-    everyone = z_peers + y_peers + rep_peers + [x_peer]
+    xz_peers = z_peers + [x_peer] + [me.at(x=1 - me.x, z=me.dz(n)) for n in (1, 2, 3)]
+    everyone = xz_peers + y_peers + rep_peers
     barrier = pltpu.get_barrier_semaphore()
     for peer in everyone:
         pl.semaphore_signal(barrier, inc=1, device_id=peer, device_id_type=MESH)
@@ -107,74 +108,46 @@
 
         lax.fori_loop(0, 8, tiles, 0)
 
-    narrow(0)
-    pl.semaphore_wait(barrier, len(everyone))
-    copies = Copies(send, recv)
-
-    def cot_rows(rep):
-        return cot.at[pl.ds(pl.multiple_of(rep * 256, 256), 256), :]
-
-    mask_copies = []
-    for q in range(3):
-        if q:
-            narrow(q)
-        mask_copies.append(copies.start(m16.at[q], rm.at[me.y], y_peers[Y_ORDER[q] - 1]))
-    early = []
-    for peer in rep_peers:
-        early.append(copies.start(cot_rows(peer[1]), cotr.at[me.rep], peer))
-        early.append(copies.start(w, wc.at[me.rep], peer))
-    narrow(3)
     for copy in small:
         copy.wait()
-    tile_row = lax.broadcasted_iota(jnp.int32, (8, 128), 0)
-
-    def scan(q, degrees):
-        n = Y_ORDER[q % 4]
-        half = own if q < 4 else other
-        if q >= 4:
-            loads[q].wait()
-
-        def tiles(xz, degrees):
-            first = ((xz * 4 + me.dy(n)) * 2 + half) * 4
+
+    def fill(xz, _):
+        for q in range(4):
+            first = ((xz * 4 + me.dy(Y_ORDER[q])) * 2 + own) * 4
             for tc in range(4):
                 count = counts_ref[0, first + tc]
                 for s in range(4):
-                    slot = tc * 4 + s
-                    t = jnp.where(s < count, rows_ref[s, first + tc], 8)
-                    tile = words[q, xz, slot]
-                    if q < 4:
-                        slots_s[q, 0, xz * 16 + slot] = t
-                    joined = jnp.bitwise_or(tile[:8], jnp.left_shift(tile[8:], 8))
-                    counted = jnp.sum(lax.population_count(joined), axis=0, keepdims=True)
-                    degrees = degrees + jnp.where(tile_row == t, counted, 0)
-            return degrees
-
-        return lax.fori_loop(0, 8, tiles, degrees)
-
-    degrees = jnp.zeros((8, 128), jnp.int32)
-    for q in range(8):
-        degrees = scan(q, degrees)
-
-    inv = lax.rsqrt(1.0 + degrees.astype(F32))
+                    slots_s[q, 0, xz * 16 + tc * 4 + s] = jnp.where(s < count, rows_ref[s, first + tc], 8)
+        return 0
+
+    lax.fori_loop(0, 8, fill, 0)
+    to_vmem = pltpu.make_async_copy(slots_s, slots_v, local.at[2])
+    to_vmem.start()
+
     place = lax.broadcasted_iota(jnp.int32, (128, 128), 1)
     source = 8 * jnp.bitwise_and(place, 15) + jnp.right_shift(place, 4)
     perm = jnp.where(lax.broadcasted_iota(jnp.int32, (128, 128), 0) == source, 1.0, 0.0).astype(BF16)
     feat_load.wait()
     for t in range(8):
-        lanes = inv[t:t + 1, :]
-        row[:, t * 128:(t + 1) * 128] = jnp.broadcast_to(lanes, (8, 128))
-        spread = jnp.broadcast_to(lanes, (128, 128))
-        col[t * 128:(t + 1) * 128, :] = spread.T
-        scaled = (feat[t * 128:(t + 1) * 128, :].astype(F32).T * spread).astype(BF16)
-        moved = jnp.dot(scaled, perm, preferred_element_type=F32).astype(BF16)
+        turned = feat[t * 128:(t + 1) * 128, :].astype(F32).T.astype(BF16)
+        moved = jnp.dot(turned, perm, preferred_element_type=F32).astype(BF16)
         xt[t // 4, :, (t % 4) * 128:(t % 4 + 1) * 128] = moved
+    narrow(0)
+    to_vmem.wait()
+    pl.semaphore_wait(barrier, len(everyone))
+    copies = Copies(send, recv)
+
+    def cot_rows(rep):
+        return cot.at[pl.ds(pl.multiple_of(rep * 256, 256), 256), :]
 
     def at(core, xz):
         return g.at[xz, core]
 
+    slot_copies = [copies.start(slots_v.at[q], landed_v.at[me.y], y_peers[Y_ORDER[q] - 1]) for q in range(3)]
     to_sibling = copies.start(xt.at[other], at(own, me.xz), sibling)
     first = [copies.start(xt.at[own], at(own, me.xz), p) for p in z_peers]
     across = copies.start(xt.at[own], at(own, me.xz), x_peer)
+    mask_copies = [copies.start(m16.at[0], rm.at[me.y], y_peers[Y_ORDER[0] - 1])]
     stays = [
         pltpu.make_async_copy(xt.at[own], at(own, me.xz), local.at[0]),
         pltpu.make_async_copy(w, wc.at[me.rep], local.at[1]),
@@ -183,16 +156,70 @@
     ]
     for copy in stays:
         copy.start()
-    to_vmem = pltpu.make_async_copy(slots_s, slots_v, local.at[2])
-    to_vmem.start()
-    to_vmem.wait()
-    slot_copies = [copies.start(slots_v.at[q], landed_v.at[me.y], y_peers[Y_ORDER[q] - 1]) for q in range(3)]
     kept = pltpu.make_async_copy(slots_v.at[3], landed_v.at[me.y], local.at[3])
     kept.start()
-
+    tile_row = lax.broadcasted_iota(jnp.int32, (8, 128), 0)
+
+    def scan(q, degrees):
+        n = Y_ORDER[q % 4]
+        half = own if q < 4 else other
+        if q >= 4:
+            loads[q].wait()
+
+        def tiles(xz, degrees):
+            first = ((xz * 4 + me.dy(n)) * 2 + half) * 4
+            for tc in range(4):
+                count = counts_ref[0, first + tc]
+                for s in range(4):
+                    t = jnp.where(s < count, rows_ref[s, first + tc], 8)
+                    tile = words[q, xz, tc * 4 + s]
+                    joined = jnp.bitwise_or(tile[:8], jnp.left_shift(tile[8:], 8))
+                    counted = jnp.sum(lax.population_count(joined), axis=0, keepdims=True)
+                    degrees = degrees + jnp.where(tile_row == t, counted, 0)
+            return degrees
+
+        return lax.fori_loop(0, 8, tiles, degrees)
+
+    degrees = scan(0, jnp.zeros((8, 128), jnp.int32))
+    narrow(1)
     to_sibling.wait_recv()
     other_x = copies.start(at(other, me.xz), at(other, me.xz), x_peer)
     second = [copies.start(at(other, me.xz), at(other, me.xz), p) for p in z_peers]
+    degrees = scan(1, degrees)
+    narrow(2)
+    for q in (1, 2):
+        mask_copies.append(copies.start(m16.at[q], rm.at[me.y], y_peers[Y_ORDER[q] - 1]))
+    early = []
+    for peer in rep_peers:
+        early.append(copies.start(cot_rows(peer[1]), cotr.at[me.rep], peer))
+        early.append(copies.start(w, wc.at[me.rep], peer))
+    narrow(3)
+    for q in (2, 3, 4):
+        degrees = scan(q, degrees)
+    last = []
+    for n in (1, 2, 3):
+        first[n - 1].wait_recv()
+        source = me.x * 4 + me.dz(4 - n)
+        last.append(copies.start(at(own, source), at(own, source), x_peer))
+    for q in (5, 6, 7):
+        degrees = scan(q, degrees)
+
+    degrees = 1.0 + degrees.astype(F32)
+    high = jnp.floor(degrees * (1.0 / 256.0))
+    low = degrees - high * 256.0
+    placed = 256.0 * jnp.dot(high.astype(BF16), perm, preferred_element_type=F32)
+    placed = placed + jnp.dot(low.astype(BF16), perm, preferred_element_type=F32)
+    inv_s[...] = lax.rsqrt(placed)
+    inv_copies = [copies.start(inv_s, scale.at[me.xz], peer) for peer in xz_peers]
+    inv = lax.rsqrt(degrees)
+    other_x.wait_recv()
+    far = (1 - me.x) * 4 + me.z
+    last += [copies.start(at(other, far), at(other, far), p) for p in z_peers]
+    scale[me.xz] = inv_s[...]
+    for t in range(8):
+        lanes = inv[t:t + 1, :]
+        row[:, t * 128:(t + 1) * 128] = jnp.broadcast_to(lanes, (8, 128))
+        col[t * 128:(t + 1) * 128, :] = jnp.broadcast_to(lanes, (128, 128)).T
 
     def put_tiles(n, slot_rows, at):
         i = me.dy(n)
@@ -211,14 +238,6 @@
         lax.fori_loop(0, 8, column, 0)
 
     put_tiles(0, slots_s, 3)
-    last = []
-    for n in (1, 2, 3):
-        first[n - 1].wait_recv()
-        source = me.x * 4 + me.dz(4 - n)
-        last.append(copies.start(at(own, source), at(own, source), x_peer))
-    other_x.wait_recv()
-    far = (1 - me.x) * 4 + me.z
-    last += [copies.start(at(other, far), at(other, far), p) for p in z_peers]
 
     def arrive(column):
         n = column % 4
@@ -231,6 +250,14 @@
         else:
             last[n - 1].wait_recv()
             last[n + 2].wait_recv()
+        if column:
+            inv_copies[column - 1].wait_recv()
+        xz = me.column(column)
+        for t in range(4):
+            lanes = slice(t * 128, (t + 1) * 128)
+            factor = scale[xz, pl.ds(own * 4 + t, 1), :]
+            for core in range(2):
+                gs[xz, core, :, lanes] = (g[xz, core, :, lanes].astype(F32) * factor).astype(BF16)
 
     def slots():
         kept.wait()
@@ -293,21 +320,22 @@
 
     def to_owner(k, m):
         return pltpu.make_async_remote_copy(
-            src_ref=snd.at[k - 1, m], dst_ref=ry.at[k - 1, m],
-            send_sem=sum_s.at[k * 4 + m - 4], recv_sem=sum_r.at[k * 4 + m - 4],
-            device_id=me.at(y=me.dy(table(ROWS, k))), device_id_type=MESH,
+            src_ref=snd.at[k, m], dst_ref=ry.at[k, m], send_sem=sum_s.at[k * 4 + m], recv_sem=sum_r.at[k * 4 + m],
+            device_id=me.at(y=me.dy(table((2, 1, 3), k))), device_id_type=MESH,
         )
 
     def pass_on(k):
         to_sibling(k).wait_recv()
         for m in range(4):
             rows = slice(m * 256, (m + 1) * 256)
-            snd[k - 1, m] = (part[k, own, :, rows].astype(F32) + rc[k, :, rows].astype(F32)).astype(BF16)
+            snd[k, m] = (part[k, own, :, rows].astype(F32) + rc[k, :, rows].astype(F32)).astype(BF16)
             to_owner(k, m).start()
 
     def chunk(c):
         return me.dy(table(ROWS, c // 8)), me.column(lax.rem(c, 8))
 
+    slots()
+    place_tiles(ROWS[0])
     bufs = (a0, a1)
     unpack(dense, *chunk(0), a0)
 
@@ -319,11 +347,9 @@
                 arrive(step * 2)
                 arrive(step * 2 + 1)
 
-        for step in range(1, 4):
+        for step in (1, 2):
             @pl.when(n == step * 4 - 1)
             def _():
-                if step == 1:
-                    slots()
                 place_tiles(ROWS[step])
 
         for h in range(2):
@@ -340,21 +366,20 @@
             part[k, 1] = acc[128:256].astype(BF16)
             to_sibling(k).start()
 
-        @pl.when(jnp.logical_and(pair == 0, k >= 2))
+        @pl.when(jnp.logical_and(pair == 0, k >= 1))
         def _():
             pass_on(k - 1)
 
         return 0
 
     lax.fori_loop(0, 16, two_chunks, 0)
-    pass_on(3)
-    to_sibling(0).wait_recv()
+    to_sibling(3).wait_recv()
 
     def finish_sum(m, out):
-        for k in (1, 2, 3):
+        for k in range(3):
             to_owner(k, m).wait_recv()
         rows = rows_of(m)
-        total = part[0, own, :, rows].astype(F32) + rc[0, :, rows].astype(F32)
+        total = part[3, own, :, rows].astype(F32) + rc[3, :, rows].astype(F32)
         for k in range(3):
             total = total + ry[k, m].astype(F32)
         total = total * row[0:1, rows]
@@ -444,7 +469,7 @@
             copy.wait_recv()
         act_kept.wait()
         copies.wait_sends()
-        for k in (1, 2, 3):
+        for k in range(3):
             for m in range(4):
                 to_owner(k, m).wait_send()
         for k in range(4):
@@ -453,7 +478,7 @@
     return finish
 
 
-BLOCKS = ((1, 2), (0, 2), (1, 1), (1, 3), (0, 1), (0, 3), (1, 0), (0, 0))
+BLOCKS = ((1, 2), (1, 1), (1, 3), (1, 0), (0, 2), (0, 1), (0, 3), (0, 0))
 ORDER = {key: n for n, key in enumerate(BLOCKS)}
 
 
@@ -519,13 +544,13 @@
     actions = {n: [] for n in range(8)}
     for n in range(4):
         actions[ORDER[1, n]].append(x_first[n].start)
+    for n in (2, 1, 3):
+        actions[ORDER[0, n]].append(functools.partial(pass_b, n))
     for key, copy in z_first.items():
         actions[ORDER[key]].append(copy.start)
-    for n, step in ((2, 2), (1, 4), (3, 5)):
-        actions[step].append(functools.partial(pass_b, n))
-    actions[1].append(weights_z)
-    actions[3].append(weights_x)
-    actions[6].append(pass_a)
+    actions[3].append(weights_z)
+    actions[4].append(pass_a)
+    actions[5].append(weights_x)
     actions[6].append(weights_back)
 
     for copy in w_y:
@@ -628,6 +653,9 @@
     pltpu.SMEM((4, 256), jnp.int32),
     pltpu.SMEM((1, 256), jnp.int32),
     pltpu.VMEM((1024, 128), BF16),
+    pltpu.VMEM((8, 2, 128, 512), BF16),
+    pltpu.VMEM((8, 128), F32),
+    pltpu.VMEM((8, 8, 128), F32),
     pltpu.VMEM((8, 8, 16, 16, 128), jnp.int32),
     pltpu.VMEM((3, 8, 16, 16, 128), jnp.int16),
     pltpu.VMEM((4, 8, 16, 16, 128), jnp.int16),
@@ -636,8 +664,8 @@
     pltpu.VMEM((4, 1, 128), jnp.int32),
     pltpu.SMEM((4, 1, 128), jnp.int32),
     pltpu.VMEM((2, 128, 512), BF16),
-    DMA((27,)),
-    DMA((27,)),
+    DMA((34,)),
+    DMA((34,)),
     DMA((8,)),
     DMA((10,)),
 )

time: 114 us -> 111 us (0.974)
  Pallas kernels: 113 us -> 109 us
    pallas_call x1, Pallas kernels: 111 us -> 107 us  [body(): pl.pallas_call(all_kernel, out_shape=(jax.ShapeDtypeStruct((1024, 128), F...]
where the time goes in v8:
time: 111 us; the launch traced here: 110 us
  Pallas kernels  109 us (98%)
    pallas_call x1, Pallas kernels, body(): pl.pallas_call(all_kernel, out_shape=(jax.ShapeDtypeStruct((1024, 128), F...  107 us

profile of v8, /device:TPU:6, one launch (start us, length us, event | category | flops | bytes accessed | tf_op | source)
XLA Modules:
  0.0 109.7 jit_solution(2765293605118479983)
XLA Ops:
  0.6 106.9 %layer.1 = (f32[1024,128]{1,0:T(8,128)}, f32[2,512,128]{2,1,0:T(8,128)}, f32[4,40,512]{2,1,0:T(8,128)}) custom-call(s32[4,256]{1,0:T(4,128)} %bitcast.10, s32[1,256]{1,0:T(1,128)} %refs_1_.1, s32[8,4,2,16,16,128]{5,4,3,2,1,0:T(8,128)} %bitcast.8, bf16[1024,128]{1,0:T(8,128)(2,1)} %refs_3_.1, bf16[128,512]{1,0:T(8,128)(2,1)} %refs_4_.1, f32[1,512]{1,0:T(1,128)} %bitcast.11, ...), custom_call_target="tpu_custom_call" | custom-call | tf_op jit(solution)/shard_map/layer/pallas_call | solution.py:760
  107.6 2.1 %results.1 = (f32[1024,128]{1,0:T(8,128)}, f32[1024,128]{1,0:T(8,128)}, f32[4,32,512]{2,1,0:T(8,128)}, f32[1,512]{1,0:T(1,128)}) custom-call(f32[1024,128]{1,0:T(8,128)} %get-tuple-element.11.act, f32[1024,128]{1,0:T(8,128)} %bitcast.9, f32[4,40,512]{2,1,0:T(8,128)} %get-tuple-element.13.gw), custom_call_target="tpu_custom_call" | custom-call | tf_op jit(solution)/shard_map/results/pallas_call | solution.py:775

commit v9 on v8

--- a/solution.py
+++ b/solution.py
@@ -48,12 +48,16 @@
         self.send, self.recv, self.used = send, recv, []
 
     def start(self, src, dst, peer):
+        copy = self.make(src, dst, peer)
+        copy.start()
+        return copy
+
+    def make(self, src, dst, peer):
         n = len(self.used)
         copy = pltpu.make_async_remote_copy(
             src_ref=src, dst_ref=dst, send_sem=self.send.at[n], recv_sem=self.recv.at[n],
             device_id=peer, device_id_type=MESH,
         )
-        copy.start()
         self.used.append(copy)
         return copy
 
@@ -191,8 +195,8 @@
         mask_copies.append(copies.start(m16.at[q], rm.at[me.y], y_peers[Y_ORDER[q] - 1]))
     early = []
     for peer in rep_peers:
-        early.append(copies.start(cot_rows(peer[1]), cotr.at[me.rep], peer))
-        early.append(copies.start(w, wc.at[me.rep], peer))
+        early.append(copies.make(cot_rows(peer[1]), cotr.at[me.rep], peer))
+        early.append(copies.make(w, wc.at[me.rep], peer))
     narrow(3)
     for q in (2, 3, 4):
         degrees = scan(q, degrees)
@@ -272,13 +276,17 @@
         mask_copies[q].wait_recv()
         put_tiles(n, landed_s, me.dy(n))
 
+    def send_parameters():
+        for copy in early:
+            copy.start()
+
     def parameters():
         for copy in early:
             copy.wait_recv()
         for copy in stays[1:]:
             copy.wait()
 
-    return arrive, slots, place_tiles, parameters, copies.wait_sends
+    return arrive, slots, place_tiles, send_parameters, parameters, copies.wait_sends
 
 
 def table(values, step):
@@ -299,7 +307,7 @@
                 out_ref[first:first + 16, t * 128:(t + 1) * 128] = bits
 
 
-def layer(me, arrive, slots, place_tiles, parameters, dense, g, row, col, wc, bias, cotr, act, ball, gwx, a0, a1,
+def layer(me, arrive, slots, place_tiles, send_parameters, parameters, dense, g, row, col, wc, bias, cotr, act, ball, gwx, a0, a1,
           acc, part, rc, snd, ry, agg_s, agg, agg_t, slope, act_s, back_s,
           core_s, core_r, sum_s, sum_r, send, recv, local):
     sibling = me.at(c=1 - me.c)
@@ -350,6 +358,8 @@
         for step in (1, 2):
             @pl.when(n == step * 4 - 1)
             def _():
+                if step == 1:
+                    send_parameters()
                 place_tiles(ROWS[step])
 
         for h in range(2):
@@ -478,12 +488,13 @@
     return finish
 
 
+SPLIT = 192
 BLOCKS = ((1, 2), (1, 1), (1, 3), (1, 0), (0, 2), (0, 1), (0, 3), (0, 0))
 ORDER = {key: n for n, key in enumerate(BLOCKS)}
 
 
 def settle(me, dense, col, ball, gwx, out, gw, a0, a1,
-           acc, part, az, a_sum, ax, bx, b_sum, bz, hold, final, wy, wz, wx_send, wx, gw_own, send, recv, local):
+           acc, part_a, part_b, az, a_sum, ax, bx, b_sum, bz, hold, final, wy, wz, wx_send, wx, gw_own, send, recv, local):
     sibling = me.at(c=1 - me.c)
     x_peer = me.at(x=1 - me.x)
     z_peers = [me.at(z=me.dz(n)) for n in (1, 2, 3)]
@@ -495,9 +506,9 @@
             device_id=peer, device_id_type=MESH,
         )
 
-    x_first = {n: remote(n, part.at[ORDER[1, n], 1], bx.at[n], x_peer) for n in range(4)}
+    x_first = {n: remote(n, part_b.at[ORDER[1, n]], bx.at[n], x_peer) for n in range(4)}
     z_first = {
-        (side, n): remote(4 + side * 3 + n - 1, part.at[ORDER[side, n], 0], az.at[side, n - 1], z_peers[n - 1])
+        (side, n): remote(4 + side * 3 + n - 1, part_a.at[ORDER[side, n]], az.at[side, n - 1], z_peers[n - 1])
         for side in range(2) for n in (1, 2, 3)
     }
     z_second = {n: remote(9 + n, b_sum.at[n - 1], bz.at[n - 1], z_peers[n - 1]) for n in (1, 2, 3)}
@@ -510,11 +521,11 @@
 
     def pass_b(n):
         x_first[n].wait_recv()
-        b_sum[n - 1] = (part[ORDER[0, n], 1].astype(F32) + bx[n].astype(F32)).astype(BF16)
+        b_sum[n - 1] = (part_b[ORDER[0, n]].astype(F32) + bx[n].astype(F32)).astype(BF16)
         z_second[n].start()
 
     def pass_a():
-        total = part[ORDER[1, 0], 0].astype(F32)
+        total = part_a[ORDER[1, 0]].astype(F32)
         for n in (1, 2, 3):
             z_first[1, n].wait_recv()
             total = total + az[1, n - 1].astype(F32)
@@ -578,8 +589,8 @@
 
         @pl.when(pair == 1)
         def _():
-            part[block, 0] = acc[0:256].astype(BF16)
-            part[block, 1] = acc[256:512].astype(BF16)
+            part_a[block] = acc[0:SPLIT].astype(BF16)
+            part_b[block] = acc[SPLIT:512].astype(BF16)
 
         for at, calls in actions.items():
             if calls:
@@ -592,10 +603,12 @@
 
     lax.fori_loop(0, 16, two_chunks, 0)
 
-    def place(tile, total):
+    def keep_rows(first, total):
+        for q in range(2):
+            hold[q * 512 + first:q * 512 + first + total.shape[0], :] = total[:, q * 128:(q + 1) * 128]
+
+    def place(tile):
         here = slice(tile * 128, tile * 128 + 256)
-        for q in range(2):
-            hold[q * 512 + tile * 128:q * 512 + tile * 128 + 256, :] = total[:, q * 128:(q + 1) * 128]
         for t in range(tile, tile + 2):
             for w in range(16):
                 first = t * 128 + w * 8
@@ -609,20 +622,22 @@
         keep.start()
         return swap, keep
 
-    total = part[ORDER[0, 0], 1].astype(F32)
+    total = part_b[ORDER[0, 0]].astype(F32)
     x_first[0].wait_recv()
     total = total + bx[0].astype(F32)
     for n in (1, 2, 3):
         z_second[n].wait_recv()
         total = total + bz[n - 1].astype(F32)
-    swaps = [place(2, total)]
-    total = part[ORDER[0, 0], 0].astype(F32)
+    keep_rows(SPLIT, total)
+    swaps = [place(2)]
+    total = part_a[ORDER[0, 0]].astype(F32)
     for n in (1, 2, 3):
         z_first[0, n].wait_recv()
         total = total + az[0, n - 1].astype(F32)
     x_second.wait_recv()
     total = total + ax[...].astype(F32)
-    swaps.append(place(0, total))
+    keep_rows(0, total)
+    swaps.append(place(0))
     for copy in w_back:
         copy.wait_recv()
     for swap, keep in swaps:
@@ -635,7 +650,7 @@
         copy.wait_send()
 
 
-HALF = (256, 256)
+PART_A, PART_B = (SPLIT, 256), (512 - SPLIT, 256)
 HELD = (
     pltpu.VMEM((32, 4, 8, 16, 128), jnp.int16),
     pltpu.VMEM((8, 1024), F32),
@@ -691,13 +706,14 @@
 )
 SETTLE = (
     pltpu.VMEM((512, 256), F32),
-    pltpu.VMEM((8, 2) + HALF, BF16),
-    pltpu.VMEM((2, 3) + HALF, BF16),
-    pltpu.VMEM(HALF, BF16),
-    pltpu.VMEM(HALF, BF16),
-    pltpu.VMEM((4,) + HALF, BF16),
-    pltpu.VMEM((3,) + HALF, BF16),
-    pltpu.VMEM((3,) + HALF, BF16),
+    pltpu.VMEM((8,) + PART_A, BF16),
+    pltpu.VMEM((8,) + PART_B, BF16),
+    pltpu.VMEM((2, 3) + PART_A, BF16),
+    pltpu.VMEM(PART_A, BF16),
+    pltpu.VMEM(PART_A, BF16),
+    pltpu.VMEM((4,) + PART_B, BF16),
+    pltpu.VMEM((3,) + PART_B, BF16),
+    pltpu.VMEM((3,) + PART_B, BF16),
     pltpu.VMEM((1024, 128), F32),
     pltpu.VMEM((2, 512, 128), F32),
     pltpu.VMEM((4, 40, 512), F32),

time: 111 us -> 107 us (0.964); the launches traced: 110 us -> 107 us
  Pallas kernels: 109 us -> 106 us
    pallas_call x1, Pallas kernels: 107 us -> 104 us  [body(): pl.pallas_call(all_kernel, out_shape=(jax.ShapeDtypeStruct((1024, 128), F...]
where the time goes in v9:
time: 107 us
  Pallas kernels  106 us (99%)
    pallas_call x1, Pallas kernels, body(): pl.pallas_call(all_kernel, out_shape=(jax.ShapeDtypeStruct((1024, 128), F...  104 us

profile of v9, /device:TPU:6, one launch (start us, length us, event | category | flops | bytes accessed | tf_op | source)
XLA Modules:
  0.0 107.1 jit_solution(2673695076304491367)
XLA Ops:
  0.6 104.3 %layer.1 = (f32[1024,128]{1,0:T(8,128)}, f32[2,512,128]{2,1,0:T(8,128)}, f32[4,40,512]{2,1,0:T(8,128)}) custom-call(s32[4,256]{1,0:T(4,128)} %bitcast.10, s32[1,256]{1,0:T(1,128)} %refs_1_.1, s32[8,4,2,16,16,128]{5,4,3,2,1,0:T(8,128)} %bitcast.8, bf16[1024,128]{1,0:T(8,128)(2,1)} %refs_3_.1, bf16[128,512]{1,0:T(8,128)(2,1)} %refs_4_.1, f32[1,512]{1,0:T(1,128)} %bitcast.11, ...), custom_call_target="tpu_custom_call" | custom-call | tf_op jit(solution)/shard_map/layer/pallas_call | solution.py:776
  104.9 2.1 %results.1 = (f32[1024,128]{1,0:T(8,128)}, f32[1024,128]{1,0:T(8,128)}, f32[4,32,512]{2,1,0:T(8,128)}, f32[1,512]{1,0:T(1,128)}) custom-call(f32[1024,128]{1,0:T(8,128)} %get-tuple-element.11.act, f32[1024,128]{1,0:T(8,128)} %bitcast.9, f32[4,40,512]{2,1,0:T(8,128)} %get-tuple-element.13.gw), custom_call_target="tpu_custom_call" | custom-call | tf_op jit(solution)/shard_map/results/pallas_call | solution.py:791

commit v10 on v9

--- a/solution.py
+++ b/solution.py
@@ -73,6 +73,8 @@
 def spread(me, rows_hbm, counts_hbm, masks, feat_hbm, w, bias_hbm, cot, dense, row, col, gs, wc, cotr, bias,
            rows_ref, counts_ref, feat, g, inv_s, scale, words, m16, rm, slots_s, slots_v, landed_v, landed_s, xt, send, recv, load, local):
     own, other = me.c, 1 - me.c
+    feat_load = pltpu.make_async_copy(feat_hbm, feat, local.at[8])
+    feat_load.start()
     small = [
         pltpu.make_async_copy(rows_hbm, rows_ref, local.at[6]),
         pltpu.make_async_copy(counts_hbm, counts_ref, local.at[7]),
@@ -84,8 +86,6 @@
         half = own if q < 4 else other
         loads.append(pltpu.make_async_copy(masks.at[:, me.dy(Y_ORDER[q % 4]), half], words.at[q], load.at[q]))
         loads[q].start()
-    feat_load = pltpu.make_async_copy(feat_hbm, feat, local.at[8])
-    feat_load.start()
 
     sibling = me.at(c=1 - me.c)
     x_peer = me.at(x=1 - me.x)
@@ -112,6 +112,26 @@
 
         lax.fori_loop(0, 8, tiles, 0)
 
+    place = lax.broadcasted_iota(jnp.int32, (128, 128), 1)
+    source = 8 * jnp.bitwise_and(place, 15) + jnp.right_shift(place, 4)
+    perm = jnp.where(lax.broadcasted_iota(jnp.int32, (128, 128), 0) == source, 1.0, 0.0).astype(BF16)
+    feat_load.wait()
+    for t in range(8):
+        turned = feat[t * 128:(t + 1) * 128, :].astype(F32).T.astype(BF16)
+        moved = jnp.dot(turned, perm, preferred_element_type=F32).astype(BF16)
+        xt[t // 4, :, (t % 4) * 128:(t % 4 + 1) * 128] = moved
+    pl.semaphore_wait(barrier, len(everyone))
+    copies = Copies(send, recv)
+
+    def cot_rows(rep):
+        return cot.at[pl.ds(pl.multiple_of(rep * 256, 256), 256), :]
+
+    def at(core, xz):
+        return g.at[xz, core]
+
+    to_sibling = copies.start(xt.at[other], at(own, me.xz), sibling)
+    first = [copies.start(xt.at[own], at(own, me.xz), p) for p in z_peers]
+    across = copies.start(xt.at[own], at(own, me.xz), x_peer)
     for copy in small:
         copy.wait()
 
@@ -127,31 +147,13 @@
     lax.fori_loop(0, 8, fill, 0)
     to_vmem = pltpu.make_async_copy(slots_s, slots_v, local.at[2])
     to_vmem.start()
-
-    place = lax.broadcasted_iota(jnp.int32, (128, 128), 1)
-    source = 8 * jnp.bitwise_and(place, 15) + jnp.right_shift(place, 4)
-    perm = jnp.where(lax.broadcasted_iota(jnp.int32, (128, 128), 0) == source, 1.0, 0.0).astype(BF16)
-    feat_load.wait()
-    for t in range(8):
-        turned = feat[t * 128:(t + 1) * 128, :].astype(F32).T.astype(BF16)
-        moved = jnp.dot(turned, perm, preferred_element_type=F32).astype(BF16)
-        xt[t // 4, :, (t % 4) * 128:(t % 4 + 1) * 128] = moved
     narrow(0)
     to_vmem.wait()
-    pl.semaphore_wait(barrier, len(everyone))
-    copies = Copies(send, recv)
-
-    def cot_rows(rep):
-        return cot.at[pl.ds(pl.multiple_of(rep * 256, 256), 256), :]
-
-    def at(core, xz):
-        return g.at[xz, core]
-
     slot_copies = [copies.start(slots_v.at[q], landed_v.at[me.y], y_peers[Y_ORDER[q] - 1]) for q in range(3)]
-    to_sibling = copies.start(xt.at[other], at(own, me.xz), sibling)
-    first = [copies.start(xt.at[own], at(own, me.xz), p) for p in z_peers]
-    across = copies.start(xt.at[own], at(own, me.xz), x_peer)
     mask_copies = [copies.start(m16.at[0], rm.at[me.y], y_peers[Y_ORDER[0] - 1])]
+    to_sibling.wait_recv()
+    other_x = copies.start(at(other, me.xz), at(other, me.xz), x_peer)
+    second = [copies.start(at(other, me.xz), at(other, me.xz), p) for p in z_peers]
     stays = [
         pltpu.make_async_copy(xt.at[own], at(own, me.xz), local.at[0]),
         pltpu.make_async_copy(w, wc.at[me.rep], local.at[1]),
@@ -186,9 +188,6 @@
 
     degrees = scan(0, jnp.zeros((8, 128), jnp.int32))
     narrow(1)
-    to_sibling.wait_recv()
-    other_x = copies.start(at(other, me.xz), at(other, me.xz), x_peer)
-    second = [copies.start(at(other, me.xz), at(other, me.xz), p) for p in z_peers]
     degrees = scan(1, degrees)
     narrow(2)
     for q in (1, 2):
@@ -559,9 +558,9 @@
         actions[ORDER[0, n]].append(functools.partial(pass_b, n))
     for key, copy in z_first.items():
         actions[ORDER[key]].append(copy.start)
-    actions[3].append(weights_z)
+    actions[2].append(weights_z)
     actions[4].append(pass_a)
-    actions[5].append(weights_x)
+    actions[4].append(weights_x)
     actions[6].append(weights_back)
 
     for copy in w_y:

time: 107 us -> 109 us (1.019)
  Pallas kernels: 106 us -> 109 us
    pallas_call x1, Pallas kernels: 104 us -> 106 us  [body(): pl.pallas_call(all_kernel, out_shape=(jax.ShapeDtypeStruct((1024, 128), F...]
where the time goes in v10:
time: 109 us
  Pallas kernels  109 us (100%)
    pallas_call x1, Pallas kernels, body(): pl.pallas_call(all_kernel, out_shape=(jax.ShapeDtypeStruct((1024, 128), F...  106 us

profile of v10, /device:TPU:6, one launch (start us, length us, event | category | flops | bytes accessed | tf_op | source)
XLA Modules:
  0.0 109.2 jit_solution(782781343192503177)
XLA Ops:
  0.6 106.5 %layer.1 = (f32[1024,128]{1,0:T(8,128)}, f32[2,512,128]{2,1,0:T(8,128)}, f32[4,40,512]{2,1,0:T(8,128)}) custom-call(s32[4,256]{1,0:T(4,128)} %bitcast.10, s32[1,256]{1,0:T(1,128)} %refs_1_.1, s32[8,4,2,16,16,128]{5,4,3,2,1,0:T(8,128)} %bitcast.8, bf16[1024,128]{1,0:T(8,128)(2,1)} %refs_3_.1, bf16[128,512]{1,0:T(8,128)(2,1)} %refs_4_.1, f32[1,512]{1,0:T(1,128)} %bitcast.11, ...), custom_call_target="tpu_custom_call" | custom-call | tf_op jit(solution)/shard_map/layer/pallas_call | solution.py:775
  107.1 2.1 %results.1 = (f32[1024,128]{1,0:T(8,128)}, f32[1024,128]{1,0:T(8,128)}, f32[4,32,512]{2,1,0:T(8,128)}, f32[1,512]{1,0:T(1,128)}) custom-call(f32[1024,128]{1,0:T(8,128)} %get-tuple-element.11.act, f32[1024,128]{1,0:T(8,128)} %bitcast.9, f32[4,40,512]{2,1,0:T(8,128)} %get-tuple-element.13.gw), custom_call_target="tpu_custom_call" | custom-call | tf_op jit(solution)/shard_map/results/pallas_call | solution.py:790

commit v11 on v9

--- a/solution.py
+++ b/solution.py
@@ -73,6 +73,8 @@
 def spread(me, rows_hbm, counts_hbm, masks, feat_hbm, w, bias_hbm, cot, dense, row, col, gs, wc, cotr, bias,
            rows_ref, counts_ref, feat, g, inv_s, scale, words, m16, rm, slots_s, slots_v, landed_v, landed_s, xt, send, recv, load, local):
     own, other = me.c, 1 - me.c
+    feat_load = pltpu.make_async_copy(feat_hbm, feat, local.at[8])
+    feat_load.start()
     small = [
         pltpu.make_async_copy(rows_hbm, rows_ref, local.at[6]),
         pltpu.make_async_copy(counts_hbm, counts_ref, local.at[7]),
@@ -84,8 +86,6 @@
         half = own if q < 4 else other
         loads.append(pltpu.make_async_copy(masks.at[:, me.dy(Y_ORDER[q % 4]), half], words.at[q], load.at[q]))
         loads[q].start()
-    feat_load = pltpu.make_async_copy(feat_hbm, feat, local.at[8])
-    feat_load.start()
 
     sibling = me.at(c=1 - me.c)
     x_peer = me.at(x=1 - me.x)

time: 107 us -> 107 us (level)
  no operation moved by 1% of the time
where the time goes in v11:
time: 107 us
  Pallas kernels  106 us (99%)
    pallas_call x1, Pallas kernels, body(): pl.pallas_call(all_kernel, out_shape=(jax.ShapeDtypeStruct((1024, 128), F...  104 us

profile of v11, /device:TPU:6, one launch (start us, length us, event | category | flops | bytes accessed | tf_op | source)
XLA Modules:
  0.0 107.1 jit_solution(620150390384963051)
XLA Ops:
  0.6 104.3 %layer.1 = (f32[1024,128]{1,0:T(8,128)}, f32[2,512,128]{2,1,0:T(8,128)}, f32[4,40,512]{2,1,0:T(8,128)}) custom-call(s32[4,256]{1,0:T(4,128)} %bitcast.10, s32[1,256]{1,0:T(1,128)} %refs_1_.1, s32[8,4,2,16,16,128]{5,4,3,2,1,0:T(8,128)} %bitcast.8, bf16[1024,128]{1,0:T(8,128)(2,1)} %refs_3_.1, bf16[128,512]{1,0:T(8,128)(2,1)} %refs_4_.1, f32[1,512]{1,0:T(1,128)} %bitcast.11, ...), custom_call_target="tpu_custom_call" | custom-call | tf_op jit(solution)/shard_map/layer/pallas_call | solution.py:776
  105.0 2.1 %results.1 = (f32[1024,128]{1,0:T(8,128)}, f32[1024,128]{1,0:T(8,128)}, f32[4,32,512]{2,1,0:T(8,128)}, f32[1,512]{1,0:T(1,128)}) custom-call(f32[1024,128]{1,0:T(8,128)} %get-tuple-element.11.act, f32[1024,128]{1,0:T(8,128)} %bitcast.9, f32[4,40,512]{2,1,0:T(8,128)} %get-tuple-element.13.gw), custom_call_target="tpu_custom_call" | custom-call | tf_op jit(solution)/shard_map/results/pallas_call | solution.py:791
